TPU v7x, 32 devices: a whole 2x2x4 slice. The times are simulated.
32 devices in a mesh: dp: 4 (over y, x), expert: 8 (over z, core).
Axes of the slice: x: 2, y: 2, z: 4, core: 2. Of those that a mesh axis runs over, the one named last changes fastest.
Arguments:
- tokens: bfloat16 [8192, 1536], P(('dp', 'expert')), may hold values from -6 to 6
- cotangent: bfloat16 [8192, 1536], P(('dp', 'expert')), may hold values from -0.59765625 to 0.59765625
- chosen: int32 [128, 8, 16], P(('dp', 'expert')), may hold values from 0 to 63, as said below
- w_router: bfloat16 [1536, 8], replicated, may hold values from -0.15625 to 0.15625
- w_gate: bfloat16 [8, 1536, 1024], P('expert', 'dp'), may hold values from -0.15625 to 0.15625
- w_up: bfloat16 [8, 1536, 1024], P('expert', 'dp'), may hold values from -0.15625 to 0.15625
- w_down: bfloat16 [8, 1024, 1536], P('expert', 'dp'), may hold values from -0.1875 to 0.1875
Outputs:
- mixed: bfloat16 [8192, 1536], P(('dp', 'expert'))
- grad_tokens: bfloat16 [8192, 1536], P(('dp', 'expert'))
- grad_gate: float32 [8, 1536, 1024], P('expert', 'dp')
- grad_up: float32 [8, 1536, 1024], P('expert', 'dp')
- down_weight_gradient: float32 [8, 1024, 1536], P('expert', 'dp')
- grad_router: float32 [1536, 8], replicated
Inputs may be any that keep to these rules, and one draw needn't show every extreme that they name: `chosen`: for each aligned block of 64 token rows and each expert, 16 different row numbers within the block; so every device has exactly 64 slots for each expert.
All inputs are finite; a program needn't handle non-finite values.
Results may differ from a plain program's by a relative error of at most 0.017.
Values may be sent and summed in bfloat16 or wider, within the bound.
No kernel may reach another device: no remote copies, remote signals or barrier semaphores. Data moves between devices by JAX's collectives and lax.ppermute only.
A program may use at most 128 MiB of HBM per device.

v0:
```python
import functools

import jax
import jax.numpy as jnp
from jax import lax
from jax.experimental import pallas as pl
from jax.experimental.pallas import tpu as pltpu
from jax.sharding import PartitionSpec as P

F32 = jnp.float32
BF16 = jnp.bfloat16
VMEM = pl.BlockSpec(memory_space=pltpu.VMEM)
SMEM = pl.BlockSpec(memory_space=pltpu.SMEM)


def dot(a, b, dims=((1,), (0,))):
    return lax.dot_general(a, b, (dims, ((), ())), preferred_element_type=F32)


def call(kernel, outs, args, flops, scalars=0, scratch=()):
    sizes = [a.size * a.dtype.itemsize for a in args] + [
        o.size * o.dtype.itemsize for o in outs
    ]
    return pl.pallas_call(
        kernel,
        out_shape=list(outs),
        in_specs=[SMEM] * scalars + [VMEM] * (len(args) - scalars),
        out_specs=[VMEM] * len(outs),
        scratch_shapes=list(scratch),
        compiler_params=pltpu.CompilerParams(vmem_limit_bytes=40 << 20),
        cost_estimate=pl.CostEstimate(
            flops=int(flops), bytes_accessed=int(sum(sizes)), transcendentals=0
        ),
    )(*args)


def shape(dims, dtype):
    return jax.ShapeDtypeStruct(tuple(dims), dtype)


def hop(x, axis, size, target):
    return lax.ppermute(x, axis, [(i, target(i)) for i in range(size)])


def ring_order(n):
    return [i for i in range(0, n, 2)] + [i for i in range(n - 1, 0, -2)]


def ring_hop(x, n, step):
    order = ring_order(n)
    place = {d: q for q, d in enumerate(order)}
    return hop(x, "dp", n, lambda i: order[(place[i] + step) % n])


def hits(rows_ref, start, count, tok_rows, dtype=BF16):
    line = rows_ref[:, start : start + count]
    grid = lax.broadcasted_iota(jnp.int32, (tok_rows, count), 0)
    return (grid == line).astype(F32).astype(dtype)


def pick_rows(rows_ref, src_ref, start, count):
    one = hits(rows_ref, start, count, src_ref.shape[0])
    return dot(one, src_ref[...], ((0,), (0,))).astype(BF16)


def pick_kernel(part, rows_ref, src_ref, *outs):
    for k, out in enumerate(outs):
        out[...] = pick_rows(rows_ref, src_ref, k * 2 * part, 2 * part)


def pick_split_kernel(part, chips, rows_ref, src_ref, keep_ref, give_ref):
    for k in range(chips):
        both = pick_rows(rows_ref, src_ref, k * 2 * part, 2 * part)
        keep_ref[k * part : (k + 1) * part, :] = both[:part]
        give_ref[k * part : (k + 1) * part, :] = both[part:]


def front_kernel(part, chips, n, ids, *refs):
    recs = refs[:chips]
    sw, wr = refs[chips : chips + 2]
    gates = refs[chips + 2 : chips + 2 + n]
    ups = refs[chips + 2 + n : chips + 2 + 2 * n]
    xc, hd, sa, ua, gcol, x = refs[chips + 2 + 2 * n :]
    for k in range(chips):
        x[2 * k * part : (2 * k + 1) * part, :] = recs[k][:part, :]
        x[(2 * k + 1) * part : (2 * k + 2) * part, :] = sw[k * part : (k + 1) * part, :]
    width = x.shape[1] // n
    for d in range(n):
        xc[d] = x[:, d * width : (d + 1) * width]
    logits = dot(x[...], wr[...])
    lanes = lax.broadcasted_iota(jnp.int32, logits.shape, 1)
    mine = jnp.sum(jnp.where(lanes == ids[n], logits, 0.0), axis=1, keepdims=True)
    gcol[...] = jax.nn.sigmoid(mine)
    tile = 256
    hidden = hd.shape[1]

    def step(t, carry):
        cols = pl.ds(pl.multiple_of(t * tile, tile), tile)
        a = dot(xc[ids[0]], gates[0][:, cols])
        b = dot(xc[ids[0]], ups[0][:, cols])
        for s in range(1, n):
            a = a + dot(xc[ids[s]], gates[s][:, cols])
            b = b + dot(xc[ids[s]], ups[s][:, cols])
        sig = jax.nn.sigmoid(a)
        silu = a * sig
        hd[:, cols] = (silu * b).astype(BF16)
        sa[:, cols] = silu
        ua[:, cols] = b * sig * (1.0 + a * (1.0 - sig))
        return carry

    lax.fori_loop(0, hidden // tile, step, 0)


def down_kernel(part, chips, n, ids, keep0, got0, *refs):
    recs = refs[: chips - 1]
    gcol, hd = refs[chips - 1 : chips + 1]
    c, g = refs[chips + 1 : chips + 3]
    outs = refs[chips + 3 :]
    c[:part, :] = keep0[...]
    c[part : 2 * part, :] = got0[...]
    for k in range(1, chips):
        c[2 * k * part : 2 * (k + 1) * part, :] = recs[k - 1][...]
    g[...] = (gcol[...] * c[...].astype(F32)).astype(BF16)
    width = hd.shape[1] // n
    half = n // 2

    def chunk(s):
        cols = pl.ds(pl.multiple_of(ids[s] * width, 128), width)
        return dot(hd[:, cols], g[...], ((0,), (0,))).astype(BF16)

    far = chunk(half)
    outs[0][...] = far[: width // 2]
    outs[1][...] = far[width // 2 :]
    place = 2
    for s in range(n):
        if s != half:
            outs[place][...] = chunk(s)
            place += 1


def out_kernel(part, chips, n, ids, hd, c, gcol, xc, *refs):
    downs = refs[: n + 1]
    gos = refs[n + 1 : n + 1 + chips]
    dl, router = refs[n + 1 + chips : n + 3 + chips]
    width = hd.shape[1] // n
    half = n // 2

    def term(s):
        cols = pl.ds(pl.multiple_of(ids[s] * width, 128), width)
        if s == half:
            w = jnp.concatenate([downs[half][...], downs[n][...]], axis=0)
        else:
            w = downs[s][...]
        return dot(hd[:, cols], w)

    o = term(0)
    for s in range(1, n):
        o = o + term(s)
    o = o.astype(BF16).astype(F32)
    gate = gcol[...]
    go = (gate * o).astype(BF16)
    for k in range(chips):
        gos[k][...] = go[2 * k * part : 2 * (k + 1) * part]
    dgate = jnp.sum(c[...].astype(F32) * o, axis=1, keepdims=True)
    dlogit = (dgate * gate * (1.0 - gate)).astype(BF16)
    dl[...] = dlogit.astype(F32)
    chunk = xc.shape[2]
    for d in range(n):
        router[:, d * chunk : (d + 1) * chunk] = jnp.sum(
            xc[d].astype(F32) * dlogit.astype(F32), axis=0, keepdims=True
        )


def hidden_kernel(n, ids, g, sa, ua, *refs):
    downs = refs[: n + 1]
    da, db = refs[n + 1 :]
    width = sa.shape[1] // n
    half = n // 2
    for s in range(n):
        cols = pl.ds(pl.multiple_of(ids[s] * width, 128), width)
        if s == half:
            w = jnp.concatenate([downs[half][...], downs[n][...]], axis=0)
        else:
            w = downs[s][...]
        dh = dot(g[...], w, ((1,), (1,)))
        da[:, cols] = (dh * ua[:, cols]).astype(BF16)
        db[:, cols] = (dh * sa[:, cols]).astype(BF16)


def weight_kernel(n, order, ids, xc, da, db, *outs):
    tile = 256
    for place, s in enumerate(order):
        xt = xc[ids[s]].T
        gate, up = outs[2 * place], outs[2 * place + 1]

        def step(t, carry, xt=xt, gate=gate, up=up):
            cols = pl.ds(pl.multiple_of(t * tile, tile), tile)
            gate[:, cols] = dot(xt, da[:, cols]).astype(BF16)
            up[:, cols] = dot(xt, db[:, cols]).astype(BF16)
            return carry

        lax.fori_loop(0, da.shape[1] // tile, step, 0)


def rows_kernel(part, chips, n, ids, da, db, dl, wr, *refs):
    gates = refs[:n]
    ups = refs[n : 2 * n]
    keep, give, scr = refs[2 * n :]
    for s in range(n):
        scr[ids[s]] = dot(da[...], gates[s][...], ((1,), (1,))) + dot(
            db[...], ups[s][...], ((1,), (1,))
        )
    chunk = scr.shape[2]
    for d in range(n):
        cols = slice(d * chunk, (d + 1) * chunk)
        total = (scr[d] + dl[...] * wr[:, cols].astype(F32)).astype(BF16)
        for k in range(chips):
            lo = 2 * k * part
            keep[k * part : (k + 1) * part, cols] = total[lo : lo + part]
            give[k * part : (k + 1) * part, cols] = total[lo + part : lo + 2 * part]


def mixed_kernel(part, chips, rows_ref, *refs):
    recs = refs[:chips]
    sw, out = refs[chips:]
    tok_rows = out.shape[0]
    total = None
    for k in range(chips):
        one = hits(rows_ref, 2 * k * part, 2 * part, tok_rows)
        rows = jnp.concatenate([recs[k][:part, :], sw[k * part : (k + 1) * part, :]], axis=0)
        now = dot(one, rows)
        total = now if total is None else total + now
    out[...] = total.astype(BF16)


def grad_kernel(part, chips, rows_ref, keep0, got0, *refs):
    recs = refs[: chips - 1]
    out = refs[chips - 1]
    tok_rows = out.shape[0]
    total = None
    for k in range(chips):
        one = hits(rows_ref, 2 * k * part, 2 * part, tok_rows)
        if k == 0:
            rows = jnp.concatenate([keep0[...], got0[...]], axis=0)
        else:
            rows = recs[k - 1][...]
        now = dot(one, rows)
        total = now if total is None else total + now
    out[...] = total.astype(BF16)


def body(n, experts, tokens, cotangent, chosen, w_router, w_gate, w_up, w_down):
    tok_rows, model = tokens.shape
    blocks, _, picks = chosen.shape
    block_rows = tok_rows // blocks
    part = blocks * picks
    chips = experts // 2
    slots = experts * part
    half = n // 2
    gate_w, up_w, down_w = w_gate[0], w_up[0], w_down[0]
    hidden = gate_w.shape[1]

    d_me = lax.axis_index("dp")
    e_me = lax.axis_index("expert")
    place = jnp.where(d_me % 2 == 0, d_me // 2, n - 1 - d_me // 2)
    order = jnp.asarray(ring_order(n), jnp.int32)
    ids = jnp.concatenate(
        [order[(place + jnp.arange(n, dtype=jnp.int32)) % n], e_me[None].astype(jnp.int32)]
    )

    gate_p, up_n = ring_hop(gate_w, n, 1), ring_hop(up_w, n, -1)
    up_p, gate_n = ring_hop(up_w, n, 1), ring_hop(gate_w, n, -1)

    offsets = (jnp.arange(blocks, dtype=jnp.int32) * block_rows)[:, None, None]
    peers = e_me ^ jnp.arange(experts, dtype=jnp.int32)
    rows = jnp.transpose(jnp.take(chosen + offsets, peers, axis=1), (1, 0, 2)).reshape(1, slots)

    def exchange_z(bufs):
        return [
            bufs[k] if k == 0 else hop(bufs[k], "expert", experts, lambda i, k=k: i ^ (2 * k))
            for k in range(chips)
        ]

    def swap(x):
        return hop(x, "expert", experts, lambda i: i ^ 1)

    pick_flops = 2 * slots * tok_rows * model
    x_bufs = call(
        functools.partial(pick_kernel, part),
        [shape((2 * part, model), BF16)] * chips,
        [rows, tokens],
        pick_flops,
    )
    x_recs = exchange_z(x_bufs)
    x_sw = swap(jnp.concatenate([r[part:] for r in x_recs], axis=0))

    c_keep, c_give = call(
        functools.partial(pick_split_kernel, part, chips),
        [shape((chips * part, model), BF16)] * 2,
        [rows, cotangent],
        pick_flops,
    )
    c_got = swap(c_give)
    c_recs = exchange_z(
        [
            jnp.concatenate(
                [c_keep[k * part : (k + 1) * part], c_got[k * part : (k + 1) * part]], axis=0
            )
            if k
            else None
            for k in range(chips)
        ]
    )[1:]

    gates, ups = {0: gate_w, n - 1: gate_p, 1: gate_n}, {0: up_w, n - 1: up_p, 1: up_n}
    for s in range(2, half):
        gates[n - s] = ring_hop(gates[n - s + 1], n, 1)
        ups[s] = ring_hop(ups[s - 1], n, -1)
        ups[n - s] = ring_hop(ups[n - s + 1], n, 1)
        gates[s] = ring_hop(gates[s - 1], n, -1)
    if n > 2:
        gates[half] = ring_hop(gates[half + 1], n, 1)
        ups[half] = ring_hop(ups[half - 1], n, -1)
    downs = {0: down_w}
    for s in range(1, half):
        downs[n - s] = ring_hop(downs[(n - s + 1) % n], n, 1)
        downs[s] = ring_hop(downs[s - 1], n, -1)
    cut = down_w.shape[0] // 2
    far_a = ring_hop(downs[(half + 1) % n][:cut], n, 1)
    far_b = ring_hop(downs[half - 1][cut:], n, -1)
    gate_list = [gates[s] for s in range(n)]
    up_list = [ups[s] for s in range(n)]
    down_list = [far_a if s == half else downs[s] for s in range(n)] + [far_b]

    matmul = 2 * slots * model * hidden
    xc, hd, sa, ua, gcol = call(
        functools.partial(front_kernel, part, chips, n),
        [
            shape((n, slots, model // n), BF16),
            shape((slots, hidden), BF16),
            shape((slots, hidden), F32),
            shape((slots, hidden), F32),
            shape((slots, 1), F32),
        ],
        [ids, *x_recs, x_sw, w_router, *gate_list, *up_list],
        2 * matmul,
        scalars=1,
        scratch=[pltpu.VMEM((slots, model), BF16)],
    )
    width = hidden // n
    c_all, g_all, *down_parts = call(
        functools.partial(down_kernel, part, chips, n),
        [shape((slots, model), BF16)] * 2
        + [shape((width // 2, model), BF16)] * 2
        + [shape((width, model), BF16)] * (n - 1),
        [ids, c_keep[:part], c_got[:part], *c_recs, gcol, hd],
        matmul,
        scalars=1,
    )
    *go_bufs, dl, router_row = call(
        functools.partial(out_kernel, part, chips, n),
        [shape((2 * part, model), BF16)] * chips
        + [shape((slots, 1), F32), shape((1, model), F32)],
        [ids, hd, c_all, gcol, xc, *down_list],
        matmul,
        scalars=1,
    )
    o_recs = exchange_z(go_bufs)
    o_sw = swap(jnp.concatenate([r[part:] for r in o_recs], axis=0))

    down_of = {}
    place_in = 2
    for s in range(n):
        if s != half:
            down_of[s] = down_parts[place_in]
            place_in += 1
    low = ring_hop(down_parts[0], n, 1)
    high = ring_hop(down_parts[1], n, -1)

    def plus(a, b):
        return (a.astype(F32) + b.astype(F32)).astype(BF16)

    fwd = jnp.concatenate([plus(down_of[half - 1][:cut], low), down_of[half - 1][cut:]], axis=0)
    bwd_own = down_of[(half + 1) % n]
    bwd = jnp.concatenate([bwd_own[:cut], plus(bwd_own[cut:], high)], axis=0)
    for s in range(half - 1, 0, -1):
        fwd = ring_hop(fwd, n, 1)
        bwd = ring_hop(bwd, n, -1)
        if s > 1:
            fwd, bwd = plus(down_of[s - 1], fwd), plus(down_of[n - s + 1], bwd)
    down_grad = down_of[0].astype(F32) + fwd.astype(F32) + bwd.astype(F32)

    da, db = call(
        functools.partial(hidden_kernel, n),
        [shape((slots, hidden), BF16)] * 2,
        [ids, g_all, sa, ua, *down_list],
        matmul,
        scalars=1,
    )
    order_of = [half] + [s for s in range(n) if s != half]
    grads = call(
        functools.partial(weight_kernel, n, order_of),
        [shape((model // n, hidden), BF16)] * (2 * n),
        [ids, xc, da, db],
        2 * matmul,
        scalars=1,
    )
    gate_of = {s: grads[2 * i] for i, s in enumerate(order_of)}
    up_of = {s: grads[2 * i + 1] for i, s in enumerate(order_of)}

    wr_row = lax.dynamic_slice_in_dim(w_router.T, e_me, 1, axis=0)
    r_keep, r_give = call(
        functools.partial(rows_kernel, part, chips, n),
        [shape((chips * part, model), BF16)] * 2,
        [ids, da, db, dl, wr_row, *gate_list, *up_list],
        2 * matmul,
        scalars=1,
        scratch=[pltpu.VMEM((n, slots, model // n), F32)],
    )
    r_got = swap(r_give)
    r_recs = exchange_z(
        [
            jnp.concatenate(
                [r_keep[k * part : (k + 1) * part], r_got[k * part : (k + 1) * part]], axis=0
            )
            if k
            else None
            for k in range(chips)
        ]
    )[1:]

    fwd_g, bwd_u = ring_hop(gate_of[half], n, 1), ring_hop(up_of[half], n, -1)
    fwd = (plus(gate_of[half - 1], fwd_g), up_of[half - 1])
    bwd = (gate_of[(half + 1) % n], plus(up_of[(half + 1) % n], bwd_u))
    for s in range(half - 1, 0, -1):
        fwd = tuple(ring_hop(v, n, 1) for v in fwd)
        bwd = tuple(ring_hop(v, n, -1) for v in bwd)
        if s > 1:
            fwd = (plus(gate_of[s - 1], fwd[0]), plus(up_of[s - 1], fwd[1]))
            bwd = (plus(gate_of[n - s + 1], bwd[0]), plus(up_of[n - s + 1], bwd[1]))
    grad_gate = gate_of[0].astype(F32) + fwd[0].astype(F32) + bwd[0].astype(F32)
    grad_up = up_of[0].astype(F32) + fwd[1].astype(F32) + bwd[1].astype(F32)

    total = router_row
    bit = 1
    while bit < n:
        total = total + hop(total, "dp", n, lambda i, b=bit: i ^ b)
        bit *= 2
    bit = 1
    while bit < experts:
        total = jnp.concatenate(
            [total, hop(total, "expert", experts, lambda i, b=bit: i ^ b)], axis=0
        )
        bit *= 2
    grad_router = jnp.take(total, peers, axis=0).T

    mixed = call(
        functools.partial(mixed_kernel, part, chips),
        [shape((tok_rows, model), BF16)],
        [rows, *o_recs, o_sw],
        pick_flops,
    )[0]
    grad_tokens = call(
        functools.partial(grad_kernel, part, chips),
        [shape((tok_rows, model), BF16)],
        [rows, r_keep[:part], r_got[:part], *r_recs],
        pick_flops,
    )[0]
    return (
        mixed,
        grad_tokens,
        grad_gate[None],
        grad_up[None],
        down_grad[None],
        grad_router,
    )


def solution(mesh):
    sizes = dict(mesh.shape)
    return jax.shard_map(
        functools.partial(body, sizes["dp"], sizes["expert"]),
        mesh=mesh,
        in_specs=(
            P(("dp", "expert"), None),
            P(("dp", "expert"), None),
            P(("dp", "expert"), None, None),
            P(),
            P("expert", "dp", None),
            P("expert", "dp", None),
            P("expert", "dp", None),
        ),
        out_specs=(
            P(("dp", "expert"), None),
            P(("dp", "expert"), None),
            P("expert", "dp", None),
            P("expert", "dp", None),
            P("expert", "dp", None),
            P(),
        ),
        check_vma=False,
    )
```

profile of v0, /device:TPU:0, one launch (start us, length us, event | category | flops | bytes accessed | tf_op | source)
XLA Modules:
  0.0 267.5 jit_solution(12598100738972514162)
XLA Ops:
  4.0 3.1 %collective-permute-start = (bf16[128,1536]{1,0:T(8,128)(2,1)S(1)}, bf16[128,1536]{1,0:T(8,128)(2,1)S(1)}, u32[]{:S(2)}, u32[]{:S(2)}) collective-permute-start(bf16[128,1536]{1,0:T(8,128)(2,1)S(1)} %get-tuple-element.43), channel_id=1, source_target_pairs={{0,2},{1,3},{2,0},{3,1},{4,6},{5,7},{6,4},{7,5},{8,10},{9,11},{10,... | collective-permute-start | bytes 1179656 | tf_op jit(solution)/shard_map/ppermute | solution.py:42
  7.1 2.6 collective-permute-start.1
  9.7 1.7 collective-permute-start.5
  12.8 1.5 shard_map.129
  14.3 9.5 %collective-permute-done.refs_1_ = bf16[128,1536]{1,0:T(8,128)(2,1)S(1)} collective-permute-done((bf16[128,1536]{1,0:T(8,128)(2,1)S(1)}, bf16[128,1536]{1,0:T(8,128)(2,1)S(1)}, u32[]{:S(2)}, u32[]{:S(2)}) %collective-permute-start) | collective-permute-done | bytes 393248 | tf_op jit(solution)/shard_map/ppermute | solution.py:42
  24.7 12.2 %collective-permute-done.1.refs_2_ = bf16[128,1536]{1,0:T(8,128)(2,1)S(1)} collective-permute-done((bf16[128,1536]{1,0:T(8,128)(2,1)S(1)}, bf16[128,1536]{1,0:T(8,128)(2,1)S(1)}, u32[]{:S(2)}, u32[]{:S(2)}) %collective-permute-start.1) | collective-permute-done | bytes 393248 | tf_op jit(solution)/shard_map/ppermute | solution.py:42
  36.9 1.5 collective-permute-start.4
  40.5 1.6 collective-permute-start.15
  43.9 13.4 %collective-permute-done.4.refs_7_.refs_1_ = bf16[384,1024]{1,0:T(8,128)(2,1)} collective-permute-done((bf16[384,1024]{1,0:T(8,128)(2,1)}, bf16[384,1024]{1,0:T(8,128)(2,1)}, u32[]{:S(2)}, u32[]{:S(2)}) %collective-permute-start.4) | collective-permute-done | bytes 786464 | tf_op jit(solution)/shard_map/ppermute | solution.py:42
  57.3 1.8 collective-permute-start.6
  59.2 1.5 collective-permute-start.8
  60.8 15.1 %collective-permute-done.15.refs_3_ = bf16[256,1536]{1,0:T(8,128)(2,1)S(1)} collective-permute-done((bf16[256,1536]{1,0:T(8,128)(2,1)S(1)}, bf16[256,1536]{1,0:T(8,128)(2,1)S(1)}, u32[]{:S(2)}, u32[]{:S(2)}) %collective-permute-start.15) | collective-permute-done | bytes 786464 | tf_op jit(solution)/shard_map/ppermute | solution.py:42
  75.9 6.1 %collective-permute-start.11 = (bf16[128,1536]{1,0:T(8,128)(2,1)S(1)}, bf16[128,1536]{1,0:T(8,128)(2,1)S(1)}, u32[]{:S(2)}, u32[]{:S(2)}) collective-permute-start(bf16[128,1536]{1,0:T(8,128)(2,1)S(1)} %pad_maximum_fusion.4), channel_id=1, source_target_pairs={{0,2},{1,3},{2,0},{3,1},{4,6},{5,7},{6,4},{7,5},{8,10},{9,11},{10,... | collective-permute-start | bytes 1179656 | tf_op jit(solution)/shard_map/ppermute | solution.py:42
  83.0 1.5 collective-permute-start.13
  84.7 5.2 %collective-permute-done.6.refs_8_.refs_2_ = bf16[384,1024]{1,0:T(8,128)(2,1)S(1)} collective-permute-done((bf16[384,1024]{1,0:T(8,128)(2,1)}, bf16[384,1024]{1,0:T(8,128)(2,1)S(1)}, u32[]{:S(2)}, u32[]{:S(2)}) %collective-permute-start.6) | collective-permute-done | bytes 786464 | tf_op jit(solution)/shard_map/ppermute | solution.py:42
  91.9 9.7 %shard_map.128 = (bf16[4,512,384]{2,1,0:T(8,128)(2,1)S(1)}, bf16[512,1024]{1,0:T(8,128)(2,1)S(1)}, f32[512,1024]{1,0:T(8,128)S(1)}, f32[512,1024]{1,0:T(8,128)}, f32[512,1]{1,0:T(8,128)S(1)}) custom-call(s32[5]{0:T(128)S(1)} %pad_add_fusion.ids, bf16[128,1536]{1,0:T(8,128)(2,1)S(1)} %get-tuple-element.42.refs_0_, ...), custom_call_target="tpu_custom_call" | custom-call | flops 3221225472 | bytes 15493140 | tf_op jit(solution)/shard_map/pallas_call | solution.py:24
  101.5 8.9 %collective-permute-done.12.refs_1_ = bf16[128,1536]{1,0:T(8,128)(2,1)S(1)} collective-permute-done((bf16[128,1536]{1,0:T(8,128)(2,1)S(1)}, bf16[128,1536]{1,0:T(8,128)(2,1)S(1)}, u32[]{:S(2)}, u32[]{:S(2)}) %collective-permute-start.12) | collective-permute-done | bytes 393248 | tf_op jit(solution)/shard_map/ppermute | solution.py:42
  110.4 2.9 %shard_map.130 = (bf16[512,1536]{1,0:T(8,128)(2,1)S(1)}, bf16[512,1536]{1,0:T(8,128)(2,1)S(1)}, bf16[128,1536]{1,0:T(8,128)(2,1)}, bf16[128,1536]{1,0:T(8,128)(2...) custom-call(s32[5]{0:T(128)S(1)} %pad_add_fusion.ids, ...), custom_call_target="tpu_custom_call" | custom-call | flops 1610612736 | bytes 8914964 | tf_op jit(solution)/shard_map/pallas_call | solution.py:24
  113.3 3.5 %shard_map.131 = (bf16[128,1536]{1,0:T(8,128)(2,1)S(1)}, bf16[128,1536]{1,0:T(8,128)(2,1)}, bf16[128,1536]{1,0:T(8,128)(2,1)}, bf16[128,1536]{1,0:T(8,128)(2,1)S...) custom-call(s32[5]{0:T(128)S(1)} %pad_add_fusion.ids, bf16[512,1024]{1,0:T(8,128)(2,1)S(1)} %get-tuple-element.46.refs_4_.hd, ...), custom_call_target="tpu_custom_call" | custom-call | flops 1610612736 | bytes 8923156 | tf_op jit(solution)/shard_map/pallas_call | solution.py:24
  116.8 1.5 collective-permute-start.36
  119.0 1.6 collective-permute-start.32
  121.1 1.6 collective-permute-start.37
  122.7 2.5 shard_map.133
  125.2 3.4 %collective-permute-done.37 = f32[1,1536]{1,0:T(1,128)S(1)} collective-permute-done((f32[1,1536]{1,0:T(1,128)S(1)}, f32[1,1536]{1,0:T(1,128)S(1)}, u32[]{:S(2)}, u32[]{:S(2)}) %collective-permute-start.37) | collective-permute-done | bytes 6176 | tf_op jit(solution)/shard_map/ppermute | solution.py:42
  128.8 7.8 %shard_map.136 = (bf16[384,1024]{1,0:T(8,128)(2,1)S(1)}, bf16[384,1024]{1,0:T(8,128)(2,1)}, bf16[384,1024]{1,0:T(8,128)(2,1)S(1)}, bf16[384,1024]{1,0:T(8,128)(2...) custom-call(s32[5]{0:T(128)S(1)} %pad_add_fusion.ids, ...), custom_call_target="tpu_custom_call" | custom-call | flops 3221225472 | bytes 9961492 | tf_op jit(solution)/shard_map/pallas_call | solution.py:24
  139.2 4.8 %collective-permute-start.39 = (f32[2,1536]{1,0:T(2,128)S(1)}, f32[2,1536]{1,0:T(2,128)S(1)}, u32[]{:S(2)}, u32[]{:S(2)}) collective-permute-start(f32[2,1536]{1,0:T(2,128)S(1)} %pad_maximum_fusion.12), channel_id=1, source_target_pairs={{0,2},{1,3},{2,0},{3,1},{4,6},{5,7},{6,4},{7,5},{8,10},{9,11},{10,... | collective-permute-start | bytes 36872 | tf_op jit(solution)/shard_map/ppermute | solution.py:42
  144.0 7.4 %shard_map.134 = (bf16[256,1536]{1,0:T(8,128)(2,1)S(1)}, bf16[256,1536]{1,0:T(8,128)(2,1)S(1)}) custom-call(s32[5]{0:T(128)S(1)} %pad_add_fusion.ids, bf16[512,1024]{1,0:T(8,128)(2,1)S(1)} %get-tuple-element.59.da, bf16[512,1024]{1,0:T(8,128)(2,1)S(1)} %get-tuple-element.60.db, f32[512,1]{1,0:T(8,128)S(1)} %get-tuple-element.61.dl, ...), custom_call_target="tpu_custom_call" | custom-call | flops 3221225472 | bytes 9966612 | tf_op jit(solution)/shard_map/pallas_call | solution.py:24
  151.5 1.9 collective-permute-start.40
  156.6 1.5 collective-permute-start.19
  158.8 2.0 gather_fusion.2
  160.8 1.6 select_bitcast_fusion
  164.8 7.4 %collective-permute-done.18.refs_1_ = bf16[128,1536]{1,0:T(8,128)(2,1)S(1)} collective-permute-done((bf16[128,1536]{1,0:T(8,128)(2,1)}, bf16[128,1536]{1,0:T(8,128)(2,1)S(1)}, u32[]{:S(2)}, u32[]{:S(2)}) %collective-permute-start.18) | collective-permute-done | bytes 393248 | tf_op jit(solution)/shard_map/ppermute | solution.py:42
  173.3 13.4 %collective-permute-done.19.refs_2_ = bf16[128,1536]{1,0:T(8,128)(2,1)S(1)} collective-permute-done((bf16[128,1536]{1,0:T(8,128)(2,1)}, bf16[128,1536]{1,0:T(8,128)(2,1)S(1)}, u32[]{:S(2)}, u32[]{:S(2)}) %collective-permute-start.19) | collective-permute-done | bytes 393248 | tf_op jit(solution)/shard_map/ppermute | solution.py:42
  186.8 1.8 collective-permute-start.33
  191.0 2.6 collective-permute-start.25
  193.9 5.9 %collective-permute-start.24 = (bf16[128,1536]{1,0:T(8,128)(2,1)S(1)}, bf16[128,1536]{1,0:T(8,128)(2,1)S(1)}, u32[]{:S(2)}, u32[]{:S(2)}) collective-permute-start(bf16[128,1536]{1,0:T(8,128)(2,1)S(1)} %pad_maximum_fusion.8), channel_id=1, source_target_pairs={{0,4},{1,5},{2,6},{3,7},{4,0},{5,1},{6,2},{7,3},{8,12},{9,13},{10,... | collective-permute-start | bytes 1179656 | tf_op jit(solution)/shard_map/ppermute | solution.py:42
  199.8 5.1 %collective-permute-done.25.refs_2_ = bf16[128,1536]{1,0:T(8,128)(2,1)S(1)} collective-permute-done((bf16[128,1536]{1,0:T(8,128)(2,1)S(1)}, bf16[128,1536]{1,0:T(8,128)(2,1)S(1)}, u32[]{:S(2)}, u32[]{:S(2)}) %collective-permute-start.25) | collective-permute-done | bytes 393248 | tf_op jit(solution)/shard_map/ppermute | solution.py:42
  204.9 16.7 %collective-permute-start.23 = (bf16[128,1536]{1,0:T(8,128)(2,1)S(1)}, bf16[128,1536]{1,0:T(8,128)(2,1)S(1)}, u32[]{:S(2)}, u32[]{:S(2)}) collective-permute-start(bf16[128,1536]{1,0:T(8,128)(2,1)S(1)} %pad_maximum_fusion.7), channel_id=1, source_target_pairs={{0,2},{1,3},{2,0},{3,1},{4,6},{5,7},{6,4},{7,5},{8,10},{9,11},{10,... | collective-permute-start | bytes 1179656 | tf_op jit(solution)/shard_map/ppermute | solution.py:42
  223.0 6.5 %collective-permute-done.24.refs_1_ = bf16[128,1536]{1,0:T(8,128)(2,1)S(1)} collective-permute-done((bf16[128,1536]{1,0:T(8,128)(2,1)S(1)}, bf16[128,1536]{1,0:T(8,128)(2,1)S(1)}, u32[]{:S(2)}, u32[]{:S(2)}) %collective-permute-start.24) | collective-permute-done | bytes 393248 | tf_op jit(solution)/shard_map/ppermute | solution.py:42
  229.6 2.0 collective-permute-start.31
  231.9 1.8 shard_map.132
  233.7 4.1 %collective-permute-done.23.refs_0_ = bf16[128,1536]{1,0:T(8,128)(2,1)S(1)} collective-permute-done((bf16[128,1536]{1,0:T(8,128)(2,1)S(1)}, bf16[128,1536]{1,0:T(8,128)(2,1)S(1)}, u32[]{:S(2)}, u32[]{:S(2)}) %collective-permute-start.23) | collective-permute-done | bytes 393248 | tf_op jit(solution)/shard_map/ppermute | solution.py:42
  238.2 1.8 shard_map.135
  240.0 1.7 collective-permute-start.27
  243.1 6.8 %collective-permute-done.29 = bf16[384,1024]{1,0:T(8,128)(2,1)S(1)} collective-permute-done((bf16[384,1024]{1,0:T(8,128)(2,1)S(1)}, bf16[384,1024]{1,0:T(8,128)(2,1)S(1)}, u32[]{:S(2)}, u32[]{:S(2)}) %collective-permute-start.29) | collective-permute-done | bytes 786464 | tf_op jit(solution)/shard_map/ppermute | solution.py:42
  250.0 1.6 add_bitcast_fusion.1
  251.5 14.3 %collective-permute-done.28 = bf16[384,1024]{1,0:T(8,128)(2,1)S(1)} collective-permute-done((bf16[384,1024]{1,0:T(8,128)(2,1)S(1)}, bf16[384,1024]{1,0:T(8,128)(2,1)S(1)}, u32[]{:S(2)}, u32[]{:S(2)}) %collective-permute-start.28) | collective-permute-done | bytes 786464 | tf_op jit(solution)/shard_map/ppermute | solution.py:42
  265.9 1.6 add_bitcast_fusion.2
  (173 shorter events, 30.3 us)
Async XLA Ops:
  4.0 19.9 %collective-permute-start = (bf16[128,1536]{1,0:T(8,128)(2,1)S(1)}, bf16[128,1536]{1,0:T(8,128)(2,1)S(1)}, u32[]{:S(2)}, u32[]{:S(2)}) collective-permute-start(bf16[128,1536]{1,0:T(8,128)(2,1)S(1)} %get-tuple-element.43), channel_id=1, source_target_pairs={{0,2},{1,3},{2,0},{3,1},{4,6},{5,7},{6,4},{7,5},{8,10},{9,11},{10,... | collective-permute-start | bytes 1179656 | tf_op jit(solution)/shard_map/ppermute | solution.py:42
  7.1 29.8 %collective-permute-start.1 = (bf16[128,1536]{1,0:T(8,128)(2,1)S(1)}, bf16[128,1536]{1,0:T(8,128)(2,1)S(1)}, u32[]{:S(2)}, u32[]{:S(2)}) collective-permute-start(bf16[128,1536]{1,0:T(8,128)(2,1)S(1)} %get-tuple-element.44), channel_id=1, source_target_pairs={{0,4},{1,5},{2,6},{3,7},{4,0},{5,1},{6,2},{7,3},{8,12},{9,13},{10,... | collective-permute-start | bytes 1179656 | tf_op jit(solution)/shard_map/ppermute | solution.py:42
  9.7 28.7 %collective-permute-start.2 = (bf16[128,1536]{1,0:T(8,128)(2,1)S(1)}, bf16[128,1536]{1,0:T(8,128)(2,1)S(1)}, u32[]{:S(2)}, u32[]{:S(2)}) collective-permute-start(bf16[128,1536]{1,0:T(8,128)(2,1)S(1)} %get-tuple-element.45), channel_id=1, source_target_pairs={{0,6},{1,7},{2,4},{3,5},{4,2},{5,3},{6,0},{7,1},{8,14},{9,15},{10,... | collective-permute-start | bytes 1179656 | tf_op jit(solution)/shard_map/ppermute | solution.py:42
  9.7 30.8 %collective-permute-start.5 = (bf16[384,1024]{1,0:T(8,128)(2,1)}, bf16[384,1024]{1,0:T(8,128)(2,1)}, u32[]{:S(2)}, u32[]{:S(2)}) collective-permute-start(bf16[384,1024]{1,0:T(8,128)(2,1)} %bitcast.3.refs_6_.refs_0_), channel_id=1, source_target_pairs={{0,16},{8,0},{16,24},{24,8},{1,17},{9,1},{17,25},{25,9},{2,18},{10... | collective-permute-start | bytes 2359304 | tf_op jit(solution)/shard_map/ppermute | solution.py:42
  11.4 30.7 %collective-permute-start.7 = (bf16[384,1024]{1,0:T(8,128)(2,1)}, bf16[384,1024]{1,0:T(8,128)(2,1)}, u32[]{:S(2)}, u32[]{:S(2)}) collective-permute-start(bf16[384,1024]{1,0:T(8,128)(2,1)} %bitcast.4.refs_10_.refs_4_), channel_id=1, source_target_pairs={{0,8},{8,24},{16,0},{24,16},{1,9},{9,25},{17,1},{25,17},{2,10},{10... | collective-permute-start | bytes 2359304 | tf_op jit(solution)/shard_map/ppermute | solution.py:42
  12.8 26.3 %copy-start.25 = (s32[4]{0:T(128)S(1)}, s32[4]{0:T(128)}, u32[]{:S(2)}) copy-start(s32[4]{0:T(128)} %constant.85.clone) | copy-start | bytes 52
  14.3 24.6 %copy-start.35 = (bf16[1536,8]{0,1:T(8,128)(2,1)S(1)}, bf16[1536,8]{0,1:T(8,128)(2,1)}, u32[]{:S(2)}) copy-start(bf16[1536,8]{0,1:T(8,128)(2,1)} %param.11) | copy-start | bytes 73732
  23.8 18.8 %collective-permute-start.10 = (bf16[256,1536]{1,0:T(8,128)(2,1)}, bf16[256,1536]{1,0:T(8,128)(2,1)}, u32[]{:S(2)}, u32[]{:S(2)}) collective-permute-start(bf16[256,1536]{1,0:T(8,128)(2,1)} %get-tuple-element.48), channel_id=1, source_target_pairs={{0,1},{1,0},{2,3},{3,2},{4,5},{5,4},{6,7},{7,6},{8,9},{9,8},{10,11... | collective-permute-start | bytes 2359304 | tf_op jit(solution)/shard_map/ppermute | solution.py:42
  36.9 20.4 %collective-permute-start.4 = (bf16[384,1024]{1,0:T(8,128)(2,1)}, bf16[384,1024]{1,0:T(8,128)(2,1)}, u32[]{:S(2)}, u32[]{:S(2)}) collective-permute-start(bf16[384,1024]{1,0:T(8,128)(2,1)} %bitcast.3.refs_6_.refs_0_), channel_id=1, source_target_pairs={{0,8},{8,24},{16,0},{24,16},{1,9},{9,25},{17,1},{25,17},{2,10},{10... | collective-permute-start | bytes 2359304 | tf_op jit(solution)/shard_map/ppermute | solution.py:42
  38.4 20.8 %collective-permute-start.9 = (bf16[384,1024]{1,0:T(8,128)(2,1)}, bf16[384,1024]{1,0:T(8,128)(2,1)}, u32[]{:S(2)}, u32[]{:S(2)}) collective-permute-start(bf16[384,1024]{1,0:T(8,128)(2,1)} %bitcast.4.refs_10_.refs_4_), channel_id=1, source_target_pairs={{0,16},{8,0},{16,24},{24,8},{1,17},{9,1},{17,25},{25,9},{2,18},{10... | collective-permute-start | bytes 2359304 | tf_op jit(solution)/shard_map/ppermute | solution.py:42
  40.5 35.4 %collective-permute-start.15 = (bf16[256,1536]{1,0:T(8,128)(2,1)S(1)}, bf16[256,1536]{1,0:T(8,128)(2,1)S(1)}, u32[]{:S(2)}, u32[]{:S(2)}) collective-permute-start(bf16[256,1536]{1,0:T(8,128)(2,1)S(1)} %bitcast.18), channel_id=1, source_target_pairs={{0,16},{8,0},{16,24},{24,8},{1,17},{9,1},{17,25},{25,9},{2,18},{10... | collective-permute-start | bytes 2359304 | tf_op jit(solution)/shard_map/ppermute | solution.py:42
  42.1 39.9 %collective-permute-start.14 = (bf16[256,1536]{1,0:T(8,128)(2,1)S(1)}, bf16[256,1536]{1,0:T(8,128)(2,1)S(1)}, u32[]{:S(2)}, u32[]{:S(2)}) collective-permute-start(bf16[256,1536]{1,0:T(8,128)(2,1)S(1)} %bitcast.19), channel_id=1, source_target_pairs={{0,8},{8,24},{16,0},{24,16},{1,9},{9,25},{17,1},{25,17},{2,10},{10... | collective-permute-start | bytes 2359304 | tf_op jit(solution)/shard_map/ppermute | solution.py:42
  42.6 40.4 %collective-permute-start.3 = (bf16[256,1536]{1,0:T(8,128)(2,1)S(1)}, bf16[256,1536]{1,0:T(8,128)(2,1)S(1)}, u32[]{:S(2)}, u32[]{:S(2)}) collective-permute-start(bf16[256,1536]{1,0:T(8,128)(2,1)S(1)} %pad_maximum_fusion), channel_id=1, source_target_pairs={{0,1},{1,0},{2,3},{3,2},{4,5},{5,4},{6,7},{7,6},{8,9},{9,8},{10,11... | collective-permute-start | bytes 2359304 | tf_op jit(solution)/shard_map/ppermute | solution.py:42
  43.9 40.7 %copy-start.36 = (s32[4]{0:T(128)S(1)}, s32[4]{0:T(128)}, u32[]{:S(2)}) copy-start(s32[4]{0:T(128)} %gather_fusion.1) | copy-start | bytes 52
  57.3 32.5 %collective-permute-start.6 = (bf16[384,1024]{1,0:T(8,128)(2,1)}, bf16[384,1024]{1,0:T(8,128)(2,1)S(1)}, u32[]{:S(2)}, u32[]{:S(2)}) collective-permute-start(bf16[384,1024]{1,0:T(8,128)(2,1)} %collective-permute-done.5.refs_9_.refs_3_), channel_id=1, source_target_pairs={{0,16},{8,0},{16,24},{24,8},{1,17},{9,1},{17,25},{25,9},{2,18},{10... | collective-permute-start | bytes 2359304 | tf_op jit(solution)/shard_map/ppermute | solution.py:42
  59.2 31.4 %collective-permute-start.8 = (bf16[384,1024]{1,0:T(8,128)(2,1)}, bf16[384,1024]{1,0:T(8,128)(2,1)S(1)}, u32[]{:S(2)}, u32[]{:S(2)}) collective-permute-start(bf16[384,1024]{1,0:T(8,128)(2,1)} %collective-permute-done.7.refs_11_.refs_5_), channel_id=1, source_target_pairs={{0,8},{8,24},{16,0},{24,16},{1,9},{9,25},{17,1},{25,17},{2,10},{10... | collective-permute-start | bytes 2359304 | tf_op jit(solution)/shard_map/ppermute | solution.py:42
  75.9 25.6 %collective-permute-start.11 = (bf16[128,1536]{1,0:T(8,128)(2,1)S(1)}, bf16[128,1536]{1,0:T(8,128)(2,1)S(1)}, u32[]{:S(2)}, u32[]{:S(2)}) collective-permute-start(bf16[128,1536]{1,0:T(8,128)(2,1)S(1)} %pad_maximum_fusion.4), channel_id=1, source_target_pairs={{0,2},{1,3},{2,0},{3,1},{4,6},{5,7},{6,4},{7,5},{8,10},{9,11},{10,... | collective-permute-start | bytes 1179656 | tf_op jit(solution)/shard_map/ppermute | solution.py:42
  82.0 28.4 %collective-permute-start.12 = (bf16[128,1536]{1,0:T(8,128)(2,1)S(1)}, bf16[128,1536]{1,0:T(8,128)(2,1)S(1)}, u32[]{:S(2)}, u32[]{:S(2)}) collective-permute-start(bf16[128,1536]{1,0:T(8,128)(2,1)S(1)} %pad_maximum_fusion.5), channel_id=1, source_target_pairs={{0,4},{1,5},{2,6},{3,7},{4,0},{5,1},{6,2},{7,3},{8,12},{9,13},{10,... | collective-permute-start | bytes 1179656 | tf_op jit(solution)/shard_map/ppermute | solution.py:42
  83.0 27.4 %collective-permute-start.13 = (bf16[128,1536]{1,0:T(8,128)(2,1)S(1)}, bf16[128,1536]{1,0:T(8,128)(2,1)S(1)}, u32[]{:S(2)}, u32[]{:S(2)}) collective-permute-start(bf16[128,1536]{1,0:T(8,128)(2,1)S(1)} %pad_maximum_fusion.6), channel_id=1, source_target_pairs={{0,6},{1,7},{2,4},{3,5},{4,2},{5,3},{6,0},{7,1},{8,14},{9,15},{10,... | collective-permute-start | bytes 1179656 | tf_op jit(solution)/shard_map/ppermute | solution.py:42
  89.8 23.4 %collective-permute-start.16 = (bf16[128,1536]{1,0:T(8,128)(2,1)S(1)}, bf16[128,1536]{1,0:T(8,128)(2,1)S(1)}, u32[]{:S(2)}, u32[]{:S(2)}) collective-permute-start(bf16[128,1536]{1,0:T(8,128)(2,1)S(1)} %slice.133), channel_id=1, source_target_pairs={{0,16},{8,0},{16,24},{24,8},{1,17},{9,1},{17,25},{25,9},{2,18},{10... | collective-permute-start | bytes 1179656 | tf_op jit(solution)/shard_map/ppermute | solution.py:42
  90.5 22.7 %collective-permute-start.17 = (bf16[128,1536]{1,0:T(8,128)(2,1)S(1)}, bf16[128,1536]{1,0:T(8,128)(2,1)S(1)}, u32[]{:S(2)}, u32[]{:S(2)}) collective-permute-start(bf16[128,1536]{1,0:T(8,128)(2,1)S(1)} %slice.134), channel_id=1, source_target_pairs={{0,8},{8,24},{16,0},{24,16},{1,9},{9,25},{17,1},{25,17},{2,10},{10... | collective-permute-start | bytes 1179656 | tf_op jit(solution)/shard_map/ppermute | solution.py:42
  116.8 4.3 %collective-permute-start.36 = (f32[1,1536]{1,0:T(1,128)S(1)}, f32[1,1536]{1,0:T(1,128)S(1)}, u32[]{:S(2)}, u32[]{:S(2)}) collective-permute-start(f32[1,1536]{1,0:T(1,128)S(1)} %get-tuple-element.77), channel_id=1, source_target_pairs={{0,8},{8,0},{16,24},{24,16},{1,9},{9,1},{17,25},{25,17},{2,10},{10... | collective-permute-start | bytes 18440 | tf_op jit(solution)/shard_map/ppermute | solution.py:42
  119.0 43.4 %collective-permute-start.32 = (bf16[128,1536]{1,0:T(8,128)(2,1)}, bf16[128,1536]{1,0:T(8,128)(2,1)}, u32[]{:S(2)}, u32[]{:S(2)}) collective-permute-start(bf16[128,1536]{1,0:T(8,128)(2,1)} %get-tuple-element.74), channel_id=1, source_target_pairs={{0,16},{8,0},{16,24},{24,8},{1,17},{9,1},{17,25},{25,9},{2,18},{10... | collective-permute-start | bytes 1179656 | tf_op jit(solution)/shard_map/ppermute | solution.py:42
  120.6 68.0 %collective-permute-start.34 = (bf16[128,1536]{1,0:T(8,128)(2,1)}, bf16[128,1536]{1,0:T(8,128)(2,1)}, u32[]{:S(2)}, u32[]{:S(2)}) collective-permute-start(bf16[128,1536]{1,0:T(8,128)(2,1)} %get-tuple-element.76), channel_id=1, source_target_pairs={{0,8},{8,24},{16,0},{24,16},{1,9},{9,25},{17,1},{25,17},{2,10},{10... | collective-permute-start | bytes 1179656 | tf_op jit(solution)/shard_map/ppermute | solution.py:42
  121.1 7.6 %collective-permute-start.37 = (f32[1,1536]{1,0:T(1,128)S(1)}, f32[1,1536]{1,0:T(1,128)S(1)}, u32[]{:S(2)}, u32[]{:S(2)}) collective-permute-start(f32[1,1536]{1,0:T(1,128)S(1)} %add.125), channel_id=1, source_target_pairs={{0,16},{8,24},{16,0},{24,8},{1,17},{9,25},{17,1},{25,9},{2,18},{10... | collective-permute-start | bytes 18440 | tf_op jit(solution)/shard_map/ppermute | solution.py:42
  128.7 10.5 %collective-permute-start.38 = (f32[1,1536]{1,0:T(1,128)S(1)}, f32[1,1536]{1,0:T(1,128)S(1)}, u32[]{:S(2)}, u32[]{:S(2)}) collective-permute-start(f32[1,1536]{1,0:T(1,128)S(1)} %add.126), channel_id=1, source_target_pairs={{0,1},{1,0},{2,3},{3,2},{4,5},{5,4},{6,7},{7,6},{8,9},{9,8},{10,11... | collective-permute-start | bytes 18440 | tf_op jit(solution)/shard_map/ppermute | solution.py:42
  139.2 54.5 %collective-permute-start.30 = (bf16[384,1024]{1,0:T(8,128)(2,1)}, bf16[384,1024]{1,0:T(8,128)(2,1)}, u32[]{:S(2)}, u32[]{:S(2)}) collective-permute-start(bf16[384,1024]{1,0:T(8,128)(2,1)} %get-tuple-element.71), channel_id=1, source_target_pairs={{0,8},{8,24},{16,0},{24,16},{1,9},{9,25},{17,1},{25,17},{2,10},{10... | collective-permute-start | bytes 2359304 | tf_op jit(solution)/shard_map/ppermute | solution.py:42
  139.2 12.3 %collective-permute-start.39 = (f32[2,1536]{1,0:T(2,128)S(1)}, f32[2,1536]{1,0:T(2,128)S(1)}, u32[]{:S(2)}, u32[]{:S(2)}) collective-permute-start(f32[2,1536]{1,0:T(2,128)S(1)} %pad_maximum_fusion.12), channel_id=1, source_target_pairs={{0,2},{1,3},{2,0},{3,1},{4,6},{5,7},{6,4},{7,5},{8,10},{9,11},{10,... | collective-permute-start | bytes 36872 | tf_op jit(solution)/shard_map/ppermute | solution.py:42
  151.5 5.1 %collective-permute-start.40 = (f32[4,1536]{1,0:T(4,128)S(1)}, f32[4,1536]{1,0:T(4,128)S(1)}, u32[]{:S(2)}, u32[]{:S(2)}) collective-permute-start(f32[4,1536]{1,0:T(4,128)S(1)} %pad_maximum_fusion.11), channel_id=1, source_target_pairs={{0,4},{1,5},{2,6},{3,7},{4,0},{5,1},{6,2},{7,3},{8,12},{9,13},{10,... | collective-permute-start | bytes 73736 | tf_op jit(solution)/shard_map/ppermute | solution.py:42
  154.3 17.9 %collective-permute-start.18 = (bf16[128,1536]{1,0:T(8,128)(2,1)}, bf16[128,1536]{1,0:T(8,128)(2,1)S(1)}, u32[]{:S(2)}, u32[]{:S(2)}) collective-permute-start(bf16[128,1536]{1,0:T(8,128)(2,1)} %get-tuple-element.53), channel_id=1, source_target_pairs={{0,2},{1,3},{2,0},{3,1},{4,6},{5,7},{6,4},{7,5},{8,10},{9,11},{10,... | collective-permute-start | bytes 1179656 | tf_op jit(solution)/shard_map/ppermute | solution.py:42
  156.6 30.0 %collective-permute-start.19 = (bf16[128,1536]{1,0:T(8,128)(2,1)}, bf16[128,1536]{1,0:T(8,128)(2,1)S(1)}, u32[]{:S(2)}, u32[]{:S(2)}) collective-permute-start(bf16[128,1536]{1,0:T(8,128)(2,1)} %get-tuple-element.54), channel_id=1, source_target_pairs={{0,4},{1,5},{2,6},{3,7},{4,0},{5,1},{6,2},{7,3},{8,12},{9,13},{10,... | collective-permute-start | bytes 1179656 | tf_op jit(solution)/shard_map/ppermute | solution.py:42
  160.8 25.8 %copy-start.23 = (bf16[256,1536]{1,0:T(8,128)(2,1)S(1)}, bf16[256,1536]{1,0:T(8,128)(2,1)}, u32[]{:S(2)}) copy-start(bf16[256,1536]{1,0:T(8,128)(2,1)} %copy-done.22) | copy-start | bytes 2359300
  160.8 25.9 %copy-start.27 = (bf16[128,1536]{1,0:T(8,128)(2,1)S(1)}, bf16[128,1536]{1,0:T(8,128)(2,1)}, u32[]{:S(2)}) copy-start(bf16[128,1536]{1,0:T(8,128)(2,1)} %slice.117) | copy-start | bytes 1179652
  162.4 24.4 %collective-permute-start.20 = (bf16[128,1536]{1,0:T(8,128)(2,1)}, bf16[128,1536]{1,0:T(8,128)(2,1)S(1)}, u32[]{:S(2)}, u32[]{:S(2)}) collective-permute-start(bf16[128,1536]{1,0:T(8,128)(2,1)} %copy-done.24), channel_id=1, source_target_pairs={{0,6},{1,7},{2,4},{3,5},{4,2},{5,3},{6,0},{7,1},{8,14},{9,15},{10,... | collective-permute-start | bytes 1179656 | tf_op jit(solution)/shard_map/ppermute | solution.py:42
  172.3 21.7 %collective-permute-start.26 = (bf16[384,1024]{1,0:T(8,128)(2,1)}, bf16[384,1024]{1,0:T(8,128)(2,1)S(1)}, u32[]{:S(2)}, u32[]{:S(2)}) collective-permute-start(bf16[384,1024]{1,0:T(8,128)(2,1)} %copy-done.21), channel_id=1, source_target_pairs={{0,16},{8,0},{16,24},{24,8},{1,17},{9,1},{17,25},{25,9},{2,18},{10... | collective-permute-start | bytes 2359304 | tf_op jit(solution)/shard_map/ppermute | solution.py:42
  186.6 3.5 %collective-permute-start.22 = (bf16[256,1536]{1,0:T(8,128)(2,1)S(1)}, bf16[256,1536]{1,0:T(8,128)(2,1)S(1)}, u32[]{:S(2)}, u32[]{:S(2)}) collective-permute-start(bf16[256,1536]{1,0:T(8,128)(2,1)S(1)} %copy-done.23), channel_id=1, source_target_pairs={{0,1},{1,0},{2,3},{3,2},{4,5},{5,4},{6,7},{7,6},{8,9},{9,8},{10,11... | collective-permute-start | bytes 2359304 | tf_op jit(solution)/shard_map/ppermute | solution.py:42
  186.8 53.2 %collective-permute-start.33 = (bf16[256,1536]{1,0:T(8,128)(2,1)S(1)}, bf16[256,1536]{1,0:T(8,128)(2,1)S(1)}, u32[]{:S(2)}, u32[]{:S(2)}) collective-permute-start(bf16[256,1536]{1,0:T(8,128)(2,1)S(1)} %pad_maximum_fusion.2), channel_id=1, source_target_pairs={{0,16},{8,0},{16,24},{24,8},{1,17},{9,1},{17,25},{25,9},{2,18},{10... | collective-permute-start | bytes 2359304 | tf_op jit(solution)/shard_map/ppermute | solution.py:42
  188.6 40.9 %collective-permute-start.21 = (bf16[256,1536]{1,0:T(8,128)(2,1)S(1)}, bf16[256,1536]{1,0:T(8,128)(2,1)S(1)}, u32[]{:S(2)}, u32[]{:S(2)}) collective-permute-start(bf16[256,1536]{1,0:T(8,128)(2,1)S(1)} %pad_maximum_fusion.1), channel_id=1, source_target_pairs={{0,1},{1,0},{2,3},{3,2},{4,5},{5,4},{6,7},{7,6},{8,9},{9,8},{10,11... | collective-permute-start | bytes 2359304 | tf_op jit(solution)/shard_map/ppermute | solution.py:42
  190.2 31.4 %copy-start.3 = (bf16[384,1024]{1,0:T(8,128)(2,1)S(1)}, bf16[384,1024]{1,0:T(8,128)(2,1)}, u32[]{:S(2)}) copy-start(bf16[384,1024]{1,0:T(8,128)(2,1)} %copy-done.2) | copy-start | bytes 2359300
  191.0 13.9 %collective-permute-start.25 = (bf16[128,1536]{1,0:T(8,128)(2,1)S(1)}, bf16[128,1536]{1,0:T(8,128)(2,1)S(1)}, u32[]{:S(2)}, u32[]{:S(2)}) collective-permute-start(bf16[128,1536]{1,0:T(8,128)(2,1)S(1)} %pad_maximum_fusion.9), channel_id=1, source_target_pairs={{0,6},{1,7},{2,4},{3,5},{4,2},{5,3},{6,0},{7,1},{8,14},{9,15},{10,... | collective-permute-start | bytes 1179656 | tf_op jit(solution)/shard_map/ppermute | solution.py:42
  193.7 48.1 %collective-permute-start.35 = (bf16[256,1536]{1,0:T(8,128)(2,1)S(1)}, bf16[256,1536]{1,0:T(8,128)(2,1)S(1)}, u32[]{:S(2)}, u32[]{:S(2)}) collective-permute-start(bf16[256,1536]{1,0:T(8,128)(2,1)S(1)} %pad_maximum_fusion.3), channel_id=1, source_target_pairs={{0,8},{8,24},{16,0},{24,16},{1,9},{9,25},{17,1},{25,17},{2,10},{10... | collective-permute-start | bytes 2359304 | tf_op jit(solution)/shard_map/ppermute | solution.py:42
  193.9 35.6 %collective-permute-start.24 = (bf16[128,1536]{1,0:T(8,128)(2,1)S(1)}, bf16[128,1536]{1,0:T(8,128)(2,1)S(1)}, u32[]{:S(2)}, u32[]{:S(2)}) collective-permute-start(bf16[128,1536]{1,0:T(8,128)(2,1)S(1)} %pad_maximum_fusion.8), channel_id=1, source_target_pairs={{0,4},{1,5},{2,6},{3,7},{4,0},{5,1},{6,2},{7,3},{8,12},{9,13},{10,... | collective-permute-start | bytes 1179656 | tf_op jit(solution)/shard_map/ppermute | solution.py:42
  199.8 29.7 %copy-start.16 = (bf16[384,1024]{1,0:T(8,128)(2,1)S(1)}, bf16[384,1024]{1,0:T(8,128)(2,1)}, u32[]{:S(2)}) copy-start(bf16[384,1024]{1,0:T(8,128)(2,1)} %copy-done.15) | copy-start | bytes 2359300
  204.9 33.0 %collective-permute-start.23 = (bf16[128,1536]{1,0:T(8,128)(2,1)S(1)}, bf16[128,1536]{1,0:T(8,128)(2,1)S(1)}, u32[]{:S(2)}, u32[]{:S(2)}) collective-permute-start(bf16[128,1536]{1,0:T(8,128)(2,1)S(1)} %pad_maximum_fusion.7), channel_id=1, source_target_pairs={{0,2},{1,3},{2,0},{3,1},{4,6},{5,7},{6,4},{7,5},{8,10},{9,11},{10,... | collective-permute-start | bytes 1179656 | tf_op jit(solution)/shard_map/ppermute | solution.py:42
  229.5 20.4 %collective-permute-start.29 = (bf16[384,1024]{1,0:T(8,128)(2,1)S(1)}, bf16[384,1024]{1,0:T(8,128)(2,1)S(1)}, u32[]{:S(2)}, u32[]{:S(2)}) collective-permute-start(bf16[384,1024]{1,0:T(8,128)(2,1)S(1)} %copy-done.16), channel_id=1, source_target_pairs={{0,16},{8,0},{16,24},{24,8},{1,17},{9,1},{17,25},{25,9},{2,18},{10... | collective-permute-start | bytes 2359304 | tf_op jit(solution)/shard_map/ppermute | solution.py:42
  229.6 20.4 %collective-permute-start.31 = (bf16[384,1024]{1,0:T(8,128)(2,1)S(1)}, bf16[384,1024]{1,0:T(8,128)(2,1)S(1)}, u32[]{:S(2)}, u32[]{:S(2)}) collective-permute-start(bf16[384,1024]{1,0:T(8,128)(2,1)S(1)} %add_convert_fusion), channel_id=1, source_target_pairs={{0,8},{8,24},{16,0},{24,16},{1,9},{9,25},{17,1},{25,17},{2,10},{10... | collective-permute-start | bytes 2359304 | tf_op jit(solution)/shard_map/ppermute | solution.py:42
  237.8 28.0 %collective-permute-start.28 = (bf16[384,1024]{1,0:T(8,128)(2,1)S(1)}, bf16[384,1024]{1,0:T(8,128)(2,1)S(1)}, u32[]{:S(2)}, u32[]{:S(2)}) collective-permute-start(bf16[384,1024]{1,0:T(8,128)(2,1)S(1)} %copy-done.14), channel_id=1, source_target_pairs={{0,8},{8,24},{16,0},{24,16},{1,9},{9,25},{17,1},{25,17},{2,10},{10... | collective-permute-start | bytes 2359304 | tf_op jit(solution)/shard_map/ppermute | solution.py:42
  240.0 25.9 %collective-permute-start.27 = (bf16[384,1024]{1,0:T(8,128)(2,1)S(1)}, bf16[384,1024]{1,0:T(8,128)(2,1)S(1)}, u32[]{:S(2)}, u32[]{:S(2)}) collective-permute-start(bf16[384,1024]{1,0:T(8,128)(2,1)S(1)} %add_convert_fusion.1), channel_id=1, source_target_pairs={{0,16},{8,0},{16,24},{24,8},{1,17},{9,1},{17,25},{25,9},{2,18},{10... | collective-permute-start | bytes 2359304 | tf_op jit(solution)/shard_map/ppermute | solution.py:42
  (30 other events, 279.2 us)
where the time goes:
time: 268 us; the launch traced here: 267 us
  waiting for transfers between devices  126 us (47%)
  starting transfers between devices  74.3 us (28%)
  Pallas kernels  39.6 us (15%)
  local copies, waits for them, and re-layouts  14.3 us (5%)
  other arithmetic  12.1 us (5%)
    ppermute x41, waiting for transfers between devices, hop(): return lax.ppermute(x, axis, [(i, target(i)) for i in range(size)])  126 us
    ppermute x41, starting transfers between devices, hop(): return lax.ppermute(x, axis, [(i, target(i)) for i in range(size)])  74.3 us
    pallas_call x10, Pallas kernels, call(): pl.pallas_call(kernel, out_shape=list(outs), in_specs=[SMEM] * scalars +...  39.6 us
  transfers between devices with their start and end apart: 41, of which 17 were waited for; matrix products, arithmetic and copies ran while one was open for 7% of the time, Pallas kernels for 13%

commit v1 on v0

v1 whole, which is shorter than its diff:
```python
import functools

import jax
import jax.numpy as jnp
from jax import lax
from jax.experimental import pallas as pl
from jax.experimental.pallas import tpu as pltpu
from jax.sharding import PartitionSpec as P

F32 = jnp.float32
KF, HP, HF, HS = 0, 0, 3e-05, 12e-6
BF16 = jnp.bfloat16
VMEM = pl.BlockSpec(memory_space=pltpu.VMEM)
SMEM = pl.BlockSpec(memory_space=pltpu.SMEM)


def dot(a, b, dims=((1,), (0,))):
    return lax.dot_general(a, b, (dims, ((), ())), preferred_element_type=F32)


def call(kernel, outs, args, flops, scalars=0, scratch=(), hint=0):
    sizes = [a.size * a.dtype.itemsize for a in args] + [
        o.size * o.dtype.itemsize for o in outs
    ]
    return pl.pallas_call(
        kernel,
        out_shape=list(outs),
        in_specs=[SMEM] * scalars + [VMEM] * (len(args) - scalars),
        out_specs=[VMEM] * len(outs),
        scratch_shapes=list(scratch),
        compiler_params=pltpu.CompilerParams(vmem_limit_bytes=24 << 20),
        cost_estimate=pl.CostEstimate(
            flops=int(KF * flops + hint * 1e15) + 1,
            bytes_accessed=int(KF * sum(sizes)) + 1, transcendentals=0
        ),
    )(*args)


def shape(dims, dtype):
    return jax.ShapeDtypeStruct(tuple(dims), dtype)


def after(x, *others):
    return lax.optimization_barrier((x, *others))[0]


def hop(x, axis, size, target):
    return lax.ppermute(x, axis, [(i, target(i)) for i in range(size)])


def ring_order(n):
    return [i for i in range(0, n, 2)] + [i for i in range(n - 1, 0, -2)]


def ring_hop(x, n, step):
    order = ring_order(n)
    place = {d: q for q, d in enumerate(order)}
    return hop(x, "dp", n, lambda i: order[(place[i] + step) % n])


def hits(rows_ref, start, count, tok_rows, dtype=BF16):
    line = rows_ref[:, start : start + count]
    grid = lax.broadcasted_iota(jnp.int32, (tok_rows, count), 0)
    return (grid == line).astype(F32).astype(dtype)


def pick_kernel(rows_ref, src_ref, out_ref):
    tile = 128
    for start in range(0, out_ref.shape[0], tile):
        one = hits(rows_ref, start, tile, src_ref.shape[0])
        out_ref[start : start + tile, :] = dot(one, src_ref[...], ((0,), (0,))).astype(BF16)


def front_kernel(n, ids, x, wr, *refs):
    gates = refs[:n]
    ups = refs[n : 2 * n]
    xt, hd, hdt, sa, ua, gcol, xc = refs[2 * n :]
    width = x.shape[1] // n
    for d in range(n):
        xc[d] = x[:, d * width : (d + 1) * width]
    logits = dot(x[...], wr[...])
    lanes = lax.broadcasted_iota(jnp.int32, logits.shape, 1)
    mine = jnp.sum(jnp.where(lanes == ids[n], logits, 0.0), axis=1, keepdims=True)
    gcol[...] = jax.nn.sigmoid(mine)
    tile = 256
    hidden = hd.shape[1]

    def step(t, carry):
        cols = pl.ds(pl.multiple_of(t * tile, tile), tile)
        a = dot(xc[ids[0]], gates[0][:, cols])
        b = dot(xc[ids[0]], ups[0][:, cols])
        for s in range(1, n):
            a = a + dot(xc[ids[s]], gates[s][:, cols])
            b = b + dot(xc[ids[s]], ups[s][:, cols])
        sig = jax.nn.sigmoid(a)
        silu = a * sig
        h = (silu * b).astype(BF16)
        hd[:, cols] = h
        hdt[cols, :] = h.T
        sa[:, cols] = silu
        ua[:, cols] = b * sig * (1.0 + a * (1.0 - sig))
        return carry

    lax.fori_loop(0, hidden // tile, step, 0)
    for d in range(n):
        xt[d] = xc[d].T


def chunk_of(ids, s, width):
    return pl.ds(pl.multiple_of(ids[s] * width, width), width)


def down_far_kernel(n, ids, c, gcol, hdt, g, low, high):
    g[...] = (gcol[...] * c[...].astype(F32)).astype(BF16)
    width = hdt.shape[0] // n
    far = dot(hdt[chunk_of(ids, n // 2, width), :], g[...]).astype(BF16)
    low[...] = far[: width // 2]
    high[...] = far[width // 2 :]


def down_kernel(n, ids, g, hdt, *outs):
    width = hdt.shape[0] // n
    for out, s in zip(outs, [s for s in range(n) if s != n // 2]):
        out[...] = dot(hdt[chunk_of(ids, s, width), :], g[...]).astype(BF16)


def out_kernel(n, ids, hd, gcol, *refs):
    downs = refs[: n + 1]
    go, o_ref = refs[n + 1 :]
    width = hd.shape[1] // n
    half = n // 2

    def term(s):
        cols = pl.ds(pl.multiple_of(ids[s] * width, 128), width)
        if s == half:
            w = jnp.concatenate([downs[half][...], downs[n][...]], axis=0)
        else:
            w = downs[s][...]
        return dot(hd[:, cols], w)

    o = term(0)
    for s in range(1, n):
        o = o + term(s)
    o = o.astype(BF16)
    o_ref[...] = o
    go[...] = (gcol[...] * o.astype(F32)).astype(BF16)


def hidden_kernel(n, ids, g, sa, ua, *refs):
    downs = refs[: n + 1]
    da, db = refs[n + 1 :]
    width = sa.shape[1] // n
    half = n // 2
    for s in range(n):
        cols = pl.ds(pl.multiple_of(ids[s] * width, 128), width)
        if s == half:
            w = jnp.concatenate([downs[half][...], downs[n][...]], axis=0)
        else:
            w = downs[s][...]
        dh = dot(g[...], w, ((1,), (1,)))
        da[:, cols] = (dh * ua[:, cols]).astype(BF16)
        db[:, cols] = (dh * sa[:, cols]).astype(BF16)


def router_kernel(c, o, gcol, x, dl, router):
    gate = gcol[...]
    dgate = jnp.sum(c[...].astype(F32) * o[...].astype(F32), axis=1, keepdims=True)
    dlogit = (dgate * gate * (1.0 - gate)).astype(BF16)
    dl[...] = dlogit.astype(F32)
    router[...] = dot(dlogit, x[...], ((0,), (0,)))


def weight_kernel(order, ids, xt, da, db, *outs):
    tile = 256
    for place, s in enumerate(order):
        gate, up = outs[2 * place], outs[2 * place + 1]

        def step(t, carry, s=s, gate=gate, up=up):
            cols = pl.ds(pl.multiple_of(t * tile, tile), tile)
            gate[:, cols] = dot(xt[ids[s]], da[:, cols]).astype(BF16)
            up[:, cols] = dot(xt[ids[s]], db[:, cols]).astype(BF16)
            return carry

        lax.fori_loop(0, da.shape[1] // tile, step, 0)


def rows_kernel(n, ids, da, db, dl, wr, *refs):
    gates = refs[:n]
    ups = refs[n : 2 * n]
    out, scr = refs[2 * n :]
    for s in range(n):
        scr[ids[s]] = dot(da[...], gates[s][...], ((1,), (1,))) + dot(
            db[...], ups[s][...], ((1,), (1,))
        )
    chunk = scr.shape[2]
    for d in range(n):
        cols = slice(d * chunk, (d + 1) * chunk)
        out[:, cols] = (scr[d] + dl[...] * wr[:, cols].astype(F32)).astype(BF16)


def sum_far_kernel(low, high, nxt, prv, fwd, bwd):
    cut = low.shape[0]
    fwd[:cut, :] = (nxt[:cut, :].astype(F32) + low[...].astype(F32)).astype(BF16)
    fwd[cut:, :] = nxt[cut:, :]
    bwd[:cut, :] = prv[:cut, :]
    bwd[cut:, :] = (prv[cut:, :].astype(F32) + high[...].astype(F32)).astype(BF16)


def sum_pair_kernel(a, b, c, d, first, second):
    first[...] = (a[...].astype(F32) + b[...].astype(F32)).astype(BF16)
    second[...] = (c[...].astype(F32) + d[...].astype(F32)).astype(BF16)


def scatter_kernel(rows_ref, src_ref, out_ref):
    one = hits(rows_ref, 0, src_ref.shape[0], out_ref.shape[0])
    out_ref[...] = dot(one, src_ref[...]).astype(BF16)


def body(n, experts, tokens, cotangent, chosen, w_router, w_gate, w_up, w_down):
    tok_rows, model = tokens.shape
    blocks, _, picks = chosen.shape
    block_rows = tok_rows // blocks
    part = blocks * picks
    slots = experts * part
    half = n // 2
    gate_w, up_w, down_w = w_gate[0], w_up[0], w_down[0]
    hidden = gate_w.shape[1]

    d_me = lax.axis_index("dp")
    e_me = lax.axis_index("expert")
    place = jnp.where(d_me % 2 == 0, d_me // 2, n - 1 - d_me // 2)
    order = jnp.asarray(ring_order(n), jnp.int32)
    ids = jnp.concatenate(
        [order[(place + jnp.arange(n, dtype=jnp.int32)) % n], e_me[None].astype(jnp.int32)]
    )

    gate_p, up_n = ring_hop(gate_w, n, 1), ring_hop(up_w, n, -1)
    up_p, gate_n = ring_hop(up_w, n, 1), ring_hop(gate_w, n, -1)

    offsets = (jnp.arange(blocks, dtype=jnp.int32) * block_rows)[:, None, None]
    rows = jnp.transpose(chosen + offsets, (1, 0, 2)).reshape(1, slots)

    def exchange(x):
        return lax.all_to_all(
            x.reshape(experts, part, model), "expert", split_axis=0, concat_axis=0, tiled=True
        ).reshape(slots, model)

    pick_flops = 2 * slots * tok_rows * model

    def pick(source, hint=0):
        return call(
            pick_kernel, [shape((slots, model), BF16)], [rows, source], pick_flops, hint=hint
        )[0]

    x_all = exchange(pick(tokens))
    c_rows = pick(after(cotangent, gate_p, up_n), hint=HP)
    c_all = exchange(c_rows)

    gates, ups = {0: gate_w, n - 1: gate_p, 1: gate_n}, {0: up_w, n - 1: up_p, 1: up_n}
    for s in range(2, half):
        gates[n - s] = ring_hop(gates[n - s + 1], n, 1)
        ups[s] = ring_hop(ups[s - 1], n, -1)
        ups[n - s] = ring_hop(ups[n - s + 1], n, 1)
        gates[s] = ring_hop(gates[s - 1], n, -1)
    if n > 2:
        gates[half] = ring_hop(gates[half + 1], n, 1)
        ups[half] = ring_hop(ups[half - 1], n, -1)
    downs = {0: down_w}
    for s in range(1, half):
        down_f, down_b = downs[(n - s + 1) % n], downs[s - 1]
        if s == 1:
            down_f, down_b = after(down_w, up_p, c_rows, x_all), after(down_w, gate_n, c_rows, x_all)
        downs[n - s] = ring_hop(down_f, n, 1)
        downs[s] = ring_hop(down_b, n, -1)
    gate_list = [gates[s] for s in range(n)]
    up_list = [ups[s] for s in range(n)]
    matmul = 2 * slots * model * hidden
    xt, hd, hdt, sa, ua, gcol = call(
        functools.partial(front_kernel, n),
        [
            shape((n, model // n, slots), BF16),
            shape((slots, hidden), BF16),
            shape((hidden, slots), BF16),
            shape((slots, hidden), F32),
            shape((slots, hidden), F32),
            shape((slots, 1), F32),
        ],
        [ids, x_all, w_router, *gate_list, *up_list],
        2 * matmul,
        scalars=1,
        scratch=[pltpu.VMEM((n, slots, model // n), BF16)],
        hint=HF,
    )
    cut = down_w.shape[0] // 2
    far_a = ring_hop(after(downs[(half + 1) % n], hd)[:cut], n, 1)
    far_b = ring_hop(after(downs[half - 1], hd)[cut:], n, -1)
    down_list = [far_a if s == half else downs[s] for s in range(n)] + [far_b]
    width = hidden // n
    go, o_all = call(
        functools.partial(out_kernel, n),
        [shape((slots, model), BF16)] * 2,
        [ids, hd, gcol, *down_list],
        matmul,
        scalars=1,
    )
    o_rows = exchange(go)
    g_all, low, high = call(
        functools.partial(down_far_kernel, n),
        [shape((slots, model), BF16)] + [shape((width // 2, model), BF16)] * 2,
        [ids, c_all, after(gcol, go), hdt],
        matmul / n,
        scalars=1,
    )
    down_rest = call(
        functools.partial(down_kernel, n),
        [shape((width, model), BF16)] * (n - 1),
        [ids, g_all, hdt],
        matmul * (n - 1) / n,
        scalars=1,
    )
    down_of = dict(zip([s for s in range(n) if s != half], down_rest))
    low, high = ring_hop(low, n, 1), ring_hop(high, n, -1)

    def plus(a, b):
        return (a.astype(F32) + b.astype(F32)).astype(BF16)

    da, db = call(
        functools.partial(hidden_kernel, n),
        [shape((slots, hidden), BF16)] * 2,
        [ids, after(g_all, *down_rest), sa, ua, *down_list],
        matmul,
        scalars=1,
    )
    low, high = after(low, da), after(high, da)
    fwd, bwd = call(
        sum_far_kernel,
        [shape((width, model), BF16)] * 2,
        [low, high, down_of[half - 1], down_of[(half + 1) % n]],
        0,
    )
    for s in range(half - 1, 0, -1):
        fwd = ring_hop(fwd, n, 1)
        bwd = ring_hop(bwd, n, -1)
        if s > 1:
            fwd, bwd = plus(down_of[s - 1], fwd), plus(down_of[n - s + 1], bwd)
    down_grad = down_of[0].astype(F32) + fwd.astype(F32) + bwd.astype(F32)

    gate_of, up_of = {}, {}

    def weights(order_of, da):
        grads = call(
            functools.partial(weight_kernel, order_of),
            [shape((model // n, hidden), BF16)] * (2 * len(order_of)),
            [ids, xt, da, db],
            2 * matmul * len(order_of) / n,
            scalars=1,
        )
        for i, s in enumerate(order_of):
            gate_of[s], up_of[s] = grads[2 * i], grads[2 * i + 1]

    weights([half], da)
    far_w = list(gate_of.values())
    dl, router_row = call(
        router_kernel,
        [shape((slots, 1), F32), shape((1, model), F32)],
        [c_all, after(o_all, *far_w), gcol, x_all],
        0,
    )

    total = router_row
    bit = 1
    while bit < n:
        total = total + hop(total, "dp", n, lambda i, b=bit: i ^ b)
        bit *= 2
    bit = 1
    while bit < experts:
        total = jnp.concatenate(
            [total, hop(total, "expert", experts, lambda i, b=bit: i ^ b)], axis=0
        )
        bit *= 2
    grad_router = jnp.take(total, e_me ^ jnp.arange(experts, dtype=jnp.int32), axis=0).T

    def scatter(source):
        return call(
            scatter_kernel, [shape((tok_rows, model), BF16)], [rows, source], pick_flops
        )[0]

    mixed = scatter(o_rows)
    wr_row = lax.dynamic_slice_in_dim(w_router.T, e_me, 1, axis=0)
    d_rows = call(
        functools.partial(rows_kernel, n),
        [shape((slots, model), BF16)],
        [ids, after(da, *gate_of.values()), db, dl, wr_row, *gate_list, *up_list],
        2 * matmul,
        scalars=1,
        scratch=[pltpu.VMEM((n, slots, model // n), F32)],
    )[0]
    r_rows = exchange(after(d_rows, fwd, bwd))
    weights([s for s in range(n) if s != half], after(da, d_rows))

    far_g = ring_hop(after(gate_of[half], low), n, 1)
    far_u = ring_hop(after(up_of[half], high), n, -1)
    fwd_u, bwd_g = after(up_of[half - 1], fwd), after(gate_of[(half + 1) % n], bwd)
    far_g, far_u = after(far_g, mixed, down_grad), after(far_u, mixed, down_grad)
    fwd_g, bwd_u = call(
        sum_pair_kernel,
        [shape((model // n, hidden), BF16)] * 2,
        [gate_of[half - 1], far_g, up_of[(half + 1) % n], far_u],
        0,
        hint=HS,
    )
    for s in range(half - 1, 0, -1):
        fwd_u, fwd_g = ring_hop(fwd_u, n, 1), ring_hop(fwd_g, n, 1)
        bwd_g, bwd_u = ring_hop(bwd_g, n, -1), ring_hop(bwd_u, n, -1)
        if s > 1:
            fwd_u, fwd_g = plus(up_of[s - 1], fwd_u), plus(gate_of[s - 1], fwd_g)
            bwd_g, bwd_u = plus(gate_of[n - s + 1], bwd_g), plus(up_of[n - s + 1], bwd_u)
    fwd, bwd = (fwd_g, fwd_u), (bwd_g, bwd_u)
    grad_gate = gate_of[0].astype(F32) + fwd[0].astype(F32) + bwd[0].astype(F32)
    grad_up = up_of[0].astype(F32) + fwd[1].astype(F32) + bwd[1].astype(F32)

    grad_tokens = scatter(after(r_rows, total))
    return (
        mixed,
        grad_tokens,
        grad_gate[None],
        grad_up[None],
        down_grad[None],
        grad_router,
    )


def solution(mesh):
    sizes = dict(mesh.shape)
    return jax.shard_map(
        functools.partial(body, sizes["dp"], sizes["expert"]),
        mesh=mesh,
        in_specs=(
            P(("dp", "expert"), None),
            P(("dp", "expert"), None),
            P(("dp", "expert"), None, None),
            P(),
            P("expert", "dp", None),
            P("expert", "dp", None),
            P("expert", "dp", None),
        ),
        out_specs=(
            P(("dp", "expert"), None),
            P(("dp", "expert"), None),
            P("expert", "dp", None),
            P("expert", "dp", None),
            P("expert", "dp", None),
            P(),
        ),
        check_vma=False,
    )
```

time: 268 us -> 218 us (0.81)
  waiting for transfers between devices: 126 us -> 86.6 us
  starting transfers between devices: 74.3 us -> 44.3 us
  local copies, waits for them, and re-layouts: 14.3 us -> 27.1 us
  Pallas kernels: 39.6 us -> 47.5 us
    ppermute x41 -> x25, waiting for transfers between devices: 126 us -> 74.9 us  [hop(): return lax.ppermute(x, axis, [(i, target(i)) for i in range(size)])]
    ppermute x41 -> x25, starting transfers between devices: 74.3 us -> 26.1 us  [hop(): return lax.ppermute(x, axis, [(i, target(i)) for i in range(size)])]
    unnamed x75 -> x99, local copies, waits for them, and re-layouts: 4.29 us -> 25.7 us
    all_to_all x0 -> x4, starting transfers between devices: none -> 18.2 us  [exchange(): lax.all_to_all(x.reshape(experts, part, model), 'expert', split_axis=0, c...]
    all_to_all x0 -> x4, waiting for transfers between devices: none -> 11.7 us  [exchange(): lax.all_to_all(x.reshape(experts, part, model), 'expert', split_axis=0, c...]
    pallas_call x10 -> x15, Pallas kernels: 39.6 us -> 47.5 us  [call(): pl.pallas_call(kernel, out_shape=list(outs), in_specs=[SMEM] * scalars +...]
    slice x16 -> x2, local copies, waits for them, and re-layouts: 5.47 us -> 0.05 us  [the longest x1 0.03 us: body(): far_a = ring_hop(after(downs[(half + 1) % n], hd)[:cut], n, 1)]
    convert_element_type x4 -> x0, other arithmetic: 3.91 us -> none  [plus(): return (a.astype(F32) + b.astype(F32)).astype(BF16)]
  transfers between devices with their start and end apart: 41 -> 29, of which waited for: 17 -> 13; matrix products, arithmetic and copies ran while one was open for 7% -> 5% of each run, Pallas kernels for 13% -> 20%
where the time goes in v1:
time: 218 us; the launch traced here: 217 us
  waiting for transfers between devices  86.6 us (40%)
  Pallas kernels  47.5 us (22%)
  starting transfers between devices  44.3 us (20%)
  local copies, waits for them, and re-layouts  27.1 us (12%)
  other arithmetic  10.3 us (5%)
    ppermute x25, waiting for transfers between devices, hop(): return lax.ppermute(x, axis, [(i, target(i)) for i in range(size)])  74.9 us
    pallas_call x15, Pallas kernels, call(): pl.pallas_call(kernel, out_shape=list(outs), in_specs=[SMEM] * scalars +...  47.5 us
    ppermute x25, starting transfers between devices, hop(): return lax.ppermute(x, axis, [(i, target(i)) for i in range(size)])  26.1 us
    unnamed x99, local copies, waits for them, and re-layouts  25.7 us
    all_to_all x4, starting transfers between devices, exchange(): lax.all_to_all(x.reshape(experts, part, model), 'expert', split_axis=0, c...  18.2 us
    all_to_all x4, waiting for transfers between devices, exchange(): lax.all_to_all(x.reshape(experts, part, model), 'expert', split_axis=0, c...  11.7 us
  transfers between devices with their start and end apart: 29, of which 13 were waited for; matrix products, arithmetic and copies ran while one was open for 5% of the time, Pallas kernels for 20%

profile of v1, /device:TPU:0, one launch (start us, length us, event | category | flops | bytes accessed | tf_op | source)
XLA Modules:
  0.0 216.9 jit_solution(18016782393963129279)
XLA Ops:
  2.7 1.8 shard_map.127
  4.4 6.4 %all-to-all-start = ((bf16[8,64,1536]{2,1,0:T(8,128)(2,1)}), bf16[8,64,1536]{2,1,0:T(8,128)(2,1)S(1)}, u32[]{:S(2)}, u32[]{:S(2)}) async-start(bf16[8,64,1536]{2,1,0:T(8,128)(2,1)} %bitcast.3), calls=%async_computation | async-start | bytes 3145728 | tf_op jit(solution)/shard_map/all_to_all | solution.py:244
  10.9 1.5 collective-permute-start.1
  12.9 1.5 collective-permute-start
  14.9 16.6 %collective-permute-done.1.refs_3_ = bf16[384,1024]{1,0:T(8,128)(2,1)} collective-permute-done((bf16[384,1024]{1,0:T(8,128)(2,1)}, bf16[384,1024]{1,0:T(8,128)(2,1)}, u32[]{:S(2)}, u32[]{:S(2)}) %collective-permute-start.1) | collective-permute-done | bytes 786464 | tf_op jit(solution)/shard_map/ppermute | solution.py:48
  31.5 1.5 collective-permute-start.2
  37.0 11.7 %all-to-all-done = bf16[8,64,1536]{2,1,0:T(8,128)(2,1)S(1)} async-done(((bf16[8,64,1536]{2,1,0:T(8,128)(2,1)}), bf16[8,64,1536]{2,1,0:T(8,128)(2,1)S(1)}, u32[]{:S(2)}, u32[]{:S(2)}) %all-to-all-start) | async-done | bytes 1572896 | tf_op jit(solution)/shard_map/all_to_all | solution.py:244
  48.7 3.6 %all-to-all-start.2 = ((bf16[8,64,1536]{2,1,0:T(8,128)(2,1)}), bf16[8,64,1536]{2,1,0:T(8,128)(2,1)S(1)}, u32[]{:S(2)}, u32[]{:S(2)}) async-start(bf16[8,64,1536]{2,1,0:T(8,128)(2,1)} %bitcast.32), calls=%async_computation.2 | async-start | bytes 3145728 | tf_op jit(solution)/shard_map/all_to_all | solution.py:244
  52.3 1.6 collective-permute-start.6
  54.4 10.8 %collective-permute-done.2.refs_2_ = bf16[384,1024]{1,0:T(8,128)(2,1)} collective-permute-done((bf16[384,1024]{1,0:T(8,128)(2,1)}, bf16[384,1024]{1,0:T(8,128)(2,1)}, u32[]{:S(2)}, u32[]{:S(2)}) %collective-permute-start.2) | collective-permute-done | bytes 786464 | tf_op jit(solution)/shard_map/ppermute | solution.py:48
  65.2 1.6 collective-permute-done.4.refs_6_
  67.8 9.5 %shard_map.128 = (bf16[4,384,512]{2,1,0:T(8,128)(2,1)S(1)}, bf16[512,1024]{1,0:T(8,128)(2,1)S(1)}, bf16[1024,512]{1,0:T(8,128)(2,1)S(1)}, f32[512,1024]{1,0:T(8,...) custom-call(s32[5]{0:T(128)S(1)} %pad_add_fusion.ids, bf16[512,1536]{1,0:T(8,128)(2,1)S(1)} %bitcast.29, ...), custom_call_target="tpu_custom_call" | custom-call | flops 30000001024 | bytes 1 | tf_op jit(solution)/shard_map/pallas_call | solution.py:25
  77.4 1.2 copy-done.5
  79.6 1.4 copy-done.17
  80.9 1.3 copy-done.19
  82.3 1.5 collective-permute-start.8
  84.5 8.0 %collective-permute-done.8.refs_2_ = bf16[128,1536]{1,0:T(8,128)(2,1)S(1)} collective-permute-done((bf16[128,1536]{1,0:T(8,128)(2,1)S(1)}, bf16[128,1536]{1,0:T(8,128)(2,1)S(1)}, u32[]{:S(2)}, u32[]{:S(2)}) %collective-permute-start.8) | collective-permute-done | bytes 393248 | tf_op jit(solution)/shard_map/ppermute | solution.py:48
  92.4 1.3 collective-permute-done.9.refs_4_
  93.8 2.4 %shard_map.130 = (bf16[512,1536]{1,0:T(8,128)(2,1)S(1)}, bf16[512,1536]{1,0:T(8,128)(2,1)S(1)}) custom-call(s32[5]{0:T(128)S(1)} %pad_add_fusion.ids, bf16[512,1024]{1,0:T(8,128)(2,1)S(1)} %get-tuple-element.56.hd, f32[512,1]{1,0:T(8,128)S(1)} %get-tuple-element.64.gcol, bf16[256,1536]{1,0:T(8,128)(2,1)S(1)} %bitcast.36, ...), custom_call_target="tpu_custom_call" | custom-call | flops 1 | bytes 1 | tf_op jit(solution)/shard_map/pallas_call | solution.py:25
  100.0 4.5 %all-to-all-start.1 = ((bf16[8,64,1536]{2,1,0:T(8,128)(2,1)}), bf16[8,64,1536]{2,1,0:T(8,128)(2,1)}, u32[]{:S(2)}, u32[]{:S(2)}) async-start(bf16[8,64,1536]{2,1,0:T(8,128)(2,1)} %bitcast.38), calls=%async_computation.1 | async-start | bytes 3145728 | tf_op jit(solution)/shard_map/all_to_all | solution.py:244
  104.5 2.1 shard_map.132
  106.6 1.5 collective-permute-start.10
  108.7 1.9 shard_map.133
  113.3 1.6 copy-done.20
  114.9 2.6 %shard_map.134 = (bf16[512,1024]{1,0:T(8,128)(2,1)S(1)}, bf16[512,1024]{1,0:T(8,128)(2,1)S(1)}) custom-call(s32[5]{0:T(128)S(1)} %pad_add_fusion.ids, bf16[512,1536]{1,0:T(8,128)(2,1)S(1)} %get-tuple-element.70.g, f32[512,1024]{1,0:T(8,128)S(1)} %copy-done.18, f32[512,1024]{1,0:T(8,128)S(1)} %copy-done.20, bf16[256,1536]{1,0:T(8,128)(2,1)S(1)} %bitcast.37, ...), custom_call_target="tpu_custom_call" | custom-call | flops 1 | bytes 1 | tf_op jit(solution)/shard_map/pallas_call | solution.py:25
  117.5 3.2 %shard_map.135 = (bf16[384,1024]{1,0:T(8,128)(2,1)}, bf16[384,1024]{1,0:T(8,128)(2,1)}) custom-call(s32[5]{0:T(128)S(1)} %pad_add_fusion.ids, bf16[4,384,512]{2,1,0:T(8,128)(2,1)S(1)} %copy-done.6, bf16[512,1024]{1,0:T(8,128)(2,1)S(1)} %get-tuple-element.90.da, bf16[512,1024]{1,0:T(8,128)(2,1)S(1)} %get-tuple-element.75.db), custom_call_target="tpu_custom_call" | custom-call | flops 1 | bytes 1 | tf_op jit(solution)/shard_map/pallas_call | solution.py:25
  122.7 3.1 %collective-permute-done.14 = f32[1,1536]{1,0:T(1,128)S(1)} collective-permute-done((f32[1,1536]{1,0:T(1,128)S(1)}, f32[1,1536]{1,0:T(1,128)S(1)}, u32[]{:S(2)}, u32[]{:S(2)}) %collective-permute-start.14) | collective-permute-done | bytes 6176 | tf_op jit(solution)/shard_map/ppermute | solution.py:48
  125.9 1.5 collective-permute-start.15
  129.7 1.4 shard_map.138
  131.7 1.5 collective-permute-start.13
  134.4 2.1 collective-permute-start.17
  136.5 7.9 %shard_map.137 = bf16[512,1536]{1,0:T(8,128)(2,1)S(1)} custom-call(s32[5]{0:T(128)S(1)} %pad_add_fusion.ids, bf16[512,1024]{1,0:T(8,128)(2,1)S(1)} %get-tuple-element.90.da, bf16[512,1024]{1,0:T(8,128)(2,1)S(1)} %copy-done.1, f32[512,1]{1,0:T(8,128)S(1)} %copy-done.40, bf16[1,1536]{1,0:T(2,128)(2,1)S(1)} %dynamic-slice_bitcast_fusion.wr, ...), custom_call_target="tpu_custom_call" | custom-call | flops 1 | bytes 1 | tf_op jit(solution)/shard_map/pallas_call | solution.py:25
  145.6 6.1 %shard_map.140 = (bf16[384,1024]{1,0:T(8,128)(2,1)S(1)}, bf16[384,1024]{1,0:T(8,128)(2,1)S(1)}, bf16[384,1024]{1,0:T(8,128)(2,1)S(1)}, bf16[384,1024]{1,0:T(8,12...) custom-call(s32[5]{0:T(128)S(1)} %pad_add_fusion.ids, bf16[4,384,512]{2,1,0:T(8,128)(2,1)S(1)} %copy-done.7, ...), custom_call_target="tpu_custom_call" | custom-call | flops 1 | bytes 1 | tf_op jit(solution)/shard_map/pallas_call | solution.py:25
  154.9 1.5 collective-permute-start.20
  156.4 2.4 %collective-permute-start.18 = (f32[4,1536]{1,0:T(4,128)S(1)}, f32[4,1536]{1,0:T(4,128)S(1)}, u32[]{:S(2)}, u32[]{:S(2)}) collective-permute-start(f32[4,1536]{1,0:T(4,128)S(1)} %pad_maximum_fusion.1), channel_id=1, source_target_pairs={{0,4},{1,5},{2,6},{3,7},{4,0},{5,1},{6,2},{7,3},{8,12},{9,13},{10,... | collective-permute-start | bytes 73736 | tf_op jit(solution)/shard_map/ppermute | solution.py:48
  161.2 3.7 %all-to-all-start.3 = ((bf16[8,64,1536]{2,1,0:T(8,128)(2,1)}), bf16[8,64,1536]{2,1,0:T(8,128)(2,1)S(1)}, u32[]{:S(2)}, u32[]{:S(2)}) async-start(bf16[8,64,1536]{2,1,0:T(8,128)(2,1)} %bitcast.33), calls=%async_computation.3 | async-start | bytes 3145728 | tf_op jit(solution)/shard_map/all_to_all | solution.py:244
  164.9 2.8 %convert_add_fusion = f32[256,1536]{1,0:T(8,128)} fusion(bf16[256,1536]{1,0:T(8,128)(2,1)} %copy-done.47, bf16[256,1536]{1,0:T(8,128)(2,1)} %copy-done.46, bf16[256,1536]{1,0:T(8,128)(2,1)S(1)} %copy-done.35), kind=kLoop, calls=%fused_computation.4 | loop fusion | flops 1966080 | bytes 3932160 | tf_op jit(solution)/shard_map/add | solution.py:346
  167.7 3.0 %shard_map.131 = bf16[256,1536]{1,0:T(8,128)(2,1)} custom-call(s32[1,512]{1,0:T(1,128)S(1)} %reshape.114.rows_ref, bf16[512,1536]{1,0:T(8,128)(2,1)} %bitcast.9.src_ref), custom_call_target="tpu_custom_call" | custom-call | flops 1 | bytes 1 | tf_op jit(solution)/shard_map/pallas_call | solution.py:25
  170.7 3.4 %collective-permute-done.19.b = bf16[384,1024]{1,0:T(8,128)(2,1)} collective-permute-done((bf16[384,1024]{1,0:T(8,128)(2,1)}, bf16[384,1024]{1,0:T(8,128)(2,1)}, u32[]{:S(2)}, u32[]{:S(2)}) %collective-permute-start.19) | collective-permute-done | bytes 786464 | tf_op jit(solution)/shard_map/ppermute | solution.py:48
  174.0 1.7 collective-permute-done.20.d
  175.7 2.8 %shard_map.141 = (bf16[384,1024]{1,0:T(8,128)(2,1)}, bf16[384,1024]{1,0:T(8,128)(2,1)}) custom-call(bf16[384,1024]{1,0:T(8,128)(2,1)S(1)} %copy-done.42, bf16[384,1024]{1,0:T(8,128)(2,1)} %collective-permute-done.19.b, bf16[384,1024]{1,0:T(8,128)(2,1)S(1)} %copy-done.44, bf16[384,1024]{1,0:T(8,128)(2,1)} %collective-permute-done.20.d), custom_call_target="tpu_custom_call" | custom-call | flops 12000000000 | bytes 1 | tf_op jit(solution)/shard_map/pallas_call | solution.py:25
  179.0 1.5 collective-permute-start.23
  182.3 10.2 %collective-permute-done.22 = bf16[384,1024]{1,0:T(8,128)(2,1)} collective-permute-done((bf16[384,1024]{1,0:T(8,128)(2,1)}, bf16[384,1024]{1,0:T(8,128)(2,1)}, u32[]{:S(2)}, u32[]{:S(2)}) %collective-permute-start.22) | collective-permute-done | bytes 786464 | tf_op jit(solution)/shard_map/ppermute | solution.py:48
  192.5 6.7 %collective-permute-done.21 = bf16[384,1024]{1,0:T(8,128)(2,1)} collective-permute-done((bf16[384,1024]{1,0:T(8,128)(2,1)}, bf16[384,1024]{1,0:T(8,128)(2,1)}, u32[]{:S(2)}, u32[]{:S(2)}) %collective-permute-start.21) | collective-permute-done | bytes 786464 | tf_op jit(solution)/shard_map/ppermute | solution.py:48
  199.3 2.9 %add_bitcast_fusion.1 = f32[1,384,1024]{2,1,0:T(8,128)} fusion(bf16[384,1024]{1,0:T(8,128)(2,1)} %collective-permute-done.22, bf16[384,1024]{1,0:T(8,128)(2,1)} %collective-permute-done.21, bf16[384,1024]{1,0:T(8,128)(2,1)S(1)} %copy-done.37), kind=kLoop, calls=%fused_computation.3 | loop fusion | flops 1966080 | bytes 3932160 | tf_op jit(solution)/shard_map/broadcast_in_dim | solution.py:426
  202.2 10.3 %collective-permute-done.23 = bf16[384,1024]{1,0:T(8,128)(2,1)} collective-permute-done((bf16[384,1024]{1,0:T(8,128)(2,1)}, bf16[384,1024]{1,0:T(8,128)(2,1)}, u32[]{:S(2)}, u32[]{:S(2)}) %collective-permute-start.23) | collective-permute-done | bytes 786464 | tf_op jit(solution)/shard_map/ppermute | solution.py:48
  212.5 2.9 %add_bitcast_fusion = f32[1,384,1024]{2,1,0:T(8,128)} fusion(bf16[384,1024]{1,0:T(8,128)(2,1)} %collective-permute-done.24, bf16[384,1024]{1,0:T(8,128)(2,1)} %collective-permute-done.23, bf16[384,1024]{1,0:T(8,128)(2,1)S(1)} %get-tuple-element.102), kind=kLoop, calls=%fused_computation.2 | loop fusion | flops 1966080 | bytes 3932160 | tf_op jit(solution)/shard_map/broadcast_in_dim | solution.py:427
  215.4 1.5 shard_map.139
  (148 shorter events, 32.3 us)
Async XLA Ops:
  4.4 29.2 %copy-start.48 = (bf16[1536,8]{0,1:T(8,128)(2,1)S(1)}, bf16[1536,8]{0,1:T(8,128)(2,1)}, u32[]{:S(2)}) copy-start(bf16[1536,8]{0,1:T(8,128)(2,1)} %param.11) | copy-start | bytes 73732
  4.4 30.1 %copy-start.45 = (s32[4]{0:T(128)S(1)}, s32[4]{0:T(128)}, u32[]{:S(2)}) copy-start(s32[4]{0:T(128)} %constant.72.clone) | copy-start | bytes 52
  4.4 30.8 %copy-start.29 = (bf16[256,1536]{1,0:T(8,128)(2,1)S(1)}, bf16[256,1536]{1,0:T(8,128)(2,1)}, u32[]{:S(2)}) copy-start(bf16[256,1536]{1,0:T(8,128)(2,1)} %src_ref.2) | copy-start | bytes 2359300
  4.4 44.3 %all-to-all-start = ((bf16[8,64,1536]{2,1,0:T(8,128)(2,1)}), bf16[8,64,1536]{2,1,0:T(8,128)(2,1)S(1)}, u32[]{:S(2)}, u32[]{:S(2)}) async-start(bf16[8,64,1536]{2,1,0:T(8,128)(2,1)} %bitcast.3), calls=%async_computation | async-start | bytes 3145728 | tf_op jit(solution)/shard_map/all_to_all | solution.py:244
  10.9 20.7 %collective-permute-start.1 = (bf16[384,1024]{1,0:T(8,128)(2,1)}, bf16[384,1024]{1,0:T(8,128)(2,1)}, u32[]{:S(2)}, u32[]{:S(2)}) collective-permute-start(bf16[384,1024]{1,0:T(8,128)(2,1)} %bitcast.5.refs_0_), channel_id=1, source_target_pairs={{0,16},{8,0},{16,24},{24,8},{1,17},{9,1},{17,25},{25,9},{2,18},{10... | collective-permute-start | bytes 2359304 | tf_op jit(solution)/shard_map/ppermute | solution.py:48
  12.4 20.7 %collective-permute-start.3 = (bf16[384,1024]{1,0:T(8,128)(2,1)}, bf16[384,1024]{1,0:T(8,128)(2,1)}, u32[]{:S(2)}, u32[]{:S(2)}) collective-permute-start(bf16[384,1024]{1,0:T(8,128)(2,1)} %bitcast.6.refs_4_), channel_id=1, source_target_pairs={{0,8},{8,24},{16,0},{24,16},{1,9},{9,25},{17,1},{25,17},{2,10},{10... | collective-permute-start | bytes 2359304 | tf_op jit(solution)/shard_map/ppermute | solution.py:48
  12.9 39.4 %collective-permute-start = (bf16[384,1024]{1,0:T(8,128)(2,1)}, bf16[384,1024]{1,0:T(8,128)(2,1)}, u32[]{:S(2)}, u32[]{:S(2)}) collective-permute-start(bf16[384,1024]{1,0:T(8,128)(2,1)} %bitcast.5.refs_0_), channel_id=1, source_target_pairs={{0,8},{8,24},{16,0},{24,16},{1,9},{9,25},{17,1},{25,17},{2,10},{10... | collective-permute-start | bytes 2359304 | tf_op jit(solution)/shard_map/ppermute | solution.py:48
  14.4 39.5 %collective-permute-start.5 = (bf16[384,1024]{1,0:T(8,128)(2,1)}, bf16[384,1024]{1,0:T(8,128)(2,1)}, u32[]{:S(2)}, u32[]{:S(2)}) collective-permute-start(bf16[384,1024]{1,0:T(8,128)(2,1)} %bitcast.6.refs_4_), channel_id=1, source_target_pairs={{0,16},{8,0},{16,24},{24,8},{1,17},{9,1},{17,25},{25,9},{2,18},{10... | collective-permute-start | bytes 2359304 | tf_op jit(solution)/shard_map/ppermute | solution.py:48
  31.5 33.7 %collective-permute-start.2 = (bf16[384,1024]{1,0:T(8,128)(2,1)}, bf16[384,1024]{1,0:T(8,128)(2,1)}, u32[]{:S(2)}, u32[]{:S(2)}) collective-permute-start(bf16[384,1024]{1,0:T(8,128)(2,1)} %collective-permute-done.1.refs_3_), channel_id=1, source_target_pairs={{0,16},{8,0},{16,24},{24,8},{1,17},{9,1},{17,25},{25,9},{2,18},{10... | collective-permute-start | bytes 2359304 | tf_op jit(solution)/shard_map/ppermute | solution.py:48
  33.1 33.7 %collective-permute-start.4 = (bf16[384,1024]{1,0:T(8,128)(2,1)}, bf16[384,1024]{1,0:T(8,128)(2,1)}, u32[]{:S(2)}, u32[]{:S(2)}) collective-permute-start(bf16[384,1024]{1,0:T(8,128)(2,1)} %collective-permute-done.3.refs_5_), channel_id=1, source_target_pairs={{0,8},{8,24},{16,0},{24,16},{1,9},{9,25},{17,1},{25,17},{2,10},{10... | collective-permute-start | bytes 2359304 | tf_op jit(solution)/shard_map/ppermute | solution.py:48
  48.7 18.1 %copy-start.2 = (bf16[8,64,1536]{2,1,0:T(8,128)(2,1)}, bf16[8,64,1536]{2,1,0:T(8,128)(2,1)S(1)}, u32[]{:S(2)}) copy-start(bf16[8,64,1536]{2,1,0:T(8,128)(2,1)S(1)} %all-to-all-done) | copy-start | bytes 4718596
  48.7 51.3 %all-to-all-start.2 = ((bf16[8,64,1536]{2,1,0:T(8,128)(2,1)}), bf16[8,64,1536]{2,1,0:T(8,128)(2,1)S(1)}, u32[]{:S(2)}, u32[]{:S(2)}) async-start(bf16[8,64,1536]{2,1,0:T(8,128)(2,1)} %bitcast.32), calls=%async_computation.2 | async-start | bytes 3145728 | tf_op jit(solution)/shard_map/all_to_all | solution.py:244
  52.3 31.5 %collective-permute-start.6 = (bf16[256,1536]{1,0:T(8,128)(2,1)}, bf16[256,1536]{1,0:T(8,128)(2,1)S(1)}, u32[]{:S(2)}, u32[]{:S(2)}) collective-permute-start(bf16[256,1536]{1,0:T(8,128)(2,1)} %bitcast.34), channel_id=1, source_target_pairs={{0,8},{8,24},{16,0},{24,16},{1,9},{9,25},{17,1},{25,17},{2,10},{10... | collective-permute-start | bytes 2359304 | tf_op jit(solution)/shard_map/ppermute | solution.py:48
  53.9 28.4 %collective-permute-start.7 = (bf16[256,1536]{1,0:T(8,128)(2,1)}, bf16[256,1536]{1,0:T(8,128)(2,1)S(1)}, u32[]{:S(2)}, u32[]{:S(2)}) collective-permute-start(bf16[256,1536]{1,0:T(8,128)(2,1)} %bitcast.35), channel_id=1, source_target_pairs={{0,16},{8,0},{16,24},{24,8},{1,17},{9,1},{17,25},{25,9},{2,18},{10... | collective-permute-start | bytes 2359304 | tf_op jit(solution)/shard_map/ppermute | solution.py:48
  82.2 11.5 %copy-start.15 = (bf16[1,256,1536]{2,1,0:T(8,128)(2,1)S(1)}, bf16[1,256,1536]{2,1,0:T(8,128)(2,1)}, u32[]{:S(2)}) copy-start(bf16[1,256,1536]{2,1,0:T(8,128)(2,1)} %param.14) | copy-start | bytes 2359300
  82.3 11.5 %copy-start.11 = (bf16[256,1536]{1,0:T(8,128)(2,1)}, bf16[256,1536]{1,0:T(8,128)(2,1)S(1)}, u32[]{:S(2)}) copy-start(bf16[256,1536]{1,0:T(8,128)(2,1)S(1)} %collective-permute-done.7.refs_3_) | copy-start | bytes 2359300
  82.3 10.1 %collective-permute-start.8 = (bf16[128,1536]{1,0:T(8,128)(2,1)S(1)}, bf16[128,1536]{1,0:T(8,128)(2,1)S(1)}, u32[]{:S(2)}, u32[]{:S(2)}) collective-permute-start(bf16[128,1536]{1,0:T(8,128)(2,1)S(1)} %slice.6), channel_id=1, source_target_pairs={{0,16},{8,0},{16,24},{24,8},{1,17},{9,1},{17,25},{25,9},{2,18},{10... | collective-permute-start | bytes 1179656 | tf_op jit(solution)/shard_map/ppermute | solution.py:48
  83.8 9.9 %copy-start.9 = (bf16[256,1536]{1,0:T(8,128)(2,1)}, bf16[256,1536]{1,0:T(8,128)(2,1)S(1)}, u32[]{:S(2)}) copy-start(bf16[256,1536]{1,0:T(8,128)(2,1)S(1)} %collective-permute-done.6.refs_1_) | copy-start | bytes 2359300
  83.9 9.9 %collective-permute-start.9 = (bf16[128,1536]{1,0:T(8,128)(2,1)S(1)}, bf16[128,1536]{1,0:T(8,128)(2,1)S(1)}, u32[]{:S(2)}, u32[]{:S(2)}) collective-permute-start(bf16[128,1536]{1,0:T(8,128)(2,1)S(1)} %slice.7), channel_id=1, source_target_pairs={{0,8},{8,24},{16,0},{24,16},{1,9},{9,25},{17,1},{25,17},{2,10},{10... | collective-permute-start | bytes 1179656 | tf_op jit(solution)/shard_map/ppermute | solution.py:48
  100.0 61.1 %all-to-all-start.1 = ((bf16[8,64,1536]{2,1,0:T(8,128)(2,1)}), bf16[8,64,1536]{2,1,0:T(8,128)(2,1)}, u32[]{:S(2)}, u32[]{:S(2)}) async-start(bf16[8,64,1536]{2,1,0:T(8,128)(2,1)} %bitcast.38), calls=%async_computation.1 | async-start | bytes 3145728 | tf_op jit(solution)/shard_map/all_to_all | solution.py:244
  104.5 8.8 %copy-start.18 = (f32[512,1024]{1,0:T(8,128)S(1)}, f32[512,1024]{1,0:T(8,128)}, u32[]{:S(2)}) copy-start(f32[512,1024]{1,0:T(8,128)} %copy-done.17) | copy-start | bytes 6291460
  104.5 8.8 %copy-start.22 = (bf16[128,1536]{1,0:T(8,128)(2,1)S(1)}, bf16[128,1536]{1,0:T(8,128)(2,1)}, u32[]{:S(2)}) copy-start(bf16[128,1536]{1,0:T(8,128)(2,1)} %copy-done.21) | copy-start | bytes 1179652
  104.5 8.8 %copy-start.24 = (bf16[128,1536]{1,0:T(8,128)(2,1)S(1)}, bf16[128,1536]{1,0:T(8,128)(2,1)}, u32[]{:S(2)}) copy-start(bf16[128,1536]{1,0:T(8,128)(2,1)} %copy-done.23) | copy-start | bytes 1179652
  106.6 6.7 %copy-start.10 = (bf16[256,1536]{1,0:T(8,128)(2,1)S(1)}, bf16[256,1536]{1,0:T(8,128)(2,1)}, u32[]{:S(2)}) copy-start(bf16[256,1536]{1,0:T(8,128)(2,1)} %copy-done.9) | copy-start | bytes 2359300
  106.6 6.7 %copy-start.12 = (bf16[256,1536]{1,0:T(8,128)(2,1)S(1)}, bf16[256,1536]{1,0:T(8,128)(2,1)}, u32[]{:S(2)}) copy-start(bf16[256,1536]{1,0:T(8,128)(2,1)} %copy-done.11) | copy-start | bytes 2359300
  106.6 6.7 %copy-start.16 = (bf16[1,256,1536]{2,1,0:T(8,128)(2,1)S(1)}, bf16[1,256,1536]{2,1,0:T(8,128)(2,1)}, u32[]{:S(2)}) copy-start(bf16[1,256,1536]{2,1,0:T(8,128)(2,1)} %param.14) | copy-start | bytes 2359300
  106.6 20.8 %collective-permute-start.10 = (bf16[128,1536]{1,0:T(8,128)(2,1)}, bf16[128,1536]{1,0:T(8,128)(2,1)}, u32[]{:S(2)}, u32[]{:S(2)}) collective-permute-start(bf16[128,1536]{1,0:T(8,128)(2,1)} %get-tuple-element.81), channel_id=1, source_target_pairs={{0,16},{8,0},{16,24},{24,8},{1,17},{9,1},{17,25},{25,9},{2,18},{10... | collective-permute-start | bytes 1179656 | tf_op jit(solution)/shard_map/ppermute | solution.py:48
  108.1 19.3 %collective-permute-start.11 = (bf16[128,1536]{1,0:T(8,128)(2,1)}, bf16[128,1536]{1,0:T(8,128)(2,1)}, u32[]{:S(2)}, u32[]{:S(2)}) collective-permute-start(bf16[128,1536]{1,0:T(8,128)(2,1)} %get-tuple-element.83), channel_id=1, source_target_pairs={{0,8},{8,24},{16,0},{24,16},{1,9},{9,25},{17,1},{25,17},{2,10},{10... | collective-permute-start | bytes 1179656 | tf_op jit(solution)/shard_map/ppermute | solution.py:48
  122.2 14.3 %copy-start.1 = (bf16[512,1024]{1,0:T(8,128)(2,1)S(1)}, bf16[512,1024]{1,0:T(8,128)(2,1)}, u32[]{:S(2)}) copy-start(bf16[512,1024]{1,0:T(8,128)(2,1)} %copy-done) | copy-start | bytes 3145732
  122.2 3.6 %collective-permute-start.14 = (f32[1,1536]{1,0:T(1,128)S(1)}, f32[1,1536]{1,0:T(1,128)S(1)}, u32[]{:S(2)}, u32[]{:S(2)}) collective-permute-start(f32[1,1536]{1,0:T(1,128)S(1)} %get-tuple-element.88), channel_id=1, source_target_pairs={{0,8},{8,0},{16,24},{24,16},{1,9},{9,1},{17,25},{25,17},{2,10},{10... | collective-permute-start | bytes 18440 | tf_op jit(solution)/shard_map/ppermute | solution.py:48
  125.9 7.3 %collective-permute-start.15 = (f32[1,1536]{1,0:T(1,128)S(1)}, f32[1,1536]{1,0:T(1,128)S(1)}, u32[]{:S(2)}, u32[]{:S(2)}) collective-permute-start(f32[1,1536]{1,0:T(1,128)S(1)} %add.99), channel_id=1, source_target_pairs={{0,16},{8,24},{16,0},{24,8},{1,17},{9,25},{17,1},{25,9},{2,18},{10... | collective-permute-start | bytes 18440 | tf_op jit(solution)/shard_map/ppermute | solution.py:48
  129.7 6.8 %copy-start.40 = (f32[512,1]{1,0:T(8,128)S(1)}, f32[512,1]{1,0:T(8,128)}, u32[]{:S(2)}) copy-start(f32[512,1]{1,0:T(8,128)} %copy-done.39) | copy-start | bytes 6148
  131.1 27.8 %collective-permute-start.12 = (bf16[256,1536]{1,0:T(8,128)(2,1)S(1)}, bf16[256,1536]{1,0:T(8,128)(2,1)S(1)}, u32[]{:S(2)}, u32[]{:S(2)}) collective-permute-start(bf16[256,1536]{1,0:T(8,128)(2,1)S(1)} %get-tuple-element.85), channel_id=1, source_target_pairs={{0,16},{8,0},{16,24},{24,8},{1,17},{9,1},{17,25},{25,9},{2,18},{10... | collective-permute-start | bytes 2359304 | tf_op jit(solution)/shard_map/ppermute | solution.py:48
  131.7 27.2 %collective-permute-start.13 = (bf16[256,1536]{1,0:T(8,128)(2,1)S(1)}, bf16[256,1536]{1,0:T(8,128)(2,1)S(1)}, u32[]{:S(2)}, u32[]{:S(2)}) collective-permute-start(bf16[256,1536]{1,0:T(8,128)(2,1)S(1)} %get-tuple-element.86), channel_id=1, source_target_pairs={{0,8},{8,24},{16,0},{24,16},{1,9},{9,25},{17,1},{25,17},{2,10},{10... | collective-permute-start | bytes 2359304 | tf_op jit(solution)/shard_map/ppermute | solution.py:48
  133.2 1.2 collective-permute-start.16
  134.4 22.0 %collective-permute-start.17 = (f32[2,1536]{1,0:T(2,128)S(1)}, f32[2,1536]{1,0:T(2,128)S(1)}, u32[]{:S(2)}, u32[]{:S(2)}) collective-permute-start(f32[2,1536]{1,0:T(2,128)S(1)} %pad_maximum_fusion.2), channel_id=1, source_target_pairs={{0,2},{1,3},{2,0},{3,1},{4,6},{5,7},{6,4},{7,5},{8,10},{9,11},{10,... | collective-permute-start | bytes 36872 | tf_op jit(solution)/shard_map/ppermute | solution.py:48
  136.5 9.1 %copy-start.7 = (bf16[4,384,512]{2,1,0:T(8,128)(2,1)S(1)}, bf16[4,384,512]{2,1,0:T(8,128)(2,1)}, u32[]{:S(2)}) copy-start(bf16[4,384,512]{2,1,0:T(8,128)(2,1)} %copy-done.5) | copy-start | bytes 4718596
  154.4 19.7 %collective-permute-start.19 = (bf16[384,1024]{1,0:T(8,128)(2,1)}, bf16[384,1024]{1,0:T(8,128)(2,1)}, u32[]{:S(2)}, u32[]{:S(2)}) collective-permute-start(bf16[384,1024]{1,0:T(8,128)(2,1)} %get-tuple-element.93), channel_id=1, source_target_pairs={{0,16},{8,0},{16,24},{24,8},{1,17},{9,1},{17,25},{25,9},{2,18},{10... | collective-permute-start | bytes 2359304 | tf_op jit(solution)/shard_map/ppermute | solution.py:48
  154.9 20.8 %collective-permute-start.20 = (bf16[384,1024]{1,0:T(8,128)(2,1)}, bf16[384,1024]{1,0:T(8,128)(2,1)}, u32[]{:S(2)}, u32[]{:S(2)}) collective-permute-start(bf16[384,1024]{1,0:T(8,128)(2,1)} %get-tuple-element.97), channel_id=1, source_target_pairs={{0,8},{8,24},{16,0},{24,16},{1,9},{9,25},{17,1},{25,17},{2,10},{10... | collective-permute-start | bytes 2359304 | tf_op jit(solution)/shard_map/ppermute | solution.py:48
  156.4 24.6 %collective-permute-start.18 = (f32[4,1536]{1,0:T(4,128)S(1)}, f32[4,1536]{1,0:T(4,128)S(1)}, u32[]{:S(2)}, u32[]{:S(2)}) collective-permute-start(f32[4,1536]{1,0:T(4,128)S(1)} %pad_maximum_fusion.1), channel_id=1, source_target_pairs={{0,4},{1,5},{2,6},{3,7},{4,0},{5,1},{6,2},{7,3},{8,12},{9,13},{10,... | collective-permute-start | bytes 73736 | tf_op jit(solution)/shard_map/ppermute | solution.py:48
  160.6 31.9 %collective-permute-start.22 = (bf16[384,1024]{1,0:T(8,128)(2,1)}, bf16[384,1024]{1,0:T(8,128)(2,1)}, u32[]{:S(2)}, u32[]{:S(2)}) collective-permute-start(bf16[384,1024]{1,0:T(8,128)(2,1)} %get-tuple-element.101), channel_id=1, source_target_pairs={{0,8},{8,24},{16,0},{24,16},{1,9},{9,25},{17,1},{25,17},{2,10},{10... | collective-permute-start | bytes 2359304 | tf_op jit(solution)/shard_map/ppermute | solution.py:48
  161.2 54.3 %all-to-all-start.3 = ((bf16[8,64,1536]{2,1,0:T(8,128)(2,1)}), bf16[8,64,1536]{2,1,0:T(8,128)(2,1)S(1)}, u32[]{:S(2)}, u32[]{:S(2)}) async-start(bf16[8,64,1536]{2,1,0:T(8,128)(2,1)} %bitcast.33), calls=%async_computation.3 | async-start | bytes 3145728 | tf_op jit(solution)/shard_map/all_to_all | solution.py:244
  167.7 8.0 %copy-start.42 = (bf16[384,1024]{1,0:T(8,128)(2,1)S(1)}, bf16[384,1024]{1,0:T(8,128)(2,1)}, u32[]{:S(2)}) copy-start(bf16[384,1024]{1,0:T(8,128)(2,1)} %copy-done.41) | copy-start | bytes 2359300
  167.7 8.0 %copy-start.44 = (bf16[384,1024]{1,0:T(8,128)(2,1)S(1)}, bf16[384,1024]{1,0:T(8,128)(2,1)}, u32[]{:S(2)}) copy-start(bf16[384,1024]{1,0:T(8,128)(2,1)} %copy-done.43) | copy-start | bytes 2359300
  175.7 23.6 %copy-start.37 = (bf16[384,1024]{1,0:T(8,128)(2,1)S(1)}, bf16[384,1024]{1,0:T(8,128)(2,1)}, u32[]{:S(2)}) copy-start(bf16[384,1024]{1,0:T(8,128)(2,1)} %copy-done.36) | copy-start | bytes 2359300
  178.5 20.8 %collective-permute-start.21 = (bf16[384,1024]{1,0:T(8,128)(2,1)}, bf16[384,1024]{1,0:T(8,128)(2,1)}, u32[]{:S(2)}, u32[]{:S(2)}) collective-permute-start(bf16[384,1024]{1,0:T(8,128)(2,1)} %get-tuple-element.99), channel_id=1, source_target_pairs={{0,16},{8,0},{16,24},{24,8},{1,17},{9,1},{17,25},{25,9},{2,18},{10... | collective-permute-start | bytes 2359304 | tf_op jit(solution)/shard_map/ppermute | solution.py:48
  179.0 33.5 %collective-permute-start.23 = (bf16[384,1024]{1,0:T(8,128)(2,1)}, bf16[384,1024]{1,0:T(8,128)(2,1)}, u32[]{:S(2)}, u32[]{:S(2)}) collective-permute-start(bf16[384,1024]{1,0:T(8,128)(2,1)} %get-tuple-element.104), channel_id=1, source_target_pairs={{0,16},{8,0},{16,24},{24,8},{1,17},{9,1},{17,25},{25,9},{2,18},{10... | collective-permute-start | bytes 2359304 | tf_op jit(solution)/shard_map/ppermute | solution.py:48
  180.5 32.0 %collective-permute-start.24 = (bf16[384,1024]{1,0:T(8,128)(2,1)}, bf16[384,1024]{1,0:T(8,128)(2,1)}, u32[]{:S(2)}, u32[]{:S(2)}) collective-permute-start(bf16[384,1024]{1,0:T(8,128)(2,1)} %get-tuple-element.105), channel_id=1, source_target_pairs={{0,8},{8,24},{16,0},{24,16},{1,9},{9,25},{17,1},{25,17},{2,10},{10... | collective-permute-start | bytes 2359304 | tf_op jit(solution)/shard_map/ppermute | solution.py:48
  (30 other events, 45.3 us)

commit v2 on v1

--- a/solution.py
+++ b/solution.py
@@ -8,7 +8,7 @@
 from jax.sharding import PartitionSpec as P
 
 F32 = jnp.float32
-KF, HP, HF, HS = 0, 0, 3e-05, 12e-6
+KF, HP, HF, HS = 0, 0, 3e-05, 0
 BF16 = jnp.bfloat16
 VMEM = pl.BlockSpec(memory_space=pltpu.VMEM)
 SMEM = pl.BlockSpec(memory_space=pltpu.SMEM)
@@ -36,6 +36,60 @@
     )(*args)
 
 
+class Copies:
+    def __init__(self, sems):
+        self.sems, self.used, self.sent = sems, 0, []
+
+    def _start(self, src, dst):
+        copy = pltpu.make_async_copy(src, dst, self.sems.at[self.used])
+        self.used += 1
+        copy.start()
+        return copy
+
+    def load(self, src, dst):
+        copy, waited = self._start(src, dst), []
+
+        def get():
+            if not waited:
+                copy.wait()
+                waited.append(True)
+            return dst
+
+        return get
+
+    def store(self, src, dst):
+        self.sent.append(self._start(src, dst))
+
+    def finish(self):
+        for copy in self.sent:
+            copy.wait()
+
+
+COPIES = 40
+
+
+def streamed(kernel, outs, args, scratch, scalars=0, small=0, hint=0):
+    def run(*refs):
+        copies = Copies(refs[-1])
+        kernel(copies, *refs[:-1])
+        copies.finish()
+
+    return pl.pallas_call(
+        run,
+        out_shape=list(outs),
+        in_specs=[SMEM] * scalars
+        + [VMEM] * small
+        + [pl.BlockSpec(memory_space=pl.ANY)] * (len(args) - scalars - small),
+        out_specs=[pl.BlockSpec(memory_space=pl.ANY)] * len(outs),
+        scratch_shapes=[pltpu.VMEM(tuple(d), t) for d, t in scratch]
+        + [pltpu.SemaphoreType.DMA((COPIES,))],
+        compiler_params=pltpu.CompilerParams(vmem_limit_bytes=58 << 20),
+        cost_estimate=pl.CostEstimate(
+            flops=int(hint * 1e15) + 1, bytes_accessed=1, transcendentals=0
+        ),
+    )(*args)
+
+
 def shape(dims, dtype):
     return jax.ShapeDtypeStruct(tuple(dims), dtype)
 
@@ -97,8 +151,8 @@
         h = (silu * b).astype(BF16)
         hd[:, cols] = h
         hdt[cols, :] = h.T
-        sa[:, cols] = silu
-        ua[:, cols] = b * sig * (1.0 + a * (1.0 - sig))
+        sa[:, cols] = silu.astype(BF16)
+        ua[:, cols] = (b * sig * (1.0 + a * (1.0 - sig))).astype(BF16)
         return carry
 
     lax.fori_loop(0, hidden // tile, step, 0)
@@ -110,56 +164,86 @@
     return pl.ds(pl.multiple_of(ids[s] * width, width), width)
 
 
-def down_far_kernel(n, ids, c, gcol, hdt, g, low, high):
-    g[...] = (gcol[...] * c[...].astype(F32)).astype(BF16)
-    width = hdt.shape[0] // n
-    far = dot(hdt[chunk_of(ids, n // 2, width), :], g[...]).astype(BF16)
-    low[...] = far[: width // 2]
-    high[...] = far[width // 2 :]
-
-
-def down_kernel(n, ids, g, hdt, *outs):
-    width = hdt.shape[0] // n
-    for out, s in zip(outs, [s for s in range(n) if s != n // 2]):
-        out[...] = dot(hdt[chunk_of(ids, s, width), :], g[...]).astype(BF16)
-
-
-def out_kernel(n, ids, hd, gcol, *refs):
-    downs = refs[: n + 1]
-    go, o_ref = refs[n + 1 :]
+def down_far_kernel(n, copies, ids, gcol, c_hbm, hdt_hbm, g_hbm, low, high, c, g, hdt, far):
+    width = hdt.shape[0]
+    get_c = copies.load(c_hbm, c)
+    get_h = copies.load(hdt_hbm.at[chunk_of(ids, n // 2, width), :], hdt)
+    g[...] = (gcol[...] * get_c()[...].astype(F32)).astype(BF16)
+    copies.store(g, g_hbm)
+    far[...] = dot(get_h()[...], g[...]).astype(BF16)
+    copies.store(far.at[: width // 2], low)
+    copies.store(far.at[width // 2 :], high)
+
+
+def down_kernel(n, copies, ids, g_hbm, hdt_hbm, *refs):
+    outs, (g, hdt, res) = refs[: n - 1], refs[n - 1 :]
+    width = hdt.shape[1]
+    rest = [s for s in range(n) if s != n // 2]
+    get_g = copies.load(g_hbm, g)
+    gets = [
+        copies.load(hdt_hbm.at[chunk_of(ids, s, width), :], hdt.at[i])
+        for i, s in enumerate(rest)
+    ]
+    get_g()
+    for i, out in enumerate(outs):
+        res[i] = dot(gets[i]()[...], g[...]).astype(BF16)
+        copies.store(res.at[i], out)
+
+
+def load_downs(copies, n, pieces, w):
+    half, cut = n // 2, pieces[n].shape[0]
+    gets = []
+    for s in range(n):
+        if s == half:
+            parts = [
+                copies.load(pieces[s], w.at[s, :cut]),
+                copies.load(pieces[n], w.at[s, cut:]),
+            ]
+            gets.append(lambda parts=parts: [p() for p in parts])
+        else:
+            gets.append(copies.load(pieces[s], w.at[s]))
+    return gets
+
+
+def out_kernel(n, copies, ids, gcol, hd_hbm, *refs):
+    pieces = refs[: n + 1]
+    go_hbm, o_hbm, hd, w, go, o = refs[n + 1 :]
     width = hd.shape[1] // n
-    half = n // 2
-
-    def term(s):
-        cols = pl.ds(pl.multiple_of(ids[s] * width, 128), width)
-        if s == half:
-            w = jnp.concatenate([downs[half][...], downs[n][...]], axis=0)
-        else:
-            w = downs[s][...]
-        return dot(hd[:, cols], w)
-
-    o = term(0)
-    for s in range(1, n):
-        o = o + term(s)
-    o = o.astype(BF16)
-    o_ref[...] = o
-    go[...] = (gcol[...] * o.astype(F32)).astype(BF16)
-
-
-def hidden_kernel(n, ids, g, sa, ua, *refs):
-    downs = refs[: n + 1]
-    da, db = refs[n + 1 :]
+    get_hd = copies.load(hd_hbm, hd)
+    gets = load_downs(copies, n, pieces, w)
+    get_hd()
+    for get in gets:
+        get()
+    rows = hd.shape[0] // 2
+    for h in range(2):
+        part = slice(h * rows, (h + 1) * rows)
+        total = dot(hd[part, chunk_of(ids, 0, width)], w[0])
+        for s in range(1, n):
+            total = total + dot(hd[part, chunk_of(ids, s, width)], w[s])
+        total = total.astype(BF16)
+        o[part, :] = total
+        go[part, :] = (gcol[part, :] * total.astype(F32)).astype(BF16)
+        copies.store(go.at[part], go_hbm.at[part])
+        copies.store(o.at[part], o_hbm.at[part])
+
+
+def hidden_kernel(n, copies, ids, g_hbm, sa_hbm, ua_hbm, *refs):
+    pieces = refs[: n + 1]
+    da_hbm, db_hbm, g, sa, ua, w, da, db = refs[n + 1 :]
     width = sa.shape[1] // n
-    half = n // 2
+    get_g = copies.load(g_hbm, g)
+    get_sa, get_ua = copies.load(sa_hbm, sa), copies.load(ua_hbm, ua)
+    gets = load_downs(copies, n, pieces, w)
+    get_g()
     for s in range(n):
-        cols = pl.ds(pl.multiple_of(ids[s] * width, 128), width)
-        if s == half:
-            w = jnp.concatenate([downs[half][...], downs[n][...]], axis=0)
-        else:
-            w = downs[s][...]
-        dh = dot(g[...], w, ((1,), (1,)))
-        da[:, cols] = (dh * ua[:, cols]).astype(BF16)
-        db[:, cols] = (dh * sa[:, cols]).astype(BF16)
+        cols = chunk_of(ids, s, width)
+        gets[s]()
+        dh = dot(g[...], w[s], ((1,), (1,)))
+        get_sa(), get_ua()
+        da[:, cols] = (dh * ua[:, cols].astype(F32)).astype(BF16)
+        db[:, cols] = (dh * sa[:, cols].astype(F32)).astype(BF16)
+        copies.store(da.at[:, cols], da_hbm.at[:, cols])
+        copies.store(db.at[:, cols], db_hbm.at[:, cols])
 
 
 def router_kernel(c, o, gcol, x, dl, router):
@@ -170,45 +254,79 @@
     router[...] = dot(dlogit, x[...], ((0,), (0,)))
 
 
-def weight_kernel(order, ids, xt, da, db, *outs):
-    tile = 256
-    for place, s in enumerate(order):
-        gate, up = outs[2 * place], outs[2 * place + 1]
-
-        def step(t, carry, s=s, gate=gate, up=up):
-            cols = pl.ds(pl.multiple_of(t * tile, tile), tile)
-            gate[:, cols] = dot(xt[ids[s]], da[:, cols]).astype(BF16)
-            up[:, cols] = dot(xt[ids[s]], db[:, cols]).astype(BF16)
-            return carry
-
-        lax.fori_loop(0, da.shape[1] // tile, step, 0)
-
-
-def rows_kernel(n, ids, da, db, dl, wr, *refs):
-    gates = refs[:n]
-    ups = refs[n : 2 * n]
-    out, scr = refs[2 * n :]
+def weight_kernel(order, copies, ids, da_hbm, db_hbm, xt_hbm, *refs):
+    outs = refs[: 2 * len(order)]
+    da, db, xt, res = refs[2 * len(order) :]
+    get_x = [copies.load(xt_hbm.at[ids[s]], xt.at[i]) for i, s in enumerate(order)]
+    get_da, get_db = copies.load(da_hbm, da), copies.load(db_hbm, db)
+    for i in range(len(order)):
+        get_x[i](), get_da()
+        res[2 * i] = dot(xt[i], da[...]).astype(BF16)
+        copies.store(res.at[2 * i], outs[2 * i])
+        get_db()
+        res[2 * i + 1] = dot(xt[i], db[...]).astype(BF16)
+        copies.store(res.at[2 * i + 1], outs[2 * i + 1])
+
+
+def rows_kernel(n, copies, ids, dl, wr, da_hbm, db_hbm, *refs):
+    gates, ups = refs[:n], refs[n : 2 * n]
+    out_hbm, da, db, wg, wu, scr, out = refs[2 * n :]
+    get_da, get_db = copies.load(da_hbm, da), copies.load(db_hbm, db)
+    gets = []
     for s in range(n):
-        scr[ids[s]] = dot(da[...], gates[s][...], ((1,), (1,))) + dot(
-            db[...], ups[s][...], ((1,), (1,))
-        )
+        gets += [copies.load(gates[s], wg.at[s]), copies.load(ups[s], wu.at[s])]
+    get_da(), get_db()
     chunk = scr.shape[2]
-    for d in range(n):
-        cols = slice(d * chunk, (d + 1) * chunk)
-        out[:, cols] = (scr[d] + dl[...] * wr[:, cols].astype(F32)).astype(BF16)
-
-
-def sum_far_kernel(low, high, nxt, prv, fwd, bwd):
+    for s in range(n):
+        gets[2 * s](), gets[2 * s + 1]()
+        total = dot(da[...], wg[s], ((1,), (1,))) + dot(db[...], wu[s], ((1,), (1,)))
+        scr[ids[s]] = (total + dl[...] * wr[ids[s]].astype(F32)).astype(BF16)
+        if chunk % 128 == 0:
+            copies.store(scr.at[ids[s]], out_hbm.at[:, chunk_of(ids, s, chunk)])
+    if chunk % 128:
+        for d in range(n):
+            out[:, d * chunk : (d + 1) * chunk] = scr[d]
+        copies.store(out, out_hbm)
+
+
+def sum_far_kernel(copies, low_hbm, high_hbm, nxt_hbm, prv_hbm, fwd_hbm, bwd_hbm, *bufs):
+    low, high, nxt, prv = bufs
     cut = low.shape[0]
-    fwd[:cut, :] = (nxt[:cut, :].astype(F32) + low[...].astype(F32)).astype(BF16)
-    fwd[cut:, :] = nxt[cut:, :]
-    bwd[:cut, :] = prv[:cut, :]
-    bwd[cut:, :] = (prv[cut:, :].astype(F32) + high[...].astype(F32)).astype(BF16)
-
-
-def sum_pair_kernel(a, b, c, d, first, second):
-    first[...] = (a[...].astype(F32) + b[...].astype(F32)).astype(BF16)
-    second[...] = (c[...].astype(F32) + d[...].astype(F32)).astype(BF16)
+    get_low, get_nxt = copies.load(low_hbm, low), copies.load(nxt_hbm, nxt)
+    get_high, get_prv = copies.load(high_hbm, high), copies.load(prv_hbm, prv)
+    get_low(), get_nxt()
+    nxt[:cut, :] = (nxt[:cut, :].astype(F32) + low[...].astype(F32)).astype(BF16)
+    copies.store(nxt, fwd_hbm)
+    get_high(), get_prv()
+    prv[cut:, :] = (prv[cut:, :].astype(F32) + high[...].astype(F32)).astype(BF16)
+    copies.store(prv, bwd_hbm)
+
+
+def sum_pair_kernel(copies, gate_n, far_g, up_n, up_p, far_u, gate_p, fwd, bwd, *bufs):
+    gets = [
+        copies.load(src, dst)
+        for src, dst in zip((gate_n, far_g, up_p, far_u, up_n, gate_p), bufs)
+    ]
+    a, b, c, d, e, f = bufs
+    gets[0](), gets[1]()
+    a[...] = (a[...].astype(F32) + b[...].astype(F32)).astype(BF16)
+    copies.store(a, fwd.at[0])
+    gets[2](), gets[3]()
+    c[...] = (c[...].astype(F32) + d[...].astype(F32)).astype(BF16)
+    copies.store(c, bwd.at[1])
+    gets[4](), gets[5]()
+    copies.store(e, fwd.at[1])
+    copies.store(f, bwd.at[0])
+
+
+def final_kernel(copies, gate_own, up_own, fwd, bwd, gate, up, bufs, out):
+    sources = [gate_own, up_own, fwd.at[0], fwd.at[1], bwd.at[0], bwd.at[1]]
+    gets = [copies.load(src, bufs.at[i]) for i, src in enumerate(sources)]
+    for i, dst in enumerate((gate, up)):
+        for get in gets[i::2]:
+            get()
+        out[i] = bufs[i].astype(F32) + bufs[2 + i].astype(F32) + bufs[4 + i].astype(F32)
+        copies.store(out.at[i], dst)
 
 
 def scatter_kernel(rows_ref, src_ref, out_ref):
@@ -281,8 +399,8 @@
             shape((n, model // n, slots), BF16),
             shape((slots, hidden), BF16),
             shape((hidden, slots), BF16),
-            shape((slots, hidden), F32),
-            shape((slots, hidden), F32),
+            shape((slots, hidden), BF16),
+            shape((slots, hidden), BF16),
             shape((slots, 1), F32),
         ],
         [ids, x_all, w_router, *gate_list, *up_list],
@@ -296,47 +414,53 @@
     far_b = ring_hop(after(downs[half - 1], hd)[cut:], n, -1)
     down_list = [far_a if s == half else downs[s] for s in range(n)] + [far_b]
     width = hidden // n
-    go, o_all = call(
+    g_all, low, high = streamed(
+        functools.partial(down_far_kernel, n),
+        [shape((slots, model), BF16)] + [shape((width // 2, model), BF16)] * 2,
+        [ids, gcol, c_all, hdt],
+        [((slots, model), BF16)] * 2 + [((width, slots), BF16), ((width, model), BF16)],
+        scalars=1,
+        small=1,
+    )
+    go, o_all = streamed(
         functools.partial(out_kernel, n),
         [shape((slots, model), BF16)] * 2,
-        [ids, hd, gcol, *down_list],
-        matmul,
+        [ids, after(gcol, g_all), hd, *down_list],
+        [((slots, hidden), BF16), ((n, width, model), BF16)] + [((slots, model), BF16)] * 2,
         scalars=1,
+        small=1,
     )
     o_rows = exchange(go)
-    g_all, low, high = call(
-        functools.partial(down_far_kernel, n),
-        [shape((slots, model), BF16)] + [shape((width // 2, model), BF16)] * 2,
-        [ids, c_all, after(gcol, go), hdt],
-        matmul / n,
-        scalars=1,
-    )
-    down_rest = call(
+    down_rest = streamed(
         functools.partial(down_kernel, n),
         [shape((width, model), BF16)] * (n - 1),
-        [ids, g_all, hdt],
-        matmul * (n - 1) / n,
+        [ids, after(g_all, go), hdt],
+        [((slots, model), BF16), ((n - 1, width, slots), BF16), ((n - 1, width, model), BF16)],
         scalars=1,
     )
+
     down_of = dict(zip([s for s in range(n) if s != half], down_rest))
     low, high = ring_hop(low, n, 1), ring_hop(high, n, -1)
 
     def plus(a, b):
         return (a.astype(F32) + b.astype(F32)).astype(BF16)
 
-    da, db = call(
-        functools.partial(hidden_kernel, n),
-        [shape((slots, hidden), BF16)] * 2,
-        [ids, after(g_all, *down_rest), sa, ua, *down_list],
-        matmul,
-        scalars=1,
-    )
-    low, high = after(low, da), after(high, da)
-    fwd, bwd = call(
+    fwd, bwd = streamed(
         sum_far_kernel,
         [shape((width, model), BF16)] * 2,
         [low, high, down_of[half - 1], down_of[(half + 1) % n]],
-        0,
+        [((width // 2, model), BF16)] * 2 + [((width, model), BF16)] * 2,
+        hint=25e-6,
+    )
+    da, db = streamed(
+        functools.partial(hidden_kernel, n),
+        [shape((slots, hidden), BF16)] * 2,
+        [ids, after(g_all, fwd, bwd), sa, ua, *down_list],
+        [((slots, model), BF16)]
+        + [((slots, hidden), BF16)] * 2
+        + [((n, width, model), BF16)]
+        + [((slots, hidden), BF16)] * 2,
+        scalars=1,
     )
     for s in range(half - 1, 0, -1):
         fwd = ring_hop(fwd, n, 1)
@@ -348,37 +472,25 @@
     gate_of, up_of = {}, {}
 
     def weights(order_of, da):
-        grads = call(
+        count = len(order_of)
+        grads = streamed(
             functools.partial(weight_kernel, order_of),
-            [shape((model // n, hidden), BF16)] * (2 * len(order_of)),
-            [ids, xt, da, db],
-            2 * matmul * len(order_of) / n,
+            [shape((model // n, hidden), BF16)] * (2 * count),
+            [ids, da, db, xt],
+            [((slots, hidden), BF16)] * 2
+            + [((count, model // n, slots), BF16), ((2 * count, model // n, hidden), BF16)],
             scalars=1,
         )
         for i, s in enumerate(order_of):
             gate_of[s], up_of[s] = grads[2 * i], grads[2 * i + 1]
 
     weights([half], da)
-    far_w = list(gate_of.values())
     dl, router_row = call(
         router_kernel,
         [shape((slots, 1), F32), shape((1, model), F32)],
-        [c_all, after(o_all, *far_w), gcol, x_all],
+        [c_all, after(o_all, *gate_of.values()), gcol, x_all],
         0,
     )
-
-    total = router_row
-    bit = 1
-    while bit < n:
-        total = total + hop(total, "dp", n, lambda i, b=bit: i ^ b)
-        bit *= 2
-    bit = 1
-    while bit < experts:
-        total = jnp.concatenate(
-            [total, hop(total, "expert", experts, lambda i, b=bit: i ^ b)], axis=0
-        )
-        bit *= 2
-    grad_router = jnp.take(total, e_me ^ jnp.arange(experts, dtype=jnp.int32), axis=0).T
 
     def scatter(source):
         return call(
@@ -386,40 +498,63 @@
         )[0]
 
     mixed = scatter(o_rows)
-    wr_row = lax.dynamic_slice_in_dim(w_router.T, e_me, 1, axis=0)
-    d_rows = call(
+    wr_row = lax.dynamic_slice_in_dim(w_router.T, e_me, 1, axis=0).reshape(n, 1, model // n)
+    d_rows = streamed(
         functools.partial(rows_kernel, n),
         [shape((slots, model), BF16)],
-        [ids, after(da, *gate_of.values()), db, dl, wr_row, *gate_list, *up_list],
-        2 * matmul,
+        [ids, dl, wr_row, after(da, fwd, bwd, *gate_of.values()), db, *gate_list, *up_list],
+        [((slots, hidden), BF16)] * 2
+        + [((n, model // n, hidden), BF16)] * 2
+        + [((n, slots, model // n), BF16), ((slots, model), BF16)],
         scalars=1,
-        scratch=[pltpu.VMEM((n, slots, model // n), F32)],
+        small=2,
     )[0]
-    r_rows = exchange(after(d_rows, fwd, bwd))
+    r_rows = exchange(d_rows)
     weights([s for s in range(n) if s != half], after(da, d_rows))
 
-    far_g = ring_hop(after(gate_of[half], low), n, 1)
-    far_u = ring_hop(after(up_of[half], high), n, -1)
-    fwd_u, bwd_g = after(up_of[half - 1], fwd), after(gate_of[(half + 1) % n], bwd)
-    far_g, far_u = after(far_g, mixed, down_grad), after(far_u, mixed, down_grad)
-    fwd_g, bwd_u = call(
+    far_g = ring_hop(after(gate_of[half], fwd, dl, wr_row), n, 1)
+    far_u = ring_hop(after(up_of[half], bwd, dl, wr_row), n, -1)
+    fwd, bwd = streamed(
         sum_pair_kernel,
-        [shape((model // n, hidden), BF16)] * 2,
-        [gate_of[half - 1], far_g, up_of[(half + 1) % n], far_u],
-        0,
-        hint=HS,
+        [shape((2, model // n, hidden), BF16)] * 2,
+        [
+            gate_of[half - 1],
+            far_g,
+            up_of[half - 1],
+            up_of[(half + 1) % n],
+            far_u,
+            gate_of[(half + 1) % n],
+        ],
+        [((model // n, hidden), BF16)] * 6,
+        hint=16e-6,
     )
     for s in range(half - 1, 0, -1):
-        fwd_u, fwd_g = ring_hop(fwd_u, n, 1), ring_hop(fwd_g, n, 1)
-        bwd_g, bwd_u = ring_hop(bwd_g, n, -1), ring_hop(bwd_u, n, -1)
+        fwd, bwd = ring_hop(fwd, n, 1), ring_hop(bwd, n, -1)
         if s > 1:
-            fwd_u, fwd_g = plus(up_of[s - 1], fwd_u), plus(gate_of[s - 1], fwd_g)
-            bwd_g, bwd_u = plus(gate_of[n - s + 1], bwd_g), plus(up_of[n - s + 1], bwd_u)
-    fwd, bwd = (fwd_g, fwd_u), (bwd_g, bwd_u)
-    grad_gate = gate_of[0].astype(F32) + fwd[0].astype(F32) + bwd[0].astype(F32)
-    grad_up = up_of[0].astype(F32) + fwd[1].astype(F32) + bwd[1].astype(F32)
-
-    grad_tokens = scatter(after(r_rows, total))
+            fwd = plus(jnp.stack([gate_of[s - 1], up_of[s - 1]]), fwd)
+            bwd = plus(jnp.stack([gate_of[n - s + 1], up_of[n - s + 1]]), bwd)
+    grad_tokens = scatter(r_rows)
+    router_row = after(router_row, mixed, down_grad, grad_tokens)
+    pair = jnp.concatenate(
+        [router_row, hop(router_row, "expert", experts, lambda i: i ^ 1)], axis=0
+    )
+    total = jnp.concatenate(
+        [pair]
+        + [
+            hop(pair, "expert", experts, lambda i, k=k: i ^ (2 * k))
+            for k in range(1, experts // 2)
+        ],
+        axis=0,
+    )
+    total = sum([hop(total, "dp", n, lambda i, b=b: i ^ b) for b in range(1, n)], total)
+    grad_router = jnp.take(total, e_me ^ jnp.arange(experts, dtype=jnp.int32), axis=0).T
+    grad_gate, grad_up = streamed(
+        final_kernel,
+        [shape((model // n, hidden), F32)] * 2,
+        [gate_of[0], up_of[0], fwd, bwd],
+        [((6, model // n, hidden), BF16), ((2, model // n, hidden), F32)],
+        hint=2.5e-05,
+    )
     return (
         mixed,
         grad_tokens,

time: 218 us -> 211 us (0.968)
  Pallas kernels: 47.5 us -> 71.5 us
  waiting for transfers between devices: 86.6 us -> 72.7 us
  local copies, waits for them, and re-layouts: 27.1 us -> 15.5 us
  other arithmetic: 10.3 us -> 4.42 us
    pallas_call x0 -> x10, Pallas kernels: none -> 55.8 us  [streamed(): pl.pallas_call(run, out_shape=list(outs), in_specs=[SMEM] * scalars + [VM...]
    ppermute x25, waiting for transfers between devices: 74.9 us -> 35.9 us  [hop(): return lax.ppermute(x, axis, [(i, target(i)) for i in range(size)])]
    pallas_call x15 -> x6, Pallas kernels: 47.5 us -> 15.7 us  [call(): pl.pallas_call(kernel, out_shape=list(outs), in_specs=[SMEM] * scalars +...]
    all_to_all x4, waiting for transfers between devices: 11.7 us -> 36.8 us  [exchange(): lax.all_to_all(x.reshape(experts, part, model), 'expert', split_axis=0, c...]
    unnamed x99 -> x43, local copies, waits for them, and re-layouts: 25.7 us -> 11.2 us
    broadcast_in_dim x2 -> x0, other arithmetic: 5.84 us -> none  [the longest x1 2.92 us: body(): grad_up[None]]
  transfers between devices with their start and end apart: 29 -> 29, of which waited for: 13 -> 13; matrix products, arithmetic and copies ran while one was open for 5% -> 3% of each run, Pallas kernels for 20% -> 33%
where the time goes in v2:
time: 211 us; the launch traced here: 210 us
  waiting for transfers between devices  72.7 us (34%)
  Pallas kernels  71.5 us (34%)
  starting transfers between devices  44.9 us (21%)
  local copies, waits for them, and re-layouts  15.5 us (7%)
  other arithmetic  4.42 us (2%)
    pallas_call x10, Pallas kernels, streamed(): pl.pallas_call(run, out_shape=list(outs), in_specs=[SMEM] * scalars + [VM...  55.8 us
    all_to_all x4, waiting for transfers between devices, exchange(): lax.all_to_all(x.reshape(experts, part, model), 'expert', split_axis=0, c...  36.8 us
    ppermute x25, waiting for transfers between devices, hop(): return lax.ppermute(x, axis, [(i, target(i)) for i in range(size)])  35.9 us
    ppermute x25, starting transfers between devices, hop(): return lax.ppermute(x, axis, [(i, target(i)) for i in range(size)])  26.5 us
    all_to_all x4, starting transfers between devices, exchange(): lax.all_to_all(x.reshape(experts, part, model), 'expert', split_axis=0, c...  18.4 us
    pallas_call x6, Pallas kernels, call(): pl.pallas_call(kernel, out_shape=list(outs), in_specs=[SMEM] * scalars +...  15.7 us
    unnamed x43, local copies, waits for them, and re-layouts  11.2 us
  transfers between devices with their start and end apart: 29, of which 13 were waited for; matrix products, arithmetic and copies ran while one was open for 3% of the time, Pallas kernels for 33%

profile of v2, /device:TPU:0, one launch (start us, length us, event | category | flops | bytes accessed | tf_op | source)
XLA Modules:
  0.0 210.0 jit_solution(7303187759797920014)
XLA Ops:
  1.5 1.1 copy-done.11
  2.7 1.8 shard_map.127
  4.4 6.4 %all-to-all-start = ((bf16[8,64,1536]{2,1,0:T(8,128)(2,1)}), bf16[8,64,1536]{2,1,0:T(8,128)(2,1)S(1)}, u32[]{:S(2)}, u32[]{:S(2)}) async-start(bf16[8,64,1536]{2,1,0:T(8,128)(2,1)} %bitcast.3), calls=%async_computation | async-start | bytes 3145728 | tf_op jit(solution)/shard_map/all_to_all | solution.py:362
  10.9 1.5 collective-permute-start.1
  12.9 1.5 collective-permute-start.5
  14.9 16.6 %collective-permute-done.1.refs_3_.refs_8_ = bf16[384,1024]{1,0:T(8,128)(2,1)} collective-permute-done((bf16[384,1024]{1,0:T(8,128)(2,1)}, bf16[384,1024]{1,0:T(8,128)(2,1)}, u32[]{:S(2)}, u32[]{:S(2)}) %collective-permute-start.1) | collective-permute-done | bytes 786464 | tf_op jit(solution)/shard_map/ppermute | solution.py:102
  31.5 1.5 collective-permute-start.2
  35.2 1.1 copy-done.2
  36.4 12.4 %all-to-all-done = bf16[8,64,1536]{2,1,0:T(8,128)(2,1)S(1)} async-done(((bf16[8,64,1536]{2,1,0:T(8,128)(2,1)}), bf16[8,64,1536]{2,1,0:T(8,128)(2,1)S(1)}, u32[]{:S(2)}, u32[]{:S(2)}) %all-to-all-start) | async-done | bytes 1572896 | tf_op jit(solution)/shard_map/all_to_all | solution.py:362
  48.7 3.6 %all-to-all-start.1 = ((bf16[8,64,1536]{2,1,0:T(8,128)(2,1)}), bf16[8,64,1536]{2,1,0:T(8,128)(2,1)S(1)}, u32[]{:S(2)}, u32[]{:S(2)}) async-start(bf16[8,64,1536]{2,1,0:T(8,128)(2,1)} %bitcast.30), calls=%async_computation.1 | async-start | bytes 3145728 | tf_op jit(solution)/shard_map/all_to_all | solution.py:362
  52.3 1.6 collective-permute-start.6
  54.4 10.8 %collective-permute-done.2.refs_2_.refs_7_ = bf16[384,1024]{1,0:T(8,128)(2,1)} collective-permute-done((bf16[384,1024]{1,0:T(8,128)(2,1)}, bf16[384,1024]{1,0:T(8,128)(2,1)}, u32[]{:S(2)}, u32[]{:S(2)}) %collective-permute-start.2) | collective-permute-done | bytes 786464 | tf_op jit(solution)/shard_map/ppermute | solution.py:102
  65.2 1.6 collective-permute-done.4.refs_6_.refs_11_
  66.8 9.6 %shard_map.128 = (bf16[4,384,512]{2,1,0:T(8,128)(2,1)S(1)}, bf16[512,1024]{1,0:T(8,128)(2,1)S(1)}, bf16[1024,512]{1,0:T(8,128)(2,1)S(1)}, bf16[512,1024]{1,0:T(8...) custom-call(s32[5]{0:T(128)S(1)} %pad_add_fusion.ids.refs_0_, bf16[512,1536]{1,0:T(8,128)(2,1)S(1)} %bitcast.26, ...), custom_call_target="tpu_custom_call" | custom-call | flops 30000001024 | bytes 1 | tf_op jit(solution)/shard_map/pallas_call | solution.py:25
  81.1 1.7 collective-permute-done.6.refs_4_.refs_5_
  85.0 1.6 collective-permute-start.8
  86.5 3.5 %all-to-all-done.1 = bf16[8,64,1536]{2,1,0:T(8,128)(2,1)S(1)} async-done(((bf16[8,64,1536]{2,1,0:T(8,128)(2,1)}), bf16[8,64,1536]{2,1,0:T(8,128)(2,1)S(1)}, u32[]{:S(2)}, u32[]{:S(2)}) %all-to-all-start.1) | async-done | bytes 1572896 | tf_op jit(solution)/shard_map/all_to_all | solution.py:362
  90.1 1.1 copy-done
  91.2 4.5 %shard_map.130 = (bf16[512,1536]{1,0:T(8,128)(2,1)}, bf16[128,1536]{1,0:T(8,128)(2,1)}, bf16[128,1536]{1,0:T(8,128)(2,1)}) custom-call(s32[5]{0:T(128)} %copy-done.14, f32[512,1]{1,0:T(8,128)} %copy-done.5, bf16[512,1536]{1,0:T(8,128)(2,1)} %bitcast.24, bf16[1024,512]{1,0:T(8,128)(2,1)} %copy-done.4), custom_call_target="tpu_custom_call" | custom-call | flops 1 | bytes 1 | tf_op jit(solution)/shard_map/pallas_call | solution.py:77
  95.7 1.6 collective-permute-start.10
  98.5 6.4 %shard_map.131 = (bf16[512,1536]{1,0:T(8,128)(2,1)}, bf16[512,1536]{1,0:T(8,128)(2,1)}) custom-call(s32[5]{0:T(128)} %copy-done.14, f32[512,1]{1,0:T(8,128)} %copy-done.5, bf16[512,1024]{1,0:T(8,128)(2,1)} %copy-done.8, bf16[256,1536]{1,0:T(8,128)(2,1)} %bitcast.34, bf16[256,1536]{1,0:T(8,128)(2,1)} %copy-done.16, ...), custom_call_target="tpu_custom_call" | custom-call | flops 1 | bytes 1 | tf_op jit(solution)/shard_map/pallas_call | solution.py:77
  105.0 3.6 %all-to-all-start.2 = ((bf16[8,64,1536]{2,1,0:T(8,128)(2,1)}), bf16[8,64,1536]{2,1,0:T(8,128)(2,1)S(1)}, u32[]{:S(2)}, u32[]{:S(2)}) async-start(bf16[8,64,1536]{2,1,0:T(8,128)(2,1)} %bitcast.36), calls=%async_computation.2 | async-start | bytes 3145728 | tf_op jit(solution)/shard_map/all_to_all | solution.py:362
  108.6 5.1 %shard_map.133 = (bf16[256,1536]{1,0:T(8,128)(2,1)}, bf16[256,1536]{1,0:T(8,128)(2,1)}, bf16[256,1536]{1,0:T(8,128)(2,1)}) custom-call(s32[5]{0:T(128)} %copy-done.14, bf16[512,1536]{1,0:T(8,128)(2,1)} %get-tuple-element.71.refs_1_, bf16[1024,512]{1,0:T(8,128)(2,1)} %copy-done.4), custom_call_target="tpu_custom_call" | custom-call | flops 1 | bytes 1 | tf_op jit(solution)/shard_map/pallas_call | solution.py:77
  113.7 3.0 %shard_map.134 = (bf16[256,1536]{1,0:T(8,128)(2,1)}, bf16[256,1536]{1,0:T(8,128)(2,1)}) custom-call(bf16[128,1536]{1,0:T(8,128)(2,1)} %collective-permute-done.10.refs_0_, bf16[128,1536]{1,0:T(8,128)(2,1)} %collective-permute-done.11.refs_1_, bf16[256,1536]{1,0:T(8,128)(2,1)} %get-tuple-element.67.refs_2_, bf16[256,1536]{1,0:T(8,128)(2,1)} %get-tuple-element.68.refs_3_), custom_call_target="tpu_custom_call" | custom-call | flops 24999999488 | bytes 1 | tf_op jit(solution)/shard_map/pallas_call | solution.py:77
  116.6 1.6 collective-permute-start.13
  118.7 1.3 constant_dynamic-slice_fusion
  120.0 8.2 %shard_map.135 = (bf16[512,1024]{1,0:T(8,128)(2,1)}, bf16[512,1024]{1,0:T(8,128)(2,1)}) custom-call(s32[5]{0:T(128)} %copy-done.14, bf16[512,1536]{1,0:T(8,128)(2,1)} %get-tuple-element.71.refs_1_, bf16[512,1024]{1,0:T(8,128)(2,1)} %copy-done.9, bf16[512,1024]{1,0:T(8,128)(2,1)} %copy-done.10, bf16[256,1536]{1,0:T(8,128)(2,1)} %bitcast.35, ...), custom_call_target="tpu_custom_call" | custom-call | flops 1 | bytes 1 | tf_op jit(solution)/shard_map/pallas_call | solution.py:77
  128.2 4.6 %shard_map.136 = (bf16[384,1024]{1,0:T(8,128)(2,1)}, bf16[384,1024]{1,0:T(8,128)(2,1)}) custom-call(s32[5]{0:T(128)} %copy-done.14, bf16[512,1024]{1,0:T(8,128)(2,1)} %get-tuple-element.81.refs_1_.refs_3_, bf16[512,1024]{1,0:T(8,128)(2,1)} %get-tuple-element.75.refs_2_.refs_4_, bf16[4,384,512]{2,1,0:T(8,128)(2,1)} %copy-done.3), custom_call_target="tpu_custom_call" | custom-call | flops 1 | bytes 1 | tf_op jit(solution)/shard_map/pallas_call | solution.py:77
  132.8 1.4 copy-done.7
  135.7 1.1 collective-permute-done.13
  136.9 1.2 collective-permute-done.12
  138.6 1.5 collective-permute-start.15
  140.1 9.2 %shard_map.138 = bf16[512,1536]{1,0:T(8,128)(2,1)} custom-call(s32[5]{0:T(128)} %copy-done.14, f32[512,1]{1,0:T(8,128)} %copy-done.13, bf16[4,1,384]{2,1,0:T(2,128)(2,1)} %bitcast.38, bf16[512,1024]{1,0:T(8,128)(2,1)} %get-tuple-element.81.refs_1_.refs_3_, bf16[512,1024]{1,0:T(8,128)(2,1)} %get-tuple-element.75.refs_2_.refs_4_, ...), custom_call_target="tpu_custom_call" | custom-call | flops 1 | bytes 1 | tf_op jit(solution)/shard_map/pallas_call | solution.py:77
  149.4 4.8 %all-to-all-start.3 = ((bf16[8,64,1536]{2,1,0:T(8,128)(2,1)}), bf16[8,64,1536]{2,1,0:T(8,128)(2,1)S(1)}, u32[]{:S(2)}, u32[]{:S(2)}) async-start(bf16[8,64,1536]{2,1,0:T(8,128)(2,1)} %bitcast.31), calls=%async_computation.3 | async-start | bytes 3145728 | tf_op jit(solution)/shard_map/all_to_all | solution.py:362
  154.1 6.6 %shard_map.140 = (bf16[384,1024]{1,0:T(8,128)(2,1)}, bf16[384,1024]{1,0:T(8,128)(2,1)}, bf16[384,1024]{1,0:T(8,128)(2,1)}, bf16[384,1024]{1,0:T(8,128)(2,1)}, bf...) custom-call(s32[5]{0:T(128)} %copy-done.14, bf16[512,1024]{1,0:T(8,128)(2,1)} %get-tuple-element.81.refs_1_.refs_3_, ...), custom_call_target="tpu_custom_call" | custom-call | flops 1 | bytes 1 | tf_op jit(solution)/shard_map/pallas_call | solution.py:77
  160.8 3.9 %shard_map.141 = (bf16[2,384,1024]{2,1,0:T(8,128)(2,1)}, bf16[2,384,1024]{2,1,0:T(8,128)(2,1)}) custom-call(bf16[384,1024]{1,0:T(8,128)(2,1)} %get-tuple-element.84.refs_0_, bf16[384,1024]{1,0:T(8,128)(2,1)} %collective-permute-done.14.refs_1_, bf16[384,1024]{1,0:T(8,128)(2,1)} %get-tuple-element.86.refs_2_, bf16[384,1024]{1,0:T(8,128)(2,1)} %get-tuple-element.87.refs_3_, ...), custom_call_target="tpu_custom_call" | custom-call | flops 16000000000 | bytes 1 | tf_op jit(solution)/shard_map/pallas_call | solution.py:77
  165.3 1.5 collective-permute-start.17
  166.8 2.8 %convert_add_fusion = f32[256,1536]{1,0:T(8,128)} fusion(bf16[256,1536]{1,0:T(8,128)(2,1)} %collective-permute-done.13, bf16[256,1536]{1,0:T(8,128)(2,1)} %collective-permute-done.12, bf16[256,1536]{1,0:T(8,128)(2,1)S(1)} %copy-done.19), kind=kLoop, calls=%fused_computation.2 | loop fusion | flops 1966080 | bytes 3932160 | tf_op jit(solution)/shard_map/add | solution.py:470
  169.6 1.5 shard_map.132
  171.1 20.9 %all-to-all-done.3 = bf16[8,64,1536]{2,1,0:T(8,128)(2,1)S(1)} async-done(((bf16[8,64,1536]{2,1,0:T(8,128)(2,1)}), bf16[8,64,1536]{2,1,0:T(8,128)(2,1)S(1)}, u32[]{:S(2)}, u32[]{:S(2)}) %all-to-all-start.3) | async-done | bytes 1572896 | tf_op jit(solution)/shard_map/all_to_all | solution.py:362
  192.0 1.5 shard_map.139
  193.4 1.2 collective-permute-done.18
  194.6 1.3 collective-permute-start.21
  195.9 3.1 %collective-permute-start.19 = (f32[2,1536]{1,0:T(2,128)S(1)}, f32[2,1536]{1,0:T(2,128)S(1)}, u32[]{:S(2)}, u32[]{:S(2)}) collective-permute-start(f32[2,1536]{1,0:T(2,128)S(1)} %pad_maximum_fusion), channel_id=1, source_target_pairs={{0,2},{1,3},{2,0},{3,1},{4,6},{5,7},{6,4},{7,5},{8,10},{9,11},{10,... | collective-permute-start | bytes 36872 | tf_op jit(solution)/shard_map/ppermute | solution.py:102
  199.1 1.1 collective-permute-done.21
  200.8 1.5 collective-permute-start.24
  202.3 1.5 collective-permute-start.23
  204.4 4.4 %shard_map.142 = (f32[384,1024]{1,0:T(8,128)}, f32[384,1024]{1,0:T(8,128)}) custom-call(bf16[384,1024]{1,0:T(8,128)(2,1)} %get-tuple-element.82.refs_0_, bf16[384,1024]{1,0:T(8,128)(2,1)} %get-tuple-element.83.refs_1_, bf16[2,384,1024]{2,1,0:T(8,128)(2,1)} %collective-permute-done.16.refs_2_, bf16[2,384,1024]{2,1,0:T(8,128)(2,1)} %collective-permute-done.17.refs_3_), custom_call_target="tpu_custom_call" | custom-call | flops 24999999488 | bytes 1 | tf_op jit(solution)/shard_map/pallas_call | solution.py:77
  (89 shorter events, 18.2 us)
Async XLA Ops:
  1.5 1.1 copy-start.11
  4.4 29.2 %copy-start.20 = (bf16[1536,8]{0,1:T(8,128)(2,1)S(1)}, bf16[1536,8]{0,1:T(8,128)(2,1)}, u32[]{:S(2)}) copy-start(bf16[1536,8]{0,1:T(8,128)(2,1)} %param.11) | copy-start | bytes 73732
  4.4 29.4 %copy-start.15 = (s32[4]{0:T(128)S(1)}, s32[4]{0:T(128)}, u32[]{:S(2)}) copy-start(s32[4]{0:T(128)} %constant.72.clone) | copy-start | bytes 52
  4.4 30.2 %copy-start.12 = (bf16[256,1536]{1,0:T(8,128)(2,1)S(1)}, bf16[256,1536]{1,0:T(8,128)(2,1)}, u32[]{:S(2)}) copy-start(bf16[256,1536]{1,0:T(8,128)(2,1)} %src_ref.2) | copy-start | bytes 2359300
  4.4 44.3 %all-to-all-start = ((bf16[8,64,1536]{2,1,0:T(8,128)(2,1)}), bf16[8,64,1536]{2,1,0:T(8,128)(2,1)S(1)}, u32[]{:S(2)}, u32[]{:S(2)}) async-start(bf16[8,64,1536]{2,1,0:T(8,128)(2,1)} %bitcast.3), calls=%async_computation | async-start | bytes 3145728 | tf_op jit(solution)/shard_map/all_to_all | solution.py:362
  10.9 20.7 %collective-permute-start.1 = (bf16[384,1024]{1,0:T(8,128)(2,1)}, bf16[384,1024]{1,0:T(8,128)(2,1)}, u32[]{:S(2)}, u32[]{:S(2)}) collective-permute-start(bf16[384,1024]{1,0:T(8,128)(2,1)} %bitcast.5.refs_0_.refs_5_), channel_id=1, source_target_pairs={{0,16},{8,0},{16,24},{24,8},{1,17},{9,1},{17,25},{25,9},{2,18},{10... | collective-permute-start | bytes 2359304 | tf_op jit(solution)/shard_map/ppermute | solution.py:102
  12.4 20.7 %collective-permute-start.3 = (bf16[384,1024]{1,0:T(8,128)(2,1)}, bf16[384,1024]{1,0:T(8,128)(2,1)}, u32[]{:S(2)}, u32[]{:S(2)}) collective-permute-start(bf16[384,1024]{1,0:T(8,128)(2,1)} %bitcast.6.refs_4_.refs_9_), channel_id=1, source_target_pairs={{0,8},{8,24},{16,0},{24,16},{1,9},{9,25},{17,1},{25,17},{2,10},{10... | collective-permute-start | bytes 2359304 | tf_op jit(solution)/shard_map/ppermute | solution.py:102
  12.9 39.4 %collective-permute-start.5 = (bf16[384,1024]{1,0:T(8,128)(2,1)}, bf16[384,1024]{1,0:T(8,128)(2,1)}, u32[]{:S(2)}, u32[]{:S(2)}) collective-permute-start(bf16[384,1024]{1,0:T(8,128)(2,1)} %bitcast.6.refs_4_.refs_9_), channel_id=1, source_target_pairs={{0,16},{8,0},{16,24},{24,8},{1,17},{9,1},{17,25},{25,9},{2,18},{10... | collective-permute-start | bytes 2359304 | tf_op jit(solution)/shard_map/ppermute | solution.py:102
  14.4 37.9 %collective-permute-start = (bf16[384,1024]{1,0:T(8,128)(2,1)}, bf16[384,1024]{1,0:T(8,128)(2,1)}, u32[]{:S(2)}, u32[]{:S(2)}) collective-permute-start(bf16[384,1024]{1,0:T(8,128)(2,1)} %bitcast.5.refs_0_.refs_5_), channel_id=1, source_target_pairs={{0,8},{8,24},{16,0},{24,16},{1,9},{9,25},{17,1},{25,17},{2,10},{10... | collective-permute-start | bytes 2359304 | tf_op jit(solution)/shard_map/ppermute | solution.py:102
  31.5 33.7 %collective-permute-start.2 = (bf16[384,1024]{1,0:T(8,128)(2,1)}, bf16[384,1024]{1,0:T(8,128)(2,1)}, u32[]{:S(2)}, u32[]{:S(2)}) collective-permute-start(bf16[384,1024]{1,0:T(8,128)(2,1)} %collective-permute-done.1.refs_3_.refs_8_), channel_id=1, source_target_pairs={{0,16},{8,0},{16,24},{24,8},{1,17},{9,1},{17,25},{25,9},{2,18},{10... | collective-permute-start | bytes 2359304 | tf_op jit(solution)/shard_map/ppermute | solution.py:102
  33.1 33.7 %collective-permute-start.4 = (bf16[384,1024]{1,0:T(8,128)(2,1)}, bf16[384,1024]{1,0:T(8,128)(2,1)}, u32[]{:S(2)}, u32[]{:S(2)}) collective-permute-start(bf16[384,1024]{1,0:T(8,128)(2,1)} %collective-permute-done.3.refs_5_.refs_10_), channel_id=1, source_target_pairs={{0,8},{8,24},{16,0},{24,16},{1,9},{9,25},{17,1},{25,17},{2,10},{10... | collective-permute-start | bytes 2359304 | tf_op jit(solution)/shard_map/ppermute | solution.py:102
  34.6 32.2 %copy-start.14 = (s32[5]{0:T(128)}, s32[5]{0:T(128)S(1)}, u32[]{:S(2)}) copy-start(s32[5]{0:T(128)S(1)} %pad_add_fusion.ids.refs_0_) | copy-start | bytes 64
  35.2 1.1 copy-start.2
  48.7 41.3 %all-to-all-start.1 = ((bf16[8,64,1536]{2,1,0:T(8,128)(2,1)}), bf16[8,64,1536]{2,1,0:T(8,128)(2,1)S(1)}, u32[]{:S(2)}, u32[]{:S(2)}) async-start(bf16[8,64,1536]{2,1,0:T(8,128)(2,1)} %bitcast.30), calls=%async_computation.1 | async-start | bytes 3145728 | tf_op jit(solution)/shard_map/all_to_all | solution.py:362
  52.3 30.5 %collective-permute-start.6 = (bf16[256,1536]{1,0:T(8,128)(2,1)}, bf16[256,1536]{1,0:T(8,128)(2,1)S(1)}, u32[]{:S(2)}, u32[]{:S(2)}) collective-permute-start(bf16[256,1536]{1,0:T(8,128)(2,1)} %bitcast.32), channel_id=1, source_target_pairs={{0,8},{8,24},{16,0},{24,16},{1,9},{9,25},{17,1},{25,17},{2,10},{10... | collective-permute-start | bytes 2359304 | tf_op jit(solution)/shard_map/ppermute | solution.py:102
  53.9 28.9 %collective-permute-start.7 = (bf16[256,1536]{1,0:T(8,128)(2,1)}, bf16[256,1536]{1,0:T(8,128)(2,1)S(1)}, u32[]{:S(2)}, u32[]{:S(2)}) collective-permute-start(bf16[256,1536]{1,0:T(8,128)(2,1)} %bitcast.33), channel_id=1, source_target_pairs={{0,16},{8,0},{16,24},{24,8},{1,17},{9,1},{17,25},{25,9},{2,18},{10... | collective-permute-start | bytes 2359304 | tf_op jit(solution)/shard_map/ppermute | solution.py:102
  76.4 1.0 copy-start.4
  78.2 1.0 copy-start.8
  79.2 1.0 copy-start.9
  80.1 1.0 copy-start.10
  81.1 3.8 %copy-start.3 = (bf16[4,384,512]{2,1,0:T(8,128)(2,1)}, bf16[4,384,512]{2,1,0:T(8,128)(2,1)S(1)}, u32[]{:S(2)}) copy-start(bf16[4,384,512]{2,1,0:T(8,128)(2,1)S(1)} %get-tuple-element.76.refs_3_) | copy-start | bytes 4718596
  82.8 2.1 %copy-start.16 = (bf16[256,1536]{1,0:T(8,128)(2,1)}, bf16[256,1536]{1,0:T(8,128)(2,1)S(1)}, u32[]{:S(2)}) copy-start(bf16[256,1536]{1,0:T(8,128)(2,1)S(1)} %collective-permute-done.6.refs_4_.refs_5_) | copy-start | bytes 2359300
  82.8 2.1 %copy-start.17 = (bf16[256,1536]{1,0:T(8,128)(2,1)}, bf16[256,1536]{1,0:T(8,128)(2,1)S(1)}, u32[]{:S(2)}) copy-start(bf16[256,1536]{1,0:T(8,128)(2,1)S(1)} %collective-permute-done.7.refs_6_.refs_7_) | copy-start | bytes 2359300
  84.4 13.3 %collective-permute-start.9 = (bf16[128,1536]{1,0:T(8,128)(2,1)}, bf16[128,1536]{1,0:T(8,128)(2,1)S(1)}, u32[]{:S(2)}, u32[]{:S(2)}) collective-permute-start(bf16[128,1536]{1,0:T(8,128)(2,1)} %slice.7), channel_id=1, source_target_pairs={{0,8},{8,24},{16,0},{24,16},{1,9},{9,25},{17,1},{25,17},{2,10},{10... | collective-permute-start | bytes 1179656 | tf_op jit(solution)/shard_map/ppermute | solution.py:102
  85.0 12.8 %collective-permute-start.8 = (bf16[128,1536]{1,0:T(8,128)(2,1)}, bf16[128,1536]{1,0:T(8,128)(2,1)}, u32[]{:S(2)}, u32[]{:S(2)}) collective-permute-start(bf16[128,1536]{1,0:T(8,128)(2,1)} %slice.6), channel_id=1, source_target_pairs={{0,16},{8,0},{16,24},{24,8},{1,17},{9,1},{17,25},{25,9},{2,18},{10... | collective-permute-start | bytes 1179656 | tf_op jit(solution)/shard_map/ppermute | solution.py:102
  90.1 1.1 copy-start
  95.7 17.9 %collective-permute-start.10 = (bf16[128,1536]{1,0:T(8,128)(2,1)}, bf16[128,1536]{1,0:T(8,128)(2,1)}, u32[]{:S(2)}, u32[]{:S(2)}) collective-permute-start(bf16[128,1536]{1,0:T(8,128)(2,1)} %get-tuple-element.64), channel_id=1, source_target_pairs={{0,16},{8,0},{16,24},{24,8},{1,17},{9,1},{17,25},{25,9},{2,18},{10... | collective-permute-start | bytes 1179656 | tf_op jit(solution)/shard_map/ppermute | solution.py:102
  97.3 16.4 %collective-permute-start.11 = (bf16[128,1536]{1,0:T(8,128)(2,1)}, bf16[128,1536]{1,0:T(8,128)(2,1)}, u32[]{:S(2)}, u32[]{:S(2)}) collective-permute-start(bf16[128,1536]{1,0:T(8,128)(2,1)} %get-tuple-element.65), channel_id=1, source_target_pairs={{0,8},{8,24},{16,0},{24,16},{1,9},{9,25},{17,1},{25,17},{2,10},{10... | collective-permute-start | bytes 1179656 | tf_op jit(solution)/shard_map/ppermute | solution.py:102
  97.8 0.8 copy-start.18
  105.0 44.4 %all-to-all-start.2 = ((bf16[8,64,1536]{2,1,0:T(8,128)(2,1)}), bf16[8,64,1536]{2,1,0:T(8,128)(2,1)S(1)}, u32[]{:S(2)}, u32[]{:S(2)}) async-start(bf16[8,64,1536]{2,1,0:T(8,128)(2,1)} %bitcast.36), calls=%async_computation.2 | async-start | bytes 3145728 | tf_op jit(solution)/shard_map/all_to_all | solution.py:362
  116.6 20.2 %collective-permute-start.13 = (bf16[256,1536]{1,0:T(8,128)(2,1)}, bf16[256,1536]{1,0:T(8,128)(2,1)}, u32[]{:S(2)}, u32[]{:S(2)}) collective-permute-start(bf16[256,1536]{1,0:T(8,128)(2,1)} %get-tuple-element.70), channel_id=1, source_target_pairs={{0,8},{8,24},{16,0},{24,16},{1,9},{9,25},{17,1},{25,17},{2,10},{10... | collective-permute-start | bytes 2359304 | tf_op jit(solution)/shard_map/ppermute | solution.py:102
  118.2 19.9 %collective-permute-start.12 = (bf16[256,1536]{1,0:T(8,128)(2,1)}, bf16[256,1536]{1,0:T(8,128)(2,1)}, u32[]{:S(2)}, u32[]{:S(2)}) collective-permute-start(bf16[256,1536]{1,0:T(8,128)(2,1)} %get-tuple-element.69), channel_id=1, source_target_pairs={{0,16},{8,0},{16,24},{24,8},{1,17},{9,1},{17,25},{25,9},{2,18},{10... | collective-permute-start | bytes 2359304 | tf_op jit(solution)/shard_map/ppermute | solution.py:102
  128.2 4.6 %copy-start.1 = (bf16[8,64,1536]{2,1,0:T(8,128)(2,1)S(1)}, bf16[8,64,1536]{2,1,0:T(8,128)(2,1)}, u32[]{:S(2)}) copy-start(bf16[8,64,1536]{2,1,0:T(8,128)(2,1)} %copy-done) | copy-start | bytes 4718596
  128.2 4.6 %copy-start.6 = (f32[512,1]{1,0:T(8,128)S(1)}, f32[512,1]{1,0:T(8,128)}, u32[]{:S(2)}) copy-start(f32[512,1]{1,0:T(8,128)} %copy-done.5) | copy-start | bytes 6148
  132.8 1.4 copy-start.7
  138.1 22.7 %collective-permute-start.14 = (bf16[384,1024]{1,0:T(8,128)(2,1)}, bf16[384,1024]{1,0:T(8,128)(2,1)}, u32[]{:S(2)}, u32[]{:S(2)}) collective-permute-start(bf16[384,1024]{1,0:T(8,128)(2,1)} %get-tuple-element.85), channel_id=1, source_target_pairs={{0,16},{8,0},{16,24},{24,8},{1,17},{9,1},{17,25},{25,9},{2,18},{10... | collective-permute-start | bytes 2359304 | tf_op jit(solution)/shard_map/ppermute | solution.py:102
  138.6 22.2 %collective-permute-start.15 = (bf16[384,1024]{1,0:T(8,128)(2,1)}, bf16[384,1024]{1,0:T(8,128)(2,1)}, u32[]{:S(2)}, u32[]{:S(2)}) collective-permute-start(bf16[384,1024]{1,0:T(8,128)(2,1)} %get-tuple-element.89), channel_id=1, source_target_pairs={{0,8},{8,24},{16,0},{24,16},{1,9},{9,25},{17,1},{25,17},{2,10},{10... | collective-permute-start | bytes 2359304 | tf_op jit(solution)/shard_map/ppermute | solution.py:102
  149.4 42.6 %all-to-all-start.3 = ((bf16[8,64,1536]{2,1,0:T(8,128)(2,1)}), bf16[8,64,1536]{2,1,0:T(8,128)(2,1)S(1)}, u32[]{:S(2)}, u32[]{:S(2)}) async-start(bf16[8,64,1536]{2,1,0:T(8,128)(2,1)} %bitcast.31), calls=%async_computation.3 | async-start | bytes 3145728 | tf_op jit(solution)/shard_map/all_to_all | solution.py:362
  160.8 6.0 %copy-start.19 = (bf16[256,1536]{1,0:T(8,128)(2,1)S(1)}, bf16[256,1536]{1,0:T(8,128)(2,1)}, u32[]{:S(2)}) copy-start(bf16[256,1536]{1,0:T(8,128)(2,1)} %get-tuple-element.95) | copy-start | bytes 2359300
  164.7 39.6 %collective-permute-start.16 = (bf16[2,384,1024]{2,1,0:T(8,128)(2,1)}, bf16[2,384,1024]{2,1,0:T(8,128)(2,1)}, u32[]{:S(2)}, u32[]{:S(2)}) collective-permute-start(bf16[2,384,1024]{2,1,0:T(8,128)(2,1)} %get-tuple-element.91), channel_id=1, source_target_pairs={{0,16},{8,0},{16,24},{24,8},{1,17},{9,1},{17,25},{25,9},{2,18},{10... | collective-permute-start | bytes 4718600 | tf_op jit(solution)/shard_map/ppermute | solution.py:102
  165.3 39.0 %collective-permute-start.17 = (bf16[2,384,1024]{2,1,0:T(8,128)(2,1)}, bf16[2,384,1024]{2,1,0:T(8,128)(2,1)}, u32[]{:S(2)}, u32[]{:S(2)}) collective-permute-start(bf16[2,384,1024]{2,1,0:T(8,128)(2,1)} %get-tuple-element.92), channel_id=1, source_target_pairs={{0,8},{8,24},{16,0},{24,16},{1,9},{9,25},{17,1},{25,17},{2,10},{10... | collective-permute-start | bytes 4718600 | tf_op jit(solution)/shard_map/ppermute | solution.py:102
  193.4 1.2 collective-permute-start.18
  194.6 5.6 %collective-permute-start.21 = (f32[2,1536]{1,0:T(2,128)S(1)}, f32[2,1536]{1,0:T(2,128)S(1)}, u32[]{:S(2)}, u32[]{:S(2)}) collective-permute-start(f32[2,1536]{1,0:T(2,128)S(1)} %pad_maximum_fusion), channel_id=1, source_target_pairs={{0,6},{1,7},{2,4},{3,5},{4,2},{5,3},{6,0},{7,1},{8,14},{9,15},{10,... | collective-permute-start | bytes 36872 | tf_op jit(solution)/shard_map/ppermute | solution.py:102
  195.9 4.6 %collective-permute-start.20 = (f32[2,1536]{1,0:T(2,128)S(1)}, f32[2,1536]{1,0:T(2,128)S(1)}, u32[]{:S(2)}, u32[]{:S(2)}) collective-permute-start(f32[2,1536]{1,0:T(2,128)S(1)} %pad_maximum_fusion), channel_id=1, source_target_pairs={{0,4},{1,5},{2,6},{3,7},{4,0},{5,1},{6,2},{7,3},{8,12},{9,13},{10,... | collective-permute-start | bytes 36872 | tf_op jit(solution)/shard_map/ppermute | solution.py:102
  195.9 4.8 %collective-permute-start.19 = (f32[2,1536]{1,0:T(2,128)S(1)}, f32[2,1536]{1,0:T(2,128)S(1)}, u32[]{:S(2)}, u32[]{:S(2)}) collective-permute-start(f32[2,1536]{1,0:T(2,128)S(1)} %pad_maximum_fusion), channel_id=1, source_target_pairs={{0,2},{1,3},{2,0},{3,1},{4,6},{5,7},{6,4},{7,5},{8,10},{9,11},{10,... | collective-permute-start | bytes 36872 | tf_op jit(solution)/shard_map/ppermute | solution.py:102
  200.8 7.9 %collective-permute-start.24 = (f32[8,1536]{1,0:T(8,128)S(1)}, f32[8,1536]{1,0:T(8,128)S(1)}, u32[]{:S(2)}, u32[]{:S(2)}) collective-permute-start(f32[8,1536]{1,0:T(8,128)S(1)} %concatenate.12), channel_id=1, source_target_pairs={{0,24},{8,16},{16,8},{24,0},{1,25},{9,17},{17,9},{25,1},{2,26},{10... | collective-permute-start | bytes 147464 | tf_op jit(solution)/shard_map/ppermute | solution.py:102
  202.3 6.4 %collective-permute-start.23 = (f32[8,1536]{1,0:T(8,128)S(1)}, f32[8,1536]{1,0:T(8,128)S(1)}, u32[]{:S(2)}, u32[]{:S(2)}) collective-permute-start(f32[8,1536]{1,0:T(8,128)S(1)} %concatenate.12), channel_id=1, source_target_pairs={{0,16},{8,24},{16,0},{24,8},{1,17},{9,25},{17,1},{25,9},{2,18},{10... | collective-permute-start | bytes 147464 | tf_op jit(solution)/shard_map/ppermute | solution.py:102
  203.8 4.9 %collective-permute-start.22 = (f32[8,1536]{1,0:T(8,128)S(1)}, f32[8,1536]{1,0:T(8,128)S(1)}, u32[]{:S(2)}, u32[]{:S(2)}) collective-permute-start(f32[8,1536]{1,0:T(8,128)S(1)} %concatenate.12), channel_id=1, source_target_pairs={{0,8},{8,0},{16,24},{24,16},{1,9},{9,1},{17,25},{25,17},{2,10},{10... | collective-permute-start | bytes 147464 | tf_op jit(solution)/shard_map/ppermute | solution.py:102
  (2 other events, 1.4 us)

commit v3 on v2

--- a/solution.py
+++ b/solution.py
@@ -212,13 +212,13 @@
     get_hd = copies.load(hd_hbm, hd)
     gets = load_downs(copies, n, pieces, w)
     get_hd()
-    for get in gets:
-        get()
     rows = hd.shape[0] // 2
     for h in range(2):
         part = slice(h * rows, (h + 1) * rows)
+        gets[0]()
         total = dot(hd[part, chunk_of(ids, 0, width)], w[0])
         for s in range(1, n):
+            gets[s]()
             total = total + dot(hd[part, chunk_of(ids, s, width)], w[s])
         total = total.astype(BF16)
         o[part, :] = total

time: 211 us -> 210 us (level)
  no operation moved by 1% of the time
where the time goes in v3:
time: 210 us
  waiting for transfers between devices  72.7 us (35%)
  Pallas kernels  71.1 us (34%)
  starting transfers between devices  44.9 us (21%)
  local copies, waits for them, and re-layouts  15.5 us (7%)
  other arithmetic  4.42 us (2%)
    pallas_call x10, Pallas kernels, streamed(): pl.pallas_call(run, out_shape=list(outs), in_specs=[SMEM] * scalars + [VM...  55.4 us
    all_to_all x4, waiting for transfers between devices, exchange(): lax.all_to_all(x.reshape(experts, part, model), 'expert', split_axis=0, c...  36.8 us
    ppermute x25, waiting for transfers between devices, hop(): return lax.ppermute(x, axis, [(i, target(i)) for i in range(size)])  35.9 us
    ppermute x25, starting transfers between devices, hop(): return lax.ppermute(x, axis, [(i, target(i)) for i in range(size)])  26.5 us
    all_to_all x4, starting transfers between devices, exchange(): lax.all_to_all(x.reshape(experts, part, model), 'expert', split_axis=0, c...  18.4 us
    pallas_call x6, Pallas kernels, call(): pl.pallas_call(kernel, out_shape=list(outs), in_specs=[SMEM] * scalars +...  15.7 us
    unnamed x43, local copies, waits for them, and re-layouts  11.2 us
  transfers between devices with their start and end apart: 29, of which 13 were waited for; matrix products, arithmetic and copies ran while one was open for 3% of the time, Pallas kernels for 33%

profile of v3, /device:TPU:0, one launch (start us, length us, event | category | flops | bytes accessed | tf_op | source)
XLA Modules:
  0.0 209.7 jit_solution(15629093291030761162)
XLA Ops:
  1.5 1.1 copy-done.11
  2.7 1.8 shard_map.127
  4.4 6.4 %all-to-all-start = ((bf16[8,64,1536]{2,1,0:T(8,128)(2,1)}), bf16[8,64,1536]{2,1,0:T(8,128)(2,1)S(1)}, u32[]{:S(2)}, u32[]{:S(2)}) async-start(bf16[8,64,1536]{2,1,0:T(8,128)(2,1)} %bitcast.3), calls=%async_computation | async-start | bytes 3145728 | tf_op jit(solution)/shard_map/all_to_all | solution.py:362
  10.9 1.5 collective-permute-start.1
  12.9 1.5 collective-permute-start.5
  14.9 16.6 %collective-permute-done.1.refs_3_.refs_8_ = bf16[384,1024]{1,0:T(8,128)(2,1)} collective-permute-done((bf16[384,1024]{1,0:T(8,128)(2,1)}, bf16[384,1024]{1,0:T(8,128)(2,1)}, u32[]{:S(2)}, u32[]{:S(2)}) %collective-permute-start.1) | collective-permute-done | bytes 786464 | tf_op jit(solution)/shard_map/ppermute | solution.py:102
  31.5 1.5 collective-permute-start.2
  35.2 1.1 copy-done.2
  36.4 12.4 %all-to-all-done = bf16[8,64,1536]{2,1,0:T(8,128)(2,1)S(1)} async-done(((bf16[8,64,1536]{2,1,0:T(8,128)(2,1)}), bf16[8,64,1536]{2,1,0:T(8,128)(2,1)S(1)}, u32[]{:S(2)}, u32[]{:S(2)}) %all-to-all-start) | async-done | bytes 1572896 | tf_op jit(solution)/shard_map/all_to_all | solution.py:362
  48.7 3.6 %all-to-all-start.1 = ((bf16[8,64,1536]{2,1,0:T(8,128)(2,1)}), bf16[8,64,1536]{2,1,0:T(8,128)(2,1)S(1)}, u32[]{:S(2)}, u32[]{:S(2)}) async-start(bf16[8,64,1536]{2,1,0:T(8,128)(2,1)} %bitcast.30), calls=%async_computation.1 | async-start | bytes 3145728 | tf_op jit(solution)/shard_map/all_to_all | solution.py:362
  52.3 1.6 collective-permute-start.6
  54.4 10.8 %collective-permute-done.2.refs_2_.refs_7_ = bf16[384,1024]{1,0:T(8,128)(2,1)} collective-permute-done((bf16[384,1024]{1,0:T(8,128)(2,1)}, bf16[384,1024]{1,0:T(8,128)(2,1)}, u32[]{:S(2)}, u32[]{:S(2)}) %collective-permute-start.2) | collective-permute-done | bytes 786464 | tf_op jit(solution)/shard_map/ppermute | solution.py:102
  65.2 1.6 collective-permute-done.4.refs_6_.refs_11_
  66.8 9.6 %shard_map.128 = (bf16[4,384,512]{2,1,0:T(8,128)(2,1)S(1)}, bf16[512,1024]{1,0:T(8,128)(2,1)S(1)}, bf16[1024,512]{1,0:T(8,128)(2,1)S(1)}, bf16[512,1024]{1,0:T(8...) custom-call(s32[5]{0:T(128)S(1)} %pad_add_fusion.ids.refs_0_, bf16[512,1536]{1,0:T(8,128)(2,1)S(1)} %bitcast.26, ...), custom_call_target="tpu_custom_call" | custom-call | flops 30000001024 | bytes 1 | tf_op jit(solution)/shard_map/pallas_call | solution.py:25
  81.1 1.7 collective-permute-done.6.refs_4_.refs_5_
  85.0 1.6 collective-permute-start.8
  86.5 3.5 %all-to-all-done.1 = bf16[8,64,1536]{2,1,0:T(8,128)(2,1)S(1)} async-done(((bf16[8,64,1536]{2,1,0:T(8,128)(2,1)}), bf16[8,64,1536]{2,1,0:T(8,128)(2,1)S(1)}, u32[]{:S(2)}, u32[]{:S(2)}) %all-to-all-start.1) | async-done | bytes 1572896 | tf_op jit(solution)/shard_map/all_to_all | solution.py:362
  90.1 1.1 copy-done
  91.2 4.5 %shard_map.130 = (bf16[512,1536]{1,0:T(8,128)(2,1)}, bf16[128,1536]{1,0:T(8,128)(2,1)}, bf16[128,1536]{1,0:T(8,128)(2,1)}) custom-call(s32[5]{0:T(128)} %copy-done.14, f32[512,1]{1,0:T(8,128)} %copy-done.5, bf16[512,1536]{1,0:T(8,128)(2,1)} %bitcast.24, bf16[1024,512]{1,0:T(8,128)(2,1)} %copy-done.4), custom_call_target="tpu_custom_call" | custom-call | flops 1 | bytes 1 | tf_op jit(solution)/shard_map/pallas_call | solution.py:77
  95.7 1.6 collective-permute-start.10
  98.5 6.0 %shard_map.131 = (bf16[512,1536]{1,0:T(8,128)(2,1)}, bf16[512,1536]{1,0:T(8,128)(2,1)}) custom-call(s32[5]{0:T(128)} %copy-done.14, f32[512,1]{1,0:T(8,128)} %copy-done.5, bf16[512,1024]{1,0:T(8,128)(2,1)} %copy-done.8, bf16[256,1536]{1,0:T(8,128)(2,1)} %bitcast.34, bf16[256,1536]{1,0:T(8,128)(2,1)} %copy-done.16, ...), custom_call_target="tpu_custom_call" | custom-call | flops 1 | bytes 1 | tf_op jit(solution)/shard_map/pallas_call | solution.py:77
  104.6 3.6 %all-to-all-start.2 = ((bf16[8,64,1536]{2,1,0:T(8,128)(2,1)}), bf16[8,64,1536]{2,1,0:T(8,128)(2,1)S(1)}, u32[]{:S(2)}, u32[]{:S(2)}) async-start(bf16[8,64,1536]{2,1,0:T(8,128)(2,1)} %bitcast.36), calls=%async_computation.2 | async-start | bytes 3145728 | tf_op jit(solution)/shard_map/all_to_all | solution.py:362
  108.2 5.1 %shard_map.133 = (bf16[256,1536]{1,0:T(8,128)(2,1)}, bf16[256,1536]{1,0:T(8,128)(2,1)}, bf16[256,1536]{1,0:T(8,128)(2,1)}) custom-call(s32[5]{0:T(128)} %copy-done.14, bf16[512,1536]{1,0:T(8,128)(2,1)} %get-tuple-element.71.refs_1_, bf16[1024,512]{1,0:T(8,128)(2,1)} %copy-done.4), custom_call_target="tpu_custom_call" | custom-call | flops 1 | bytes 1 | tf_op jit(solution)/shard_map/pallas_call | solution.py:77
  113.3 3.0 %shard_map.134 = (bf16[256,1536]{1,0:T(8,128)(2,1)}, bf16[256,1536]{1,0:T(8,128)(2,1)}) custom-call(bf16[128,1536]{1,0:T(8,128)(2,1)} %collective-permute-done.10.refs_0_, bf16[128,1536]{1,0:T(8,128)(2,1)} %collective-permute-done.11.refs_1_, bf16[256,1536]{1,0:T(8,128)(2,1)} %get-tuple-element.67.refs_2_, bf16[256,1536]{1,0:T(8,128)(2,1)} %get-tuple-element.68.refs_3_), custom_call_target="tpu_custom_call" | custom-call | flops 24999999488 | bytes 1 | tf_op jit(solution)/shard_map/pallas_call | solution.py:77
  116.3 1.6 collective-permute-start.13
  118.3 1.3 constant_dynamic-slice_fusion
  119.7 8.2 %shard_map.135 = (bf16[512,1024]{1,0:T(8,128)(2,1)}, bf16[512,1024]{1,0:T(8,128)(2,1)}) custom-call(s32[5]{0:T(128)} %copy-done.14, bf16[512,1536]{1,0:T(8,128)(2,1)} %get-tuple-element.71.refs_1_, bf16[512,1024]{1,0:T(8,128)(2,1)} %copy-done.9, bf16[512,1024]{1,0:T(8,128)(2,1)} %copy-done.10, bf16[256,1536]{1,0:T(8,128)(2,1)} %bitcast.35, ...), custom_call_target="tpu_custom_call" | custom-call | flops 1 | bytes 1 | tf_op jit(solution)/shard_map/pallas_call | solution.py:77
  127.9 4.6 %shard_map.136 = (bf16[384,1024]{1,0:T(8,128)(2,1)}, bf16[384,1024]{1,0:T(8,128)(2,1)}) custom-call(s32[5]{0:T(128)} %copy-done.14, bf16[512,1024]{1,0:T(8,128)(2,1)} %get-tuple-element.81.refs_1_.refs_3_, bf16[512,1024]{1,0:T(8,128)(2,1)} %get-tuple-element.75.refs_2_.refs_4_, bf16[4,384,512]{2,1,0:T(8,128)(2,1)} %copy-done.3), custom_call_target="tpu_custom_call" | custom-call | flops 1 | bytes 1 | tf_op jit(solution)/shard_map/pallas_call | solution.py:77
  132.5 1.4 copy-done.7
  135.4 1.1 collective-permute-done.13
  136.5 1.2 collective-permute-done.12
  138.2 1.5 collective-permute-start.15
  139.8 9.2 %shard_map.138 = bf16[512,1536]{1,0:T(8,128)(2,1)} custom-call(s32[5]{0:T(128)} %copy-done.14, f32[512,1]{1,0:T(8,128)} %copy-done.13, bf16[4,1,384]{2,1,0:T(2,128)(2,1)} %bitcast.38, bf16[512,1024]{1,0:T(8,128)(2,1)} %get-tuple-element.81.refs_1_.refs_3_, bf16[512,1024]{1,0:T(8,128)(2,1)} %get-tuple-element.75.refs_2_.refs_4_, ...), custom_call_target="tpu_custom_call" | custom-call | flops 1 | bytes 1 | tf_op jit(solution)/shard_map/pallas_call | solution.py:77
  149.0 4.8 %all-to-all-start.3 = ((bf16[8,64,1536]{2,1,0:T(8,128)(2,1)}), bf16[8,64,1536]{2,1,0:T(8,128)(2,1)S(1)}, u32[]{:S(2)}, u32[]{:S(2)}) async-start(bf16[8,64,1536]{2,1,0:T(8,128)(2,1)} %bitcast.31), calls=%async_computation.3 | async-start | bytes 3145728 | tf_op jit(solution)/shard_map/all_to_all | solution.py:362
  153.8 6.6 %shard_map.140 = (bf16[384,1024]{1,0:T(8,128)(2,1)}, bf16[384,1024]{1,0:T(8,128)(2,1)}, bf16[384,1024]{1,0:T(8,128)(2,1)}, bf16[384,1024]{1,0:T(8,128)(2,1)}, bf...) custom-call(s32[5]{0:T(128)} %copy-done.14, bf16[512,1024]{1,0:T(8,128)(2,1)} %get-tuple-element.81.refs_1_.refs_3_, ...), custom_call_target="tpu_custom_call" | custom-call | flops 1 | bytes 1 | tf_op jit(solution)/shard_map/pallas_call | solution.py:77
  160.4 3.9 %shard_map.141 = (bf16[2,384,1024]{2,1,0:T(8,128)(2,1)}, bf16[2,384,1024]{2,1,0:T(8,128)(2,1)}) custom-call(bf16[384,1024]{1,0:T(8,128)(2,1)} %get-tuple-element.84.refs_0_, bf16[384,1024]{1,0:T(8,128)(2,1)} %collective-permute-done.14.refs_1_, bf16[384,1024]{1,0:T(8,128)(2,1)} %get-tuple-element.86.refs_2_, bf16[384,1024]{1,0:T(8,128)(2,1)} %get-tuple-element.87.refs_3_, ...), custom_call_target="tpu_custom_call" | custom-call | flops 16000000000 | bytes 1 | tf_op jit(solution)/shard_map/pallas_call | solution.py:77
  165.0 1.5 collective-permute-start.17
  166.5 2.8 %convert_add_fusion = f32[256,1536]{1,0:T(8,128)} fusion(bf16[256,1536]{1,0:T(8,128)(2,1)} %collective-permute-done.13, bf16[256,1536]{1,0:T(8,128)(2,1)} %collective-permute-done.12, bf16[256,1536]{1,0:T(8,128)(2,1)S(1)} %copy-done.19), kind=kLoop, calls=%fused_computation.2 | loop fusion | flops 1966080 | bytes 3932160 | tf_op jit(solution)/shard_map/add | solution.py:470
  169.2 1.5 shard_map.132
  170.7 20.9 %all-to-all-done.3 = bf16[8,64,1536]{2,1,0:T(8,128)(2,1)S(1)} async-done(((bf16[8,64,1536]{2,1,0:T(8,128)(2,1)}), bf16[8,64,1536]{2,1,0:T(8,128)(2,1)S(1)}, u32[]{:S(2)}, u32[]{:S(2)}) %all-to-all-start.3) | async-done | bytes 1572896 | tf_op jit(solution)/shard_map/all_to_all | solution.py:362
  191.6 1.5 shard_map.139
  193.1 1.2 collective-permute-done.18
  194.2 1.3 collective-permute-start.21
  195.6 3.1 %collective-permute-start.19 = (f32[2,1536]{1,0:T(2,128)S(1)}, f32[2,1536]{1,0:T(2,128)S(1)}, u32[]{:S(2)}, u32[]{:S(2)}) collective-permute-start(f32[2,1536]{1,0:T(2,128)S(1)} %pad_maximum_fusion), channel_id=1, source_target_pairs={{0,2},{1,3},{2,0},{3,1},{4,6},{5,7},{6,4},{7,5},{8,10},{9,11},{10,... | collective-permute-start | bytes 36872 | tf_op jit(solution)/shard_map/ppermute | solution.py:102
  198.7 1.1 collective-permute-done.21
  200.4 1.5 collective-permute-start.24
  202.0 1.5 collective-permute-start.23
  204.0 4.4 %shard_map.142 = (f32[384,1024]{1,0:T(8,128)}, f32[384,1024]{1,0:T(8,128)}) custom-call(bf16[384,1024]{1,0:T(8,128)(2,1)} %get-tuple-element.82.refs_0_, bf16[384,1024]{1,0:T(8,128)(2,1)} %get-tuple-element.83.refs_1_, bf16[2,384,1024]{2,1,0:T(8,128)(2,1)} %collective-permute-done.16.refs_2_, bf16[2,384,1024]{2,1,0:T(8,128)(2,1)} %collective-permute-done.17.refs_3_), custom_call_target="tpu_custom_call" | custom-call | flops 24999999488 | bytes 1 | tf_op jit(solution)/shard_map/pallas_call | solution.py:77
  (89 shorter events, 18.2 us)
Async XLA Ops:
  1.5 1.1 copy-start.11
  4.4 29.2 %copy-start.20 = (bf16[1536,8]{0,1:T(8,128)(2,1)S(1)}, bf16[1536,8]{0,1:T(8,128)(2,1)}, u32[]{:S(2)}) copy-start(bf16[1536,8]{0,1:T(8,128)(2,1)} %param.11) | copy-start | bytes 73732
  4.4 29.4 %copy-start.15 = (s32[4]{0:T(128)S(1)}, s32[4]{0:T(128)}, u32[]{:S(2)}) copy-start(s32[4]{0:T(128)} %constant.72.clone) | copy-start | bytes 52
  4.4 30.2 %copy-start.12 = (bf16[256,1536]{1,0:T(8,128)(2,1)S(1)}, bf16[256,1536]{1,0:T(8,128)(2,1)}, u32[]{:S(2)}) copy-start(bf16[256,1536]{1,0:T(8,128)(2,1)} %src_ref.2) | copy-start | bytes 2359300
  4.4 44.3 %all-to-all-start = ((bf16[8,64,1536]{2,1,0:T(8,128)(2,1)}), bf16[8,64,1536]{2,1,0:T(8,128)(2,1)S(1)}, u32[]{:S(2)}, u32[]{:S(2)}) async-start(bf16[8,64,1536]{2,1,0:T(8,128)(2,1)} %bitcast.3), calls=%async_computation | async-start | bytes 3145728 | tf_op jit(solution)/shard_map/all_to_all | solution.py:362
  10.9 20.7 %collective-permute-start.1 = (bf16[384,1024]{1,0:T(8,128)(2,1)}, bf16[384,1024]{1,0:T(8,128)(2,1)}, u32[]{:S(2)}, u32[]{:S(2)}) collective-permute-start(bf16[384,1024]{1,0:T(8,128)(2,1)} %bitcast.5.refs_0_.refs_5_), channel_id=1, source_target_pairs={{0,16},{8,0},{16,24},{24,8},{1,17},{9,1},{17,25},{25,9},{2,18},{10... | collective-permute-start | bytes 2359304 | tf_op jit(solution)/shard_map/ppermute | solution.py:102
  12.4 20.7 %collective-permute-start.3 = (bf16[384,1024]{1,0:T(8,128)(2,1)}, bf16[384,1024]{1,0:T(8,128)(2,1)}, u32[]{:S(2)}, u32[]{:S(2)}) collective-permute-start(bf16[384,1024]{1,0:T(8,128)(2,1)} %bitcast.6.refs_4_.refs_9_), channel_id=1, source_target_pairs={{0,8},{8,24},{16,0},{24,16},{1,9},{9,25},{17,1},{25,17},{2,10},{10... | collective-permute-start | bytes 2359304 | tf_op jit(solution)/shard_map/ppermute | solution.py:102
  12.9 39.4 %collective-permute-start.5 = (bf16[384,1024]{1,0:T(8,128)(2,1)}, bf16[384,1024]{1,0:T(8,128)(2,1)}, u32[]{:S(2)}, u32[]{:S(2)}) collective-permute-start(bf16[384,1024]{1,0:T(8,128)(2,1)} %bitcast.6.refs_4_.refs_9_), channel_id=1, source_target_pairs={{0,16},{8,0},{16,24},{24,8},{1,17},{9,1},{17,25},{25,9},{2,18},{10... | collective-permute-start | bytes 2359304 | tf_op jit(solution)/shard_map/ppermute | solution.py:102
  14.4 37.9 %collective-permute-start = (bf16[384,1024]{1,0:T(8,128)(2,1)}, bf16[384,1024]{1,0:T(8,128)(2,1)}, u32[]{:S(2)}, u32[]{:S(2)}) collective-permute-start(bf16[384,1024]{1,0:T(8,128)(2,1)} %bitcast.5.refs_0_.refs_5_), channel_id=1, source_target_pairs={{0,8},{8,24},{16,0},{24,16},{1,9},{9,25},{17,1},{25,17},{2,10},{10... | collective-permute-start | bytes 2359304 | tf_op jit(solution)/shard_map/ppermute | solution.py:102
  31.5 33.7 %collective-permute-start.2 = (bf16[384,1024]{1,0:T(8,128)(2,1)}, bf16[384,1024]{1,0:T(8,128)(2,1)}, u32[]{:S(2)}, u32[]{:S(2)}) collective-permute-start(bf16[384,1024]{1,0:T(8,128)(2,1)} %collective-permute-done.1.refs_3_.refs_8_), channel_id=1, source_target_pairs={{0,16},{8,0},{16,24},{24,8},{1,17},{9,1},{17,25},{25,9},{2,18},{10... | collective-permute-start | bytes 2359304 | tf_op jit(solution)/shard_map/ppermute | solution.py:102
  33.1 33.7 %collective-permute-start.4 = (bf16[384,1024]{1,0:T(8,128)(2,1)}, bf16[384,1024]{1,0:T(8,128)(2,1)}, u32[]{:S(2)}, u32[]{:S(2)}) collective-permute-start(bf16[384,1024]{1,0:T(8,128)(2,1)} %collective-permute-done.3.refs_5_.refs_10_), channel_id=1, source_target_pairs={{0,8},{8,24},{16,0},{24,16},{1,9},{9,25},{17,1},{25,17},{2,10},{10... | collective-permute-start | bytes 2359304 | tf_op jit(solution)/shard_map/ppermute | solution.py:102
  34.6 32.2 %copy-start.14 = (s32[5]{0:T(128)}, s32[5]{0:T(128)S(1)}, u32[]{:S(2)}) copy-start(s32[5]{0:T(128)S(1)} %pad_add_fusion.ids.refs_0_) | copy-start | bytes 64
  35.2 1.1 copy-start.2
  48.7 41.3 %all-to-all-start.1 = ((bf16[8,64,1536]{2,1,0:T(8,128)(2,1)}), bf16[8,64,1536]{2,1,0:T(8,128)(2,1)S(1)}, u32[]{:S(2)}, u32[]{:S(2)}) async-start(bf16[8,64,1536]{2,1,0:T(8,128)(2,1)} %bitcast.30), calls=%async_computation.1 | async-start | bytes 3145728 | tf_op jit(solution)/shard_map/all_to_all | solution.py:362
  52.3 30.5 %collective-permute-start.6 = (bf16[256,1536]{1,0:T(8,128)(2,1)}, bf16[256,1536]{1,0:T(8,128)(2,1)S(1)}, u32[]{:S(2)}, u32[]{:S(2)}) collective-permute-start(bf16[256,1536]{1,0:T(8,128)(2,1)} %bitcast.32), channel_id=1, source_target_pairs={{0,8},{8,24},{16,0},{24,16},{1,9},{9,25},{17,1},{25,17},{2,10},{10... | collective-permute-start | bytes 2359304 | tf_op jit(solution)/shard_map/ppermute | solution.py:102
  53.9 28.9 %collective-permute-start.7 = (bf16[256,1536]{1,0:T(8,128)(2,1)}, bf16[256,1536]{1,0:T(8,128)(2,1)S(1)}, u32[]{:S(2)}, u32[]{:S(2)}) collective-permute-start(bf16[256,1536]{1,0:T(8,128)(2,1)} %bitcast.33), channel_id=1, source_target_pairs={{0,16},{8,0},{16,24},{24,8},{1,17},{9,1},{17,25},{25,9},{2,18},{10... | collective-permute-start | bytes 2359304 | tf_op jit(solution)/shard_map/ppermute | solution.py:102
  76.4 1.0 copy-start.4
  78.2 1.0 copy-start.8
  79.2 1.0 copy-start.9
  80.1 1.0 copy-start.10
  81.1 3.8 %copy-start.3 = (bf16[4,384,512]{2,1,0:T(8,128)(2,1)}, bf16[4,384,512]{2,1,0:T(8,128)(2,1)S(1)}, u32[]{:S(2)}) copy-start(bf16[4,384,512]{2,1,0:T(8,128)(2,1)S(1)} %get-tuple-element.76.refs_3_) | copy-start | bytes 4718596
  82.8 2.1 %copy-start.16 = (bf16[256,1536]{1,0:T(8,128)(2,1)}, bf16[256,1536]{1,0:T(8,128)(2,1)S(1)}, u32[]{:S(2)}) copy-start(bf16[256,1536]{1,0:T(8,128)(2,1)S(1)} %collective-permute-done.6.refs_4_.refs_5_) | copy-start | bytes 2359300
  82.8 2.1 %copy-start.17 = (bf16[256,1536]{1,0:T(8,128)(2,1)}, bf16[256,1536]{1,0:T(8,128)(2,1)S(1)}, u32[]{:S(2)}) copy-start(bf16[256,1536]{1,0:T(8,128)(2,1)S(1)} %collective-permute-done.7.refs_6_.refs_7_) | copy-start | bytes 2359300
  84.4 13.3 %collective-permute-start.9 = (bf16[128,1536]{1,0:T(8,128)(2,1)}, bf16[128,1536]{1,0:T(8,128)(2,1)S(1)}, u32[]{:S(2)}, u32[]{:S(2)}) collective-permute-start(bf16[128,1536]{1,0:T(8,128)(2,1)} %slice.7), channel_id=1, source_target_pairs={{0,8},{8,24},{16,0},{24,16},{1,9},{9,25},{17,1},{25,17},{2,10},{10... | collective-permute-start | bytes 1179656 | tf_op jit(solution)/shard_map/ppermute | solution.py:102
  85.0 12.8 %collective-permute-start.8 = (bf16[128,1536]{1,0:T(8,128)(2,1)}, bf16[128,1536]{1,0:T(8,128)(2,1)}, u32[]{:S(2)}, u32[]{:S(2)}) collective-permute-start(bf16[128,1536]{1,0:T(8,128)(2,1)} %slice.6), channel_id=1, source_target_pairs={{0,16},{8,0},{16,24},{24,8},{1,17},{9,1},{17,25},{25,9},{2,18},{10... | collective-permute-start | bytes 1179656 | tf_op jit(solution)/shard_map/ppermute | solution.py:102
  90.1 1.1 copy-start
  95.7 17.6 %collective-permute-start.10 = (bf16[128,1536]{1,0:T(8,128)(2,1)}, bf16[128,1536]{1,0:T(8,128)(2,1)}, u32[]{:S(2)}, u32[]{:S(2)}) collective-permute-start(bf16[128,1536]{1,0:T(8,128)(2,1)} %get-tuple-element.64), channel_id=1, source_target_pairs={{0,16},{8,0},{16,24},{24,8},{1,17},{9,1},{17,25},{25,9},{2,18},{10... | collective-permute-start | bytes 1179656 | tf_op jit(solution)/shard_map/ppermute | solution.py:102
  97.3 16.0 %collective-permute-start.11 = (bf16[128,1536]{1,0:T(8,128)(2,1)}, bf16[128,1536]{1,0:T(8,128)(2,1)}, u32[]{:S(2)}, u32[]{:S(2)}) collective-permute-start(bf16[128,1536]{1,0:T(8,128)(2,1)} %get-tuple-element.65), channel_id=1, source_target_pairs={{0,8},{8,24},{16,0},{24,16},{1,9},{9,25},{17,1},{25,17},{2,10},{10... | collective-permute-start | bytes 1179656 | tf_op jit(solution)/shard_map/ppermute | solution.py:102
  97.8 0.8 copy-start.18
  104.6 44.4 %all-to-all-start.2 = ((bf16[8,64,1536]{2,1,0:T(8,128)(2,1)}), bf16[8,64,1536]{2,1,0:T(8,128)(2,1)S(1)}, u32[]{:S(2)}, u32[]{:S(2)}) async-start(bf16[8,64,1536]{2,1,0:T(8,128)(2,1)} %bitcast.36), calls=%async_computation.2 | async-start | bytes 3145728 | tf_op jit(solution)/shard_map/all_to_all | solution.py:362
  116.3 20.2 %collective-permute-start.13 = (bf16[256,1536]{1,0:T(8,128)(2,1)}, bf16[256,1536]{1,0:T(8,128)(2,1)}, u32[]{:S(2)}, u32[]{:S(2)}) collective-permute-start(bf16[256,1536]{1,0:T(8,128)(2,1)} %get-tuple-element.70), channel_id=1, source_target_pairs={{0,8},{8,24},{16,0},{24,16},{1,9},{9,25},{17,1},{25,17},{2,10},{10... | collective-permute-start | bytes 2359304 | tf_op jit(solution)/shard_map/ppermute | solution.py:102
  117.8 19.9 %collective-permute-start.12 = (bf16[256,1536]{1,0:T(8,128)(2,1)}, bf16[256,1536]{1,0:T(8,128)(2,1)}, u32[]{:S(2)}, u32[]{:S(2)}) collective-permute-start(bf16[256,1536]{1,0:T(8,128)(2,1)} %get-tuple-element.69), channel_id=1, source_target_pairs={{0,16},{8,0},{16,24},{24,8},{1,17},{9,1},{17,25},{25,9},{2,18},{10... | collective-permute-start | bytes 2359304 | tf_op jit(solution)/shard_map/ppermute | solution.py:102
  127.8 4.6 %copy-start.1 = (bf16[8,64,1536]{2,1,0:T(8,128)(2,1)S(1)}, bf16[8,64,1536]{2,1,0:T(8,128)(2,1)}, u32[]{:S(2)}) copy-start(bf16[8,64,1536]{2,1,0:T(8,128)(2,1)} %copy-done) | copy-start | bytes 4718596
  127.9 4.6 %copy-start.6 = (f32[512,1]{1,0:T(8,128)S(1)}, f32[512,1]{1,0:T(8,128)}, u32[]{:S(2)}) copy-start(f32[512,1]{1,0:T(8,128)} %copy-done.5) | copy-start | bytes 6148
  132.5 1.4 copy-start.7
  137.7 22.7 %collective-permute-start.14 = (bf16[384,1024]{1,0:T(8,128)(2,1)}, bf16[384,1024]{1,0:T(8,128)(2,1)}, u32[]{:S(2)}, u32[]{:S(2)}) collective-permute-start(bf16[384,1024]{1,0:T(8,128)(2,1)} %get-tuple-element.85), channel_id=1, source_target_pairs={{0,16},{8,0},{16,24},{24,8},{1,17},{9,1},{17,25},{25,9},{2,18},{10... | collective-permute-start | bytes 2359304 | tf_op jit(solution)/shard_map/ppermute | solution.py:102
  138.2 22.2 %collective-permute-start.15 = (bf16[384,1024]{1,0:T(8,128)(2,1)}, bf16[384,1024]{1,0:T(8,128)(2,1)}, u32[]{:S(2)}, u32[]{:S(2)}) collective-permute-start(bf16[384,1024]{1,0:T(8,128)(2,1)} %get-tuple-element.89), channel_id=1, source_target_pairs={{0,8},{8,24},{16,0},{24,16},{1,9},{9,25},{17,1},{25,17},{2,10},{10... | collective-permute-start | bytes 2359304 | tf_op jit(solution)/shard_map/ppermute | solution.py:102
  149.0 42.6 %all-to-all-start.3 = ((bf16[8,64,1536]{2,1,0:T(8,128)(2,1)}), bf16[8,64,1536]{2,1,0:T(8,128)(2,1)S(1)}, u32[]{:S(2)}, u32[]{:S(2)}) async-start(bf16[8,64,1536]{2,1,0:T(8,128)(2,1)} %bitcast.31), calls=%async_computation.3 | async-start | bytes 3145728 | tf_op jit(solution)/shard_map/all_to_all | solution.py:362
  160.4 6.0 %copy-start.19 = (bf16[256,1536]{1,0:T(8,128)(2,1)S(1)}, bf16[256,1536]{1,0:T(8,128)(2,1)}, u32[]{:S(2)}) copy-start(bf16[256,1536]{1,0:T(8,128)(2,1)} %get-tuple-element.95) | copy-start | bytes 2359300
  164.4 39.6 %collective-permute-start.16 = (bf16[2,384,1024]{2,1,0:T(8,128)(2,1)}, bf16[2,384,1024]{2,1,0:T(8,128)(2,1)}, u32[]{:S(2)}, u32[]{:S(2)}) collective-permute-start(bf16[2,384,1024]{2,1,0:T(8,128)(2,1)} %get-tuple-element.91), channel_id=1, source_target_pairs={{0,16},{8,0},{16,24},{24,8},{1,17},{9,1},{17,25},{25,9},{2,18},{10... | collective-permute-start | bytes 4718600 | tf_op jit(solution)/shard_map/ppermute | solution.py:102
  165.0 39.0 %collective-permute-start.17 = (bf16[2,384,1024]{2,1,0:T(8,128)(2,1)}, bf16[2,384,1024]{2,1,0:T(8,128)(2,1)}, u32[]{:S(2)}, u32[]{:S(2)}) collective-permute-start(bf16[2,384,1024]{2,1,0:T(8,128)(2,1)} %get-tuple-element.92), channel_id=1, source_target_pairs={{0,8},{8,24},{16,0},{24,16},{1,9},{9,25},{17,1},{25,17},{2,10},{10... | collective-permute-start | bytes 4718600 | tf_op jit(solution)/shard_map/ppermute | solution.py:102
  193.1 1.2 collective-permute-start.18
  194.2 5.6 %collective-permute-start.21 = (f32[2,1536]{1,0:T(2,128)S(1)}, f32[2,1536]{1,0:T(2,128)S(1)}, u32[]{:S(2)}, u32[]{:S(2)}) collective-permute-start(f32[2,1536]{1,0:T(2,128)S(1)} %pad_maximum_fusion), channel_id=1, source_target_pairs={{0,6},{1,7},{2,4},{3,5},{4,2},{5,3},{6,0},{7,1},{8,14},{9,15},{10,... | collective-permute-start | bytes 36872 | tf_op jit(solution)/shard_map/ppermute | solution.py:102
  195.6 4.6 %collective-permute-start.20 = (f32[2,1536]{1,0:T(2,128)S(1)}, f32[2,1536]{1,0:T(2,128)S(1)}, u32[]{:S(2)}, u32[]{:S(2)}) collective-permute-start(f32[2,1536]{1,0:T(2,128)S(1)} %pad_maximum_fusion), channel_id=1, source_target_pairs={{0,4},{1,5},{2,6},{3,7},{4,0},{5,1},{6,2},{7,3},{8,12},{9,13},{10,... | collective-permute-start | bytes 36872 | tf_op jit(solution)/shard_map/ppermute | solution.py:102
  195.6 4.8 %collective-permute-start.19 = (f32[2,1536]{1,0:T(2,128)S(1)}, f32[2,1536]{1,0:T(2,128)S(1)}, u32[]{:S(2)}, u32[]{:S(2)}) collective-permute-start(f32[2,1536]{1,0:T(2,128)S(1)} %pad_maximum_fusion), channel_id=1, source_target_pairs={{0,2},{1,3},{2,0},{3,1},{4,6},{5,7},{6,4},{7,5},{8,10},{9,11},{10,... | collective-permute-start | bytes 36872 | tf_op jit(solution)/shard_map/ppermute | solution.py:102
  200.4 7.9 %collective-permute-start.24 = (f32[8,1536]{1,0:T(8,128)S(1)}, f32[8,1536]{1,0:T(8,128)S(1)}, u32[]{:S(2)}, u32[]{:S(2)}) collective-permute-start(f32[8,1536]{1,0:T(8,128)S(1)} %concatenate.12), channel_id=1, source_target_pairs={{0,24},{8,16},{16,8},{24,0},{1,25},{9,17},{17,9},{25,1},{2,26},{10... | collective-permute-start | bytes 147464 | tf_op jit(solution)/shard_map/ppermute | solution.py:102
  202.0 6.4 %collective-permute-start.23 = (f32[8,1536]{1,0:T(8,128)S(1)}, f32[8,1536]{1,0:T(8,128)S(1)}, u32[]{:S(2)}, u32[]{:S(2)}) collective-permute-start(f32[8,1536]{1,0:T(8,128)S(1)} %concatenate.12), channel_id=1, source_target_pairs={{0,16},{8,24},{16,0},{24,8},{1,17},{9,25},{17,1},{25,9},{2,18},{10... | collective-permute-start | bytes 147464 | tf_op jit(solution)/shard_map/ppermute | solution.py:102
  203.5 4.9 %collective-permute-start.22 = (f32[8,1536]{1,0:T(8,128)S(1)}, f32[8,1536]{1,0:T(8,128)S(1)}, u32[]{:S(2)}, u32[]{:S(2)}) collective-permute-start(f32[8,1536]{1,0:T(8,128)S(1)} %concatenate.12), channel_id=1, source_target_pairs={{0,8},{8,0},{16,24},{24,16},{1,9},{9,1},{17,25},{25,17},{2,10},{10... | collective-permute-start | bytes 147464 | tf_op jit(solution)/shard_map/ppermute | solution.py:102
  (2 other events, 1.4 us)
